TPU v7x, 256 devices: a whole 4x4x8 slice. The times are simulated.
256 devices in a mesh: dp: 4 (over x), seq: 64 (over y, z, core).
Axes of the slice: x: 4, y: 4, z: 8, core: 2. Of those that a mesh axis runs over, the one named last changes fastest.
Arguments:
- activations: bfloat16 [4, 16384, 2048], P('dp', 'seq'), may hold values from -16 to 16
- w_query: bfloat16 [2048, 2048], replicated, may hold values from -0.125 to 0.125
- all_keys: bfloat16 [4, 16384, 2048], P('dp', 'seq'), may hold values from -6 to 6
- values: bfloat16 [4, 16384, 2048], P('dp', 'seq'), may hold values from -6 to 6
- grad_out: bfloat16 [4, 16384, 2048], P('dp', 'seq'), may hold values from -0.125 to 0.125
- cluster: int32 [4, 16384, 16], P('dp', 'seq'), may hold values from 0 to 255, as said below
Outputs:
- grad_query_weight: float32 [2048, 2048], P(('dp', 'seq'))
Inputs may be any that keep to these rules, and one draw needn't show every extreme that they name: In every sequence and head, at most 2 of the 256 tokens of one device fall in one cluster, so a cluster holds at most 128 tokens. In every sequence there is a device index o along seq such that in every head each cluster whose number is o plus a multiple of the seq axis's device count holds exactly 2 tokens of every device.
All inputs are finite; a program needn't handle non-finite values.
Results may differ from a plain program's by a relative error of at most 0.0071.
Values may be sent and summed in bfloat16 or wider, within the bound.
No kernel may reach another device: no remote copies, remote signals or barrier semaphores. Data moves between devices by JAX's collectives and lax.ppermute only.
A program may use at most 128 MiB of HBM per device.

v0:
```python
import math

import jax
import jax.numpy as jnp
from jax import lax
from jax.sharding import PartitionSpec as P

BLOCK = 128


def entering(value, axis, join, neutral):
    count, mine = (lax.axis_size(axis), lax.axis_index(axis))
    pieces = lax.all_gather(value, axis)
    total = jnp.full_like(value, 0) + jnp.asarray(neutral, value.dtype)

    def lap(position, total):
        longer = join(total, pieces[position])
        return jnp.where(position < mine, longer, total)

    return lax.fori_loop(0, count - 1, lap, total)


def add_counts(earlier, later):
    return earlier + later


def on_device(activations, w_query, all_keys, values, grad_out, cluster):
    seq_count = lax.axis_size("seq")
    tokens_here = activations[0]
    assign = cluster[0]
    tok_count = assign.shape[0]
    head_count = assign.shape[1]
    head_width = all_keys.shape[2] // head_count
    block_rows = BLOCK
    per_device = block_rows // seq_count
    mean_blocks = 2 * tok_count // block_rows
    cluster_count = mean_blocks * seq_count
    owned_blocks = head_count * mean_blocks
    capacity = owned_blocks * per_device
    owned_rows = owned_blocks * block_rows
    row_count = tok_count * head_count
    scale = 1.0 / math.sqrt(head_width)
    queries = jnp.dot(tokens_here, w_query, preferred_element_type=jnp.float32).astype(jnp.bfloat16)
    onehot = (assign[:, :, None] == jnp.arange(cluster_count)[None, None, :]).astype(jnp.int32)
    counts = jnp.sum(onehot, axis=0)
    earlier = entering(counts, "seq", add_counts, jnp.zeros_like(counts))
    position = jnp.arange(tok_count)
    by_head = assign.T
    same = (by_head[:, :, None] == by_head[:, None, :]) & (
        position[None, None, :] < position[None, :, None]
    )
    within = jnp.sum(same.astype(jnp.int32), axis=2).T
    ranked = jnp.sum(onehot * earlier[None, :, :], axis=2) + within
    local_block = jnp.arange(head_count)[None, :] * mean_blocks + assign // seq_count
    target = (local_block * block_rows + ranked).reshape(row_count).astype(jnp.int32)
    owner = (assign % seq_count).reshape(row_count)
    owner_hot = (owner[:, None] == jnp.arange(seq_count)[None, :]).astype(jnp.int32)
    send_rank = jnp.sum((jnp.cumsum(owner_hot, axis=0) - owner_hot) * owner_hot, axis=1)
    slot = owner * capacity + send_rank

    def pack(data):
        return (
            jnp.zeros((seq_count * capacity, head_width), jnp.bfloat16)
            .at[slot]
            .set(data.reshape(row_count, head_width))
        )

    target_buf = jnp.full((seq_count * capacity,), owned_rows, jnp.int32).at[slot].set(target)
    got_query, got_key, got_value, got_target = (
        lax.all_to_all(pack(queries), "seq", split_axis=0, concat_axis=0, tiled=True),
        lax.all_to_all(pack(all_keys[0]), "seq", split_axis=0, concat_axis=0, tiled=True),
        lax.all_to_all(pack(values[0]), "seq", split_axis=0, concat_axis=0, tiled=True),
        lax.all_to_all(target_buf, "seq", split_axis=0, concat_axis=0, tiled=True),
    )

    def place(data):
        filled = (
            jnp.zeros((owned_rows, head_width), jnp.bfloat16).at[got_target].set(data, mode="drop")
        )
        return filled.reshape(owned_blocks, block_rows, head_width)

    query_blk = place(got_query)
    key_blk = place(got_key)
    value_blk = place(got_value)
    block_pos = jnp.arange(block_rows)
    causal = block_pos[:, None] >= block_pos[None, :]
    scores = (
        jnp.einsum("nqd,nkd->nqk", query_blk, key_blk, preferred_element_type=jnp.float32) * scale
    )
    raised = jnp.where(causal, jnp.exp(scores), 0.0)
    weights = raised / jnp.sum(raised, axis=-1, keepdims=True)
    attended = jnp.einsum(
        "nqk,nkd->nqd", weights.astype(jnp.bfloat16), value_blk, preferred_element_type=jnp.float32
    )
    grad_rows = lax.all_to_all(pack(grad_out[0]), "seq", split_axis=0, concat_axis=0, tiled=True)
    grad_blk = place(grad_rows)
    dweights = jnp.einsum("nqd,nkd->nqk", grad_blk, value_blk, preferred_element_type=jnp.float32)
    delta = jnp.sum(grad_blk.astype(jnp.float32) * attended, axis=-1, keepdims=True)
    dscores = (weights * (dweights - delta)).astype(jnp.bfloat16)
    dquery = (
        jnp.einsum("nqk,nkd->nqd", dscores, key_blk, preferred_element_type=jnp.float32) * scale
    ).astype(jnp.bfloat16)
    flat_grads = dquery.reshape(owned_rows, head_width)
    send_back = flat_grads[jnp.minimum(got_target, owned_rows - 1)]
    returned = lax.all_to_all(send_back, "seq", split_axis=0, concat_axis=0, tiled=True)
    dquery_rows = returned[slot].reshape(tok_count, head_count * head_width)
    return lax.psum_scatter(
        jnp.einsum("ti,tn->in", tokens_here, dquery_rows, preferred_element_type=jnp.float32),
        ("dp", "seq"),
        scatter_dimension=0,
        tiled=True,
    )


def solution(mesh):
    placed = (
        P("dp", "seq", None),
        P(),
        P("dp", "seq", None),
        P("dp", "seq", None),
        P("dp", "seq", None),
        P("dp", "seq", None),
    )
    return jax.shard_map(
        on_device, mesh=mesh, in_specs=placed, out_specs=P(("dp", "seq"), None), check_vma=False
    )
```

profile of v0, /device:TPU:1, one launch (start us, length us, event | category | flops | bytes accessed | tf_op | source)
XLA Modules:
  0.0 1903.2 jit_solution(5458858495444130826)
XLA Ops:
  6.5 0.9 copy.54
  7.4 1.6 convert_reduce_fusion.1
  9.4 2.1 convert_reduce_fusion
  11.8 18.4 reduce-window.6
  31.6 0.9 fusion.5
  32.6 58.2 %all-gather.3.cloned.1.call-done = s32[1024,256]{1,0:T(8,128)} async-done(((s32[16,256]{1,0:T(8,128)}), s32[1024,256]{1,0:T(8,128)}) %all-gather.3.cloned.1.call-update) | async-done | bytes 1048592 | tf_op jit(solution)/shard_map/all_gather | solution.py:13
  90.8 45.5 %while.14 = (s32[]{:T(128)}, s32[16,256]{1,0:T(8,128)S(1)}, s32[]{:T(128)}, s32[64,16,256]{2,1,0:T(8,128)}, s32[]{:T(128)}, /*index=5*/s32[]{:T(128)}) while((s32[]{:T(128)}, s32[16,256]{1,0:T(8,128)S(1)}, s32[]{:T(128)}, s32[64,16,256]{2,1,0:T(8,128)}, s32[]{:T(128)}, /*index=5*/s32[]{:T(128)}) %tuple.41), condition=%wide.region_5.6_spmd.clone, body=%wide.region_4.5_spmd.clone.sunk | while | flops 12292 | bytes 49253 | solution.py:20
  90.8 0.7 add_select_fusion.5
  92.3 0.7 add_select_fusion.5
  95.9 0.7 add_select_fusion.5
  97.3 0.7 add_select_fusion.5
  100.9 0.7 add_select_fusion.5
  136.3 5.7 select_reduce_fusion
  142.3 16.1 scatter_custom_fusion
  158.4 6.7 all-to-all-start
  165.0 5.7 convolution_convert_fusion
  171.3 12.9 scatter_custom_fusion.1
  184.2 10.3 all-to-all-start.1
  194.6 2.4 reshape.257
  196.9 12.7 scatter_custom_fusion.3
  209.7 36.2 %all-to-all-done.1 = bf16[64,128,128]{2,1,0:T(8,128)(2,1)S(1)} async-done(((bf16[64,128,128]{2,1,0:T(8,128)(2,1)}), bf16[64,128,128]{2,1,0:T(8,128)(2,1)S(1)}, u32[]{:S(2)}, u32[]{:S(2)}) %all-to-all-start.1) | async-done | bytes 2097184 | tf_op jit(solution)/shard_map/all_to_all | solution.py:70
  245.8 6.0 all-to-all-start.2
  251.8 2.4 reshape.289
  254.2 12.8 scatter_custom_fusion.7
  267.0 36.0 %all-to-all-done.2 = bf16[64,128,128]{2,1,0:T(8,128)(2,1)} async-done(((bf16[64,128,128]{2,1,0:T(8,128)(2,1)}), bf16[64,128,128]{2,1,0:T(8,128)(2,1)}, u32[]{:S(2)}, u32[]{:S(2)}) %all-to-all-start.2) | async-done | bytes 2097184 | tf_op jit(solution)/shard_map/all_to_all | solution.py:71
  303.0 6.0 all-to-all-start.4
  309.0 2.4 reshape.273
  311.4 12.8 scatter_custom_fusion.5
  324.2 36.0 %all-to-all-done.4 = bf16[64,128,128]{2,1,0:T(8,128)(2,1)} async-done(((bf16[64,128,128]{2,1,0:T(8,128)(2,1)}), bf16[64,128,128]{2,1,0:T(8,128)(2,1)}, u32[]{:S(2)}, u32[]{:S(2)}) %all-to-all-start.4) | async-done | bytes 2097184 | tf_op jit(solution)/shard_map/all_to_all | solution.py:72
  360.2 6.0 all-to-all-start.3
  366.3 22.5 %scatter_custom_fusion.2 = bf16[8192,128]{1,0:T(8,128)(2,1)} fusion(s32[8192]{0:T(1024)S(1)} %bitcast.112, bf16[8192,128]{1,0:T(8,128)(2,1)S(1)} %bitcast.100, bf16[]{:T(256)} %constant.65.clone.1), kind=kCustom, calls=%fused_computation.45 | custom fusion | bytes 2097154 | tf_op jit(solution)/shard_map/scatter | solution.py:78
  388.9 22.8 %scatter_custom_fusion.4 = bf16[8192,128]{1,0:T(8,128)(2,1)} fusion(s32[8192]{0:T(1024)S(1)} %bitcast.113, bf16[8192,128]{1,0:T(8,128)(2,1)} %bitcast.21, bf16[]{:T(256)} %constant.65.clone.1), kind=kCustom, calls=%fused_computation.41 | custom fusion | bytes 2097664 | tf_op jit(solution)/shard_map/scatter | solution.py:78
  411.7 22.8 %scatter_custom_fusion.8 = bf16[8192,128]{1,0:T(8,128)(2,1)} fusion(s32[8192]{0:T(1024)S(1)} %bitcast.114, bf16[8192,128]{1,0:T(8,128)(2,1)} %bitcast.27, bf16[]{:T(256)} %constant.65.clone.1), kind=kCustom, calls=%fused_computation.33 | custom fusion | bytes 2097664 | tf_op jit(solution)/shard_map/scatter | solution.py:78
  434.5 22.1 %scatter_custom_fusion.6 = bf16[8192,128]{1,0:T(8,128)(2,1)S(1)} fusion(s32[8192]{0:T(1024)S(1)} %bitcast.115, bf16[8192,128]{1,0:T(8,128)(2,1)} %bitcast.24, bf16[]{:T(256)} %constant.65.clone.1), kind=kCustom, calls=%fused_computation.37 | custom fusion | bytes 2097664 | tf_op jit(solution)/shard_map/scatter | solution.py:78
  456.7 3.0 copy.64
  459.6 4.0 fusion.1
  463.6 1.9 copy-done.3
  465.5 1.7 multiply_reduce_fusion
  467.2 7.3 multiply_convert_fusion
  474.5 3.2 copy.70
  477.8 29.2 %gather_fusion = bf16[8192,128]{1,0:T(8,128)(2,1)} fusion(bf16[8192,128]{1,0:T(8,128)(2,1)S(1)} %bitcast.87, s32[8192]{0:T(1024)S(1)} %broadcast_clamp_fusion), kind=kCustom, calls=%fused_computation | custom fusion | bytes 4227072 | tf_op jit(solution)/shard_map/gather | solution.py:104
  507.0 10.3 all-to-all-start.5
  517.4 51.2 %all-to-all-done.5 = bf16[64,128,128]{2,1,0:T(8,128)(2,1)S(1)} async-done(((bf16[64,128,128]{2,1,0:T(8,128)(2,1)}), bf16[64,128,128]{2,1,0:T(8,128)(2,1)S(1)}, u32[]{:S(2)}, u32[]{:S(2)}) %all-to-all-start.5) | async-done | bytes 2097184 | tf_op jit(solution)/shard_map/all_to_all | solution.py:105
  568.6 14.9 gather_fusion.1
  583.5 1.5 reshape.212
  585.0 8.1 convolution_bitcast_fusion
  593.1 17.6 copy.80
  610.7 1285.4 %reduce-scatter.4.cloned.1.call-done = f32[8,2048]{1,0:T(8,128)} async-done(((f32[2048,2048]{1,0:T(8,128)}), f32[8,2048]{1,0:T(8,128)}) %reduce-scatter.4.cloned.1.call-update) | async-done | bytes 65552 | tf_op jit(solution)/shard_map/reduce_scatter | solution.py:107
  (93 shorter events, 44.8 us)
Async XLA Ops:
  6.5 158.5 %copy-start = (bf16[1,256,2048]{2,1,0:T(8,128)(2,1)S(1)}, bf16[1,256,2048]{2,1,0:T(8,128)(2,1)}, u32[]{:S(2)}) copy-start(bf16[1,256,2048]{2,1,0:T(8,128)(2,1)} %param.8) | copy-start | bytes 3145732
  6.5 84.3 %all-gather.3.cloned.1.call-start = ((), (), s32[]{:S(2)}) async-start(), calls=%async_computation.7 | async-start | bytes 1064960 | tf_op jit(solution)/shard_map/all_gather | solution.py:13
  158.4 25.9 %all-to-all-start = ((s32[64,128,1]{1,2,0:T(1,128)}), s32[64,128,1]{1,2,0:T(1,128)S(1)}, u32[]{:S(2)}, u32[]{:S(2)}) async-start(s32[64,128,1]{1,2,0:T(1,128)} %bitcast.13), calls=%async_computation | async-start | bytes 65536 | tf_op jit(solution)/shard_map/all_to_all | solution.py:73
  184.2 61.6 %all-to-all-start.1 = ((bf16[64,128,128]{2,1,0:T(8,128)(2,1)}), bf16[64,128,128]{2,1,0:T(8,128)(2,1)S(1)}, u32[]{:S(2)}, u32[]{:S(2)}) async-start(bf16[64,128,128]{2,1,0:T(8,128)(2,1)} %bitcast.17), calls=%async_computation.1 | async-start | bytes 4194304 | tf_op jit(solution)/shard_map/all_to_all | solution.py:70
  245.8 57.2 %all-to-all-start.2 = ((bf16[64,128,128]{2,1,0:T(8,128)(2,1)}), bf16[64,128,128]{2,1,0:T(8,128)(2,1)}, u32[]{:S(2)}, u32[]{:S(2)}) async-start(bf16[64,128,128]{2,1,0:T(8,128)(2,1)} %bitcast.20), calls=%async_computation.2 | async-start | bytes 4194304 | tf_op jit(solution)/shard_map/all_to_all | solution.py:71
  303.0 57.2 %all-to-all-start.4 = ((bf16[64,128,128]{2,1,0:T(8,128)(2,1)}), bf16[64,128,128]{2,1,0:T(8,128)(2,1)}, u32[]{:S(2)}, u32[]{:S(2)}) async-start(bf16[64,128,128]{2,1,0:T(8,128)(2,1)} %bitcast.26), calls=%async_computation.4 | async-start | bytes 4194304 | tf_op jit(solution)/shard_map/all_to_all | solution.py:72
  360.2 74.4 %all-to-all-start.3 = ((bf16[64,128,128]{2,1,0:T(8,128)(2,1)}), bf16[64,128,128]{2,1,0:T(8,128)(2,1)}, u32[]{:S(2)}, u32[]{:S(2)}) async-start(bf16[64,128,128]{2,1,0:T(8,128)(2,1)} %bitcast.23), calls=%async_computation.3 | async-start | bytes 4194304 | tf_op jit(solution)/shard_map/all_to_all | solution.py:95
  459.6 5.9 copy-start.1
  459.6 5.9 copy-start.2
  463.6 1.9 copy-start.3
  507.0 61.6 %all-to-all-start.5 = ((bf16[64,128,128]{2,1,0:T(8,128)(2,1)}), bf16[64,128,128]{2,1,0:T(8,128)(2,1)S(1)}, u32[]{:S(2)}, u32[]{:S(2)}) async-start(bf16[64,128,128]{2,1,0:T(8,128)(2,1)} %bitcast.89), calls=%async_computation.5 | async-start | bytes 4194304 | tf_op jit(solution)/shard_map/all_to_all | solution.py:105
  517.3 1378.8 %reduce-scatter.4.cloned.1.call-start = ((), (), s32[]{:S(2)}) async-start(), calls=%async_computation.8 | async-start | bytes 16842752 | tf_op jit(solution)/shard_map/reduce_scatter | solution.py:107
Sparse Core Ops, SparseCore 0:
  10.1 80.6 all-gather.2
  610.8 1285.2 reduce-scatter.3
where the time goes:
time: 1920 us; the launch traced here: 1900 us
  waiting for transfers between devices  1500 us (78%)
  local copies, waits for them, and re-layouts  239 us (12%)
  other arithmetic  75.2 us (4%)
  starting transfers between devices  45.4 us (2%)
  matrix products  26.8 us (1%)
    reduce_scatter x1, waiting for transfers between devices, on_device(): lax.psum_scatter(jnp.einsum('ti,tn->in', tokens_here, dquery_rows, prefer...  1290 us
    scatter x4, local copies, waits for them, and re-layouts, place(): jnp.zeros((owned_rows, head_width), jnp.bfloat16).at[got_target]  90.3 us
    all_gather x1, waiting for transfers between devices, entering(): pieces = lax.all_gather(value, axis)  58.2 us
    scatter x4, local copies, waits for them, and re-layouts, pack(): return jnp.zeros((seq_count * capacity, head_width), jnp.bfloat16).at[slo...  51.2 us
    all_to_all x1, waiting for transfers between devices, on_device(): lax.all_to_all(send_back, 'seq', split_axis=0, concat_axis=0, tiled=True)  51.2 us
    select_n x63, other arithmetic, lap(): return jnp.where(position < mine, longer, total)  45.5 us
  transfers between devices with their start and end apart: 8, of which 6 were waited for; matrix products, arithmetic and copies ran while one was open for 8% of the time, Pallas kernels for 0%

commit v1 on v0

v1 whole, which is shorter than its diff:
```python
import functools
import math

import jax
import jax.numpy as jnp
from jax import lax
from jax.experimental import pallas as pl
from jax.experimental.pallas import tpu as pltpu
from jax.sharding import PartitionSpec as P

HEAD = 128
TOK = 256
OWNERS = 64
CELL = 8
SLOTS = OWNERS * CELL
HEADS = 16
CHUNKS = 2
HPC = HEADS // CHUNKS
EMPTY = 128.0
VMEM = 48 * 1024 * 1024
BF = jnp.bfloat16
F32 = jnp.float32


def dot(a, b, dims):
    return lax.dot_general(a, b, (dims, ((), ())), preferred_element_type=F32)


NN = ((1,), (0,))
NT = ((1,), (1,))


def params(*semantics):
    return pltpu.CompilerParams(vmem_limit_bytes=VMEM, dimension_semantics=semantics or None)


def slot_kernel(col_ref, row_ref, out_ref):
    earlier = lax.broadcasted_iota(jnp.int32, (TOK, TOK), 0) < lax.broadcasted_iota(
        jnp.int32, (TOK, TOK), 1
    )
    for h in range(HEADS):
        row = row_ref[h : h + 1, :]
        same = (col_ref[:, h : h + 1] == row) & earlier
        rank = jnp.sum(jnp.where(same, 1, 0), axis=0, keepdims=True)
        out_ref[h : h + 1, :] = (row % OWNERS) * CELL + (row // OWNERS) * 2 + rank


def slots_of(assign):
    return pl.pallas_call(
        slot_kernel,
        out_shape=jax.ShapeDtypeStruct((HEADS, TOK), jnp.int32),
        compiler_params=params(),
        name="slots",
    )(assign, assign.T)


def pack_kernel(mark, slot_ref, *refs):
    sources, out_ref = refs[:-1], refs[-1]
    place = lax.broadcasted_iota(jnp.int32, (SLOTS, TOK), 0)
    for n, source in enumerate(sources):
        parts = []
        for e in range(2):
            hot = jnp.where(place == slot_ref[0, e : e + 1, :], 1.0, 0.0)
            hot_low = hot.astype(BF)
            rows = dot(hot_low, source[:, e * HEAD : (e + 1) * HEAD], NN)
            if mark and n == 0:
                filled = dot(hot_low, jnp.ones((TOK, HEAD), BF), NN)
                rows = jnp.where(filled > 0.5, rows, EMPTY)
            parts.append(rows.reshape(OWNERS, CELL, HEAD))
        out_ref[:, :, n * HEAD : (n + 1) * HEAD] = jnp.concatenate(parts, axis=1).astype(BF)


def pack(slots, chunk, mark, *sources):
    pairs = HPC // 2
    width = HEAD * len(sources)
    return pl.pallas_call(
        functools.partial(pack_kernel, mark),
        grid=(pairs,),
        in_specs=[pl.BlockSpec((1, 2, TOK), lambda p: (chunk * pairs + p, 0, 0))]
        + [pl.BlockSpec((TOK, 2 * HEAD), lambda p: (0, chunk * pairs + p)) for _ in sources],
        out_specs=pl.BlockSpec((OWNERS, 2 * CELL, width), lambda p: (0, p, 0)),
        out_shape=jax.ShapeDtypeStruct((OWNERS, HPC * CELL, width), BF),
        compiler_params=params("arbitrary"),
        cost_estimate=pl.CostEstimate(
            flops=2 * HPC * SLOTS * TOK * width * 4, bytes_accessed=6 * 2**20, transcendentals=0
        ),
        name="pack",
    )(slots.reshape(HEADS // 2, 2, TOK), *sources)


def attention_kernel(kvg_ref, q_ref, out_ref, bias_ref):
    scale = 1.0 / math.sqrt(HEAD)
    to_exp2 = scale * math.log2(math.e)

    @pl.when(pl.program_id(0) == 0)
    def _():
        row = lax.broadcasted_iota(jnp.int32, (SLOTS, SLOTS), 0)
        col = lax.broadcasted_iota(jnp.int32, (SLOTS, SLOTS), 1)
        keep = (col <= row) & ((row % CELL) // 2 == (col % CELL) // 2)
        bias_ref[...] = jnp.where(keep, 0.0, -1e30)

    first = jnp.where(lax.broadcasted_iota(jnp.int32, (8, HEAD), 1) == 0, 1.0, 0.0).astype(BF)
    kvg_pair = kvg_ref[...].astype(F32)
    q_pair = q_ref[...].astype(F32)
    step = 128
    for e in range(2):
        kvg = kvg_pair[:, e * CELL : (e + 1) * CELL, :].reshape(SLOTS, 3 * HEAD).astype(BF)
        q = q_pair[:, e * CELL : (e + 1) * CELL, :].reshape(SLOTS, HEAD).astype(BF)
        k, v, g = (kvg[:, n * HEAD : (n + 1) * HEAD] for n in range(3))
        key_bias = jnp.where(dot(first, k, NT)[0:1, :] > 0.5 * EMPTY, -1e30, 0.0)
        for i in range(SLOTS // step):
            here = slice(i * step, (i + 1) * step)
            n = (i + 1) * step
            score = dot(q[here], k[:n], NT) * to_exp2 + bias_ref[here, :n] + key_bias[:, :n]
            raised = jnp.exp2(score)
            total = jnp.sum(raised, axis=1, keepdims=True)
            weights = raised * (1.0 / jnp.where(total == 0.0, 1.0, total))
            attended = dot(weights.astype(BF), v[:n], NN)
            dweights = dot(g[here], v[:n], NT)
            delta = jnp.sum(g[here].astype(F32) * attended, axis=1, keepdims=True)
            dscores = (weights * (dweights - delta)).astype(BF)
            dquery = (dot(dscores, k[:n], NN) * scale).astype(BF)
            tiles = step // (2 * CELL)
            out_ref[0, i * tiles : (i + 1) * tiles, e] = dquery.reshape(tiles, 2 * CELL, HEAD)


def attention(kvg, q):
    return pl.pallas_call(
        attention_kernel,
        grid=(HPC // 2,),
        in_specs=[
            pl.BlockSpec((OWNERS, 2 * CELL, 3 * HEAD), lambda p: (0, p, 0)),
            pl.BlockSpec((OWNERS, 2 * CELL, HEAD), lambda p: (0, p, 0)),
        ],
        out_specs=pl.BlockSpec((1, OWNERS // 2, 2, 2 * CELL, HEAD), lambda p: (p, 0, 0, 0, 0)),
        out_shape=jax.ShapeDtypeStruct((HPC // 2, OWNERS // 2, 2, 2 * CELL, HEAD), BF),
        scratch_shapes=[pltpu.VMEM((SLOTS, SLOTS), F32)],
        compiler_params=params("arbitrary"),
        cost_estimate=pl.CostEstimate(
            flops=HPC * 8 * SLOTS * SLOTS * HEAD,
            bytes_accessed=5 * 2**20,
            transcendentals=HPC * SLOTS * SLOTS,
        ),
        name="attention",
    )(kvg, q)


def grad_kernel(where_ref, rows_ref, slot_a, slot_b, act_a, act_b, out_ref, acc_ref):
    b = pl.program_id(0)
    head, core = where_ref[0], where_ref[1]
    rows = rows_ref[...].reshape(OWNERS * 2 * CELL, HEAD)
    lane = lax.broadcasted_iota(jnp.int32, (TOK, HEADS), 1)
    place = lax.broadcasted_iota(jnp.int32, (TOK, OWNERS * 2 * CELL), 1)
    total = None
    for slot_ref, act_ref, side in ((slot_a, act_a, core), (slot_b, act_b, 1 - core)):
        slot = jnp.sum(jnp.where(lane == head, slot_ref[0], 0), axis=1, keepdims=True)
        index = (slot // CELL) * (2 * CELL) + side * CELL + slot % CELL
        hot = jnp.where(place == index, 1.0, 0.0).astype(BF)
        dquery = dot(hot, rows, NN).astype(BF)
        term = dot(act_ref[0], dquery, NN)
        total = term if total is None else total + term

    @pl.when(b == 0)
    def _():
        acc_ref[...] = total

    @pl.when(b > 0)
    def _():
        acc_ref[...] += total

    @pl.when(b == pl.num_programs(0) - 1)
    def _():
        out_ref[...] = acc_ref[...].astype(BF)


def weight_grad(where, rows, slots, acts, features, seqs):
    def slot_spec():
        return pl.BlockSpec((1, TOK, HEADS), lambda b, w: (b, 0, 0))

    def act_spec():
        return pl.BlockSpec((1, features, TOK), lambda b, w: (b, 0, 0))

    return pl.pallas_call(
        grad_kernel,
        grid_spec=pltpu.PrefetchScalarGridSpec(
            num_scalar_prefetch=1,
            grid=(seqs,),
            in_specs=[
                pl.BlockSpec((OWNERS, 2 * CELL, HEAD), lambda b, w: (b, 0, 0)),
                slot_spec(),
                slot_spec(),
                act_spec(),
                act_spec(),
            ],
            out_specs=pl.BlockSpec((features, HEAD), lambda b, w: (0, 0)),
            scratch_shapes=[pltpu.VMEM((features, HEAD), F32)],
        ),
        out_shape=jax.ShapeDtypeStruct((features, HEAD), BF),
        compiler_params=params("arbitrary"),
        cost_estimate=pl.CostEstimate(
            flops=4 * seqs * TOK * features * HEAD * 2,
            bytes_accessed=12 * 2**20,
            transcendentals=0,
        ),
        name="weight_grad",
    )(where, rows, *slots, *acts)


def on_device(activations, w_query, all_keys, values, grad_out, cluster):
    tokens_here = activations[0]
    features = tokens_here.shape[1]
    seqs = lax.axis_size("dp")
    devices = seqs * OWNERS
    slots = slots_of(cluster[0])
    seq_send = functools.partial(
        lax.all_to_all, axis_name="seq", split_axis=0, concat_axis=0, tiled=True
    )
    all_send = functools.partial(
        lax.all_to_all, axis_name=("dp", "seq"), split_axis=0, concat_axis=0, tiled=True
    )
    kvg = [pack(slots, c, True, all_keys[0], values[0], grad_out[0]) for c in range(CHUNKS)]
    queries = jnp.dot(tokens_here, w_query, preferred_element_type=F32).astype(BF)
    q = [pack(slots, c, False, queries) for c in range(CHUNKS)]

    swap = [(i, i ^ 1) for i in range(OWNERS)]
    acts_mine = lax.all_gather(tokens_here.T, "dp")
    slots_mine = lax.all_gather(slots.T, "dp")
    acts = (acts_mine, lax.ppermute(acts_mine, "seq", swap))
    slot_cols = (slots_mine, lax.ppermute(slots_mine, "seq", swap))
    core = lax.axis_index("seq") % 2
    group = lax.axis_index("dp") * 2 + core

    sums = []
    for c in range(CHUNKS):
        got_kvg, got_q = seq_send(kvg[c]), seq_send(q[c])
        rows = attention(got_kvg, got_q)
        rows = rows.reshape(HPC // 2, OWNERS // 2, 2, 2 * CELL, HEAD)
        back = all_send(rows.reshape(devices, 2 * CELL, HEAD))
        where = jnp.stack([c * HPC + group, core]).astype(jnp.int32)
        part = weight_grad(where, back, slot_cols, acts, features, seqs)
        got = all_send(part.reshape(devices, features // devices, HEAD))
        got = got.reshape(seqs, OWNERS // 2, 2, features // devices, HEAD)
        total = jnp.sum(got.astype(F32), axis=1)
        sums.append(total.reshape(HPC, features // devices, HEAD))
    out = jnp.concatenate(sums, axis=0)
    return out.transpose(1, 0, 2).reshape(features // devices, HEADS * HEAD)


def solution(mesh):
    placed = (
        P("dp", "seq", None),
        P(),
        P("dp", "seq", None),
        P("dp", "seq", None),
        P("dp", "seq", None),
        P("dp", "seq", None),
    )
    return jax.shard_map(
        on_device, mesh=mesh, in_specs=placed, out_specs=P(("dp", "seq"), None), check_vma=False
    )
```

time: 1920 us -> 394 us (0.21)
  waiting for transfers between devices: 1500 us -> 215 us
  local copies, waits for them, and re-layouts: 239 us -> 19.5 us
  other arithmetic: 75.2 us -> 1.97 us
  Pallas kernels: 0 us -> 64.4 us
  matrix products: 26.8 us -> 6.05 us
    reduce_scatter x1 -> x0, waiting for transfers between devices: 1290 us -> none  [on_device(): lax.psum_scatter(jnp.einsum('ti,tn->in', tokens_here, dquery_rows, prefer...]
    scatter x9 -> x0, local copies, waits for them, and re-layouts: 158 us -> none  [the longest x4 90.3 us: place(): jnp.zeros((owned_rows, head_width), jnp.bfloat16).at[got_target]]
    pallas_call x0 -> x9, Pallas kernels: none -> 64.4 us  [the longest x2 33.6 us: attention(): pl.pallas_call(attention_kernel, grid=(HPC // 2,), in_specs=[pl.BlockSpec...]
    all_gather x1, waiting for transfers between devices: 58.2 us -> 0.02 us  [on_device(): acts_mine = lax.all_gather(tokens_here.T, 'dp')]
    all_to_all x6 -> x8, waiting for transfers between devices: 159 us -> 213 us  [the longest x4 161 us: on_device(): got_kvg, got_q = (seq_send(kvg[c]), seq_send(q[c]))]
    select_n x67 -> x0, other arithmetic: 45.7 us -> none  [the longest x63 45.5 us: lap(): return jnp.where(position < mine, longer, total)]
    gather x2 -> x0, local copies, waits for them, and re-layouts: 44.1 us -> none  [the longest x1 29.2 us: on_device(): send_back = flat_grads[jnp.minimum(got_target, owned_rows - 1)]]
    dot_general x5 -> x1, matrix products: 26.8 us -> 6.05 us  [on_device(): jnp.dot(tokens_here, w_query, preferred_element_type=F32).astype(BF)]
  transfers between devices with their start and end apart: 8 -> 11, of which waited for: 6 -> 9; matrix products, arithmetic and copies ran while one was open for 8% -> 2% of each run, Pallas kernels for 0% -> 16%
where the time goes in v1:
time: 394 us; the launch traced here: 393 us
  waiting for transfers between devices  215 us (55%)
  Pallas kernels  64.4 us (16%)
  starting transfers between devices  62.1 us (16%)
  local copies, waits for them, and re-layouts  19.5 us (5%)
  between operations  13.6 us (3%)
  blocking collectives  9.99 us (3%)
  matrix products  6.05 us (2%)
    all_to_all x4, waiting for transfers between devices, on_device(): got_kvg, got_q = (seq_send(kvg[c]), seq_send(q[c]))  161 us
    pallas_call x2, Pallas kernels, attention(): pl.pallas_call(attention_kernel, grid=(HPC // 2,), in_specs=[pl.BlockSpec...  33.6 us
    all_to_all x4, starting transfers between devices, on_device(): got_kvg, got_q = (seq_send(kvg[c]), seq_send(q[c]))  31.9 us
    all_to_all x2, waiting for transfers between devices, on_device(): got = all_send(part.reshape(devices, features // devices, HEAD))  30.8 us
    all_to_all x2, waiting for transfers between devices, on_device(): back = all_send(rows.reshape(devices, 2 * CELL, HEAD))  21.3 us
    pallas_call x2, Pallas kernels, weight_grad(): pl.pallas_call(grad_kernel, grid_spec=pltpu.PrefetchScalarGridSpec(num_sc...  16.8 us
    all_to_all x2, starting transfers between devices, on_device(): back = all_send(rows.reshape(devices, 2 * CELL, HEAD))  13.8 us
    pallas_call x4, Pallas kernels, pack(): pl.pallas_call(functools.partial(pack_kernel, mark), grid=(pairs,), in_sp...  13.4 us
  transfers between devices with their start and end apart: 11, of which 9 were waited for; matrix products, arithmetic and copies ran while one was open for 2% of the time, Pallas kernels for 16%

profile of v1, /device:TPU:1, one launch (start us, length us, event | category | flops | bytes accessed | tf_op | source)
XLA Modules:
  0.0 392.9 jit_solution(5536053507764618453)
XLA Ops:
  6.5 0.8 copy.7.col_ref
  7.4 0.7 copy-done.6
  8.1 0.6 slots.1
  8.7 6.0 %convolution_convert_fusion.refs_0_ = bf16[256,2048]{1,0:T(8,128)(2,1)S(1)} fusion(bf16[2048,2048]{1,0:T(8,128)(2,1)} %param.7, bf16[1,256,2048]{2,1,0:T(8,128)(2,1)} %param.6), kind=kOutput, calls=%fused_computation | convolution fusion | flops 2148007936 | bytes 10485760 | tf_op jit(solution)/shard_map/dot_general | solution.py:222
  14.8 2.4 pack.5
  17.2 13.3 %all-to-all-start.1 = ((bf16[64,64,128]{2,1,0:T(8,128)(2,1)}), bf16[64,64,128]{2,1,0:T(8,128)(2,1)S(1)}, u32[]{:S(2)}, u32[]{:S(2)}) async-start(bf16[64,64,128]{2,1,0:T(8,128)(2,1)} %pack.5), calls=%async_computation.1 | async-start | bytes 2097152 | tf_op jit(solution)/shard_map/all_to_all | solution.py:235
  30.5 2.5 pack.7
  33.0 26.1 %all-to-all-done.1.q_ref = bf16[64,64,128]{2,1,0:T(8,128)(2,1)S(1)} async-done(((bf16[64,64,128]{2,1,0:T(8,128)(2,1)}), bf16[64,64,128]{2,1,0:T(8,128)(2,1)S(1)}, u32[]{:S(2)}, u32[]{:S(2)}) %all-to-all-start.1) | async-done | bytes 1048608 | tf_op jit(solution)/shard_map/all_to_all | solution.py:235
  59.1 6.2 %all-to-all-start.5 = ((bf16[64,64,128]{2,1,0:T(8,128)(2,1)}), bf16[64,64,128]{2,1,0:T(8,128)(2,1)S(1)}, u32[]{:S(2)}, u32[]{:S(2)}) async-start(bf16[64,64,128]{2,1,0:T(8,128)(2,1)} %pack.7), calls=%async_computation.5 | async-start | bytes 2097152 | tf_op jit(solution)/shard_map/all_to_all | solution.py:235
  65.3 1.2 copy-done.9
  66.5 1.2 copy-done.11
  67.8 4.3 %pack.6 = bf16[64,64,384]{2,1,0:T(8,128)(2,1)} custom-call(s32[8,2,256]{2,1,0:T(2,128)S(1)} %reshape.33.slot_ref, bf16[256,2048]{1,0:T(8,128)(2,1)S(1)} %bitcast.40, bf16[256,2048]{1,0:T(8,128)(2,1)S(1)} %bitcast.42, bf16[256,2048]{1,0:T(8,128)(2,1)S(1)} %bitcast.44), custom_call_target="tpu_custom_call" | custom-call | flops 3221225472 | bytes 6291456 | tf_op jit(solution)/shard_map/pack/pallas_call | solution.py:76
  72.0 21.8 %all-to-all-done.5.q_ref = bf16[64,64,128]{2,1,0:T(8,128)(2,1)S(1)} async-done(((bf16[64,64,128]{2,1,0:T(8,128)(2,1)}), bf16[64,64,128]{2,1,0:T(8,128)(2,1)S(1)}, u32[]{:S(2)}, u32[]{:S(2)}) %all-to-all-start.5) | async-done | bytes 1048608 | tf_op jit(solution)/shard_map/all_to_all | solution.py:235
  93.8 1.0 copy-done.3
  94.8 6.2 %all-to-all-start.4 = ((bf16[64,64,384]{2,1,0:T(8,128)(2,1)}), bf16[64,64,384]{2,1,0:T(8,128)(2,1)S(1)}, u32[]{:S(2)}, u32[]{:S(2)}) async-start(bf16[64,64,384]{2,1,0:T(8,128)(2,1)} %pack.6), calls=%async_computation.4 | async-start | bytes 6291456 | tf_op jit(solution)/shard_map/all_to_all | solution.py:235
  101.1 0.7 all-gather.4.cloned.1.call-update
  101.8 1.2 copy-done.8
  103.0 1.2 copy-done.10
  104.2 1.2 copy-done.12
  105.5 4.2 %pack.4 = bf16[64,64,384]{2,1,0:T(8,128)(2,1)} custom-call(s32[8,2,256]{2,1,0:T(2,128)S(1)} %reshape.33.slot_ref, bf16[256,2048]{1,0:T(8,128)(2,1)S(1)} %bitcast.41, bf16[256,2048]{1,0:T(8,128)(2,1)S(1)} %bitcast.43, bf16[256,2048]{1,0:T(8,128)(2,1)S(1)} %bitcast.45), custom_call_target="tpu_custom_call" | custom-call | flops 3221225472 | bytes 6291456 | tf_op jit(solution)/shard_map/pack/pallas_call | solution.py:76
  109.7 64.8 %all-to-all-done.4.kvg_ref = bf16[64,64,384]{2,1,0:T(8,128)(2,1)S(1)} async-done(((bf16[64,64,384]{2,1,0:T(8,128)(2,1)}), bf16[64,64,384]{2,1,0:T(8,128)(2,1)S(1)}, u32[]{:S(2)}, u32[]{:S(2)}) %all-to-all-start.4) | async-done | bytes 3145760 | tf_op jit(solution)/shard_map/all_to_all | solution.py:235
  174.5 6.2 %all-to-all-start = ((bf16[64,64,384]{2,1,0:T(8,128)(2,1)}), bf16[64,64,384]{2,1,0:T(8,128)(2,1)}, u32[]{:S(2)}, u32[]{:S(2)}) async-start(bf16[64,64,384]{2,1,0:T(8,128)(2,1)} %pack.4), calls=%async_computation | async-start | bytes 6291456 | tf_op jit(solution)/shard_map/all_to_all | solution.py:235
  180.8 6.4 %copy.9 = bf16[8192,256]{1,0:T(8,128)(2,1)} copy(bf16[8192,256]{0,1:T(8,128)(2,1)} %all-gather.4.cloned.1.call-done) | data formatting | bytes 8388608 | tf_op jit(solution)/shard_map/all_gather | solution.py:226
  187.2 0.5 collective-permute-start.1
  187.7 1.2 copy-done.4
  188.9 16.1 %attention.3 = bf16[4,32,2,16,128]{4,3,2,1,0:T(8,128)(2,1)S(1)} custom-call(bf16[64,64,384]{2,1,0:T(8,128)(2,1)S(1)} %all-to-all-done.4.kvg_ref, bf16[64,64,128]{2,1,0:T(8,128)(2,1)S(1)} %copy-done.4), custom_call_target="tpu_custom_call" | custom-call | flops 2147483648 | bytes 5242880 | tf_op jit(solution)/shard_map/attention/pallas_call | solution.py:128
  205.0 1.0 copy-done.5
  206.0 48.2 %all-to-all-done.kvg_ref = bf16[64,64,384]{2,1,0:T(8,128)(2,1)} async-done(((bf16[64,64,384]{2,1,0:T(8,128)(2,1)}), bf16[64,64,384]{2,1,0:T(8,128)(2,1)}, u32[]{:S(2)}, u32[]{:S(2)}) %all-to-all-start) | async-done | bytes 3145760 | tf_op jit(solution)/shard_map/all_to_all | solution.py:235
  254.2 8.6 %all-to-all-start.6 = ((bf16[256,16,128]{2,1,0:T(8,128)(2,1)}), bf16[256,16,128]{2,1,0:T(8,128)(2,1)S(1)}, u32[]{:S(2)}, u32[]{:S(2)}) async-start(bf16[256,16,128]{2,1,0:T(8,128)(2,1)} %bitcast.36), calls=%async_computation.6 | async-start | bytes 2097152 | tf_op jit(solution)/shard_map/all_to_all | solution.py:238
  262.8 1.2 copy-done.2
  264.0 17.5 %attention.2 = bf16[4,32,2,16,128]{4,3,2,1,0:T(8,128)(2,1)} custom-call(bf16[64,64,384]{2,1,0:T(8,128)(2,1)} %all-to-all-done.kvg_ref, bf16[64,64,128]{2,1,0:T(8,128)(2,1)S(1)} %copy-done.2), custom_call_target="tpu_custom_call" | custom-call | flops 2147483648 | bytes 5242880 | tf_op jit(solution)/shard_map/attention/pallas_call | solution.py:128
  281.6 13.8 %all-to-all-done.6.rows_ref = bf16[256,16,128]{2,1,0:T(8,128)(2,1)S(1)} async-done(((bf16[256,16,128]{2,1,0:T(8,128)(2,1)}), bf16[256,16,128]{2,1,0:T(8,128)(2,1)S(1)}, u32[]{:S(2)}, u32[]{:S(2)}) %all-to-all-start.6) | async-done | bytes 1048608 | tf_op jit(solution)/shard_map/all_to_all | solution.py:238
  295.3 5.2 %all-to-all-start.2 = ((bf16[256,16,128]{2,1,0:T(8,128)(2,1)}), bf16[256,16,128]{2,1,0:T(8,128)(2,1)S(1)}, u32[]{:S(2)}, u32[]{:S(2)}) async-start(bf16[256,16,128]{2,1,0:T(8,128)(2,1)} %bitcast.8), calls=%async_computation.2 | async-start | bytes 2097152 | tf_op jit(solution)/shard_map/all_to_all | solution.py:238
  300.5 10.0 %all-gather = s32[1024,16]{0,1:T(8,128)S(1)} all-gather(s32[256,16]{0,1:T(8,128)S(1)} %bitcast.37), channel_id=2, replica_groups=mesh['dp'=4,'seq'=64] {'dp'}, dimensions={0}, use_global_device_ids=true | all-gather | bytes 81920 | tf_op jit(solution)/shard_map/all_gather | solution.py:227
  310.5 0.2 copy.8
  310.7 3.7 collective-permute-start
  314.5 1.5 collective-permute-done.slot_b
  315.9 8.0 %weight_grad.3 = bf16[2048,128]{1,0:T(8,128)(2,1)S(1)} custom-call(s32[2]{0:T(128)S(1)} %pad_add_fusion.1.where_ref, bf16[256,16,128]{2,1,0:T(8,128)(2,1)S(1)} %all-to-all-done.6.rows_ref, s32[4,256,16]{2,1,0:T(8,128)S(1)} %bitcast.33, s32[4,256,16]{2,1,0:T(8,128)S(1)} %collective-permute-done.slot_b, bf16[4,2048,256]{2,1,0:T(8,128)(2,1)} %bitcast.47, ...), custom_call_target="tpu_custom_call" | custom-call | flops 2147483648 | bytes 12582912 | tf_op jit(solution)/shard_map/weight_grad/pallas_call | solution.py:183
  324.0 0.9 copy-done
  324.8 7.6 %all-to-all-done.2.rows_ref = bf16[256,16,128]{2,1,0:T(8,128)(2,1)S(1)} async-done(((bf16[256,16,128]{2,1,0:T(8,128)(2,1)}), bf16[256,16,128]{2,1,0:T(8,128)(2,1)S(1)}, u32[]{:S(2)}, u32[]{:S(2)}) %all-to-all-start.2) | async-done | bytes 1048608 | tf_op jit(solution)/shard_map/all_to_all | solution.py:238
  332.4 6.8 %all-to-all-start.7 = ((bf16[256,8,128]{2,1,0:T(8,128)(2,1)}), bf16[256,8,128]{2,1,0:T(8,128)(2,1)}, u32[]{:S(2)}, u32[]{:S(2)}) async-start(bf16[256,8,128]{2,1,0:T(8,128)(2,1)} %bitcast.35), calls=%async_computation.7 | async-start | bytes 1048576 | tf_op jit(solution)/shard_map/all_to_all | solution.py:241
  339.2 0.1 pad_add_fusion.where_ref
  339.3 8.8 %weight_grad.2 = bf16[2048,128]{1,0:T(8,128)(2,1)} custom-call(s32[2]{0:T(128)S(1)} %pad_add_fusion.where_ref, bf16[256,16,128]{2,1,0:T(8,128)(2,1)S(1)} %all-to-all-done.2.rows_ref, s32[4,256,16]{2,1,0:T(8,128)S(1)} %bitcast.34, s32[4,256,16]{2,1,0:T(8,128)S(1)} %collective-permute-done.slot_b, bf16[4,2048,256]{2,1,0:T(8,128)(2,1)} %bitcast.48, ...), custom_call_target="tpu_custom_call" | custom-call | flops 2147483648 | bytes 12582912 | tf_op jit(solution)/shard_map/weight_grad/pallas_call | solution.py:183
  348.1 10.3 %all-to-all-done.7 = bf16[256,8,128]{2,1,0:T(8,128)(2,1)} async-done(((bf16[256,8,128]{2,1,0:T(8,128)(2,1)}), bf16[256,8,128]{2,1,0:T(8,128)(2,1)}, u32[]{:S(2)}, u32[]{:S(2)}) %all-to-all-start.7) | async-done | bytes 524320 | tf_op jit(solution)/shard_map/all_to_all | solution.py:241
  358.4 5.4 %all-to-all-start.3 = ((bf16[256,8,128]{2,1,0:T(8,128)(2,1)}), bf16[256,8,128]{2,1,0:T(8,128)(2,1)S(1)}, u32[]{:S(2)}, u32[]{:S(2)}) async-start(bf16[256,8,128]{2,1,0:T(8,128)(2,1)} %bitcast.13), calls=%async_computation.3 | async-start | bytes 1048576 | tf_op jit(solution)/shard_map/all_to_all | solution.py:241
  363.8 1.1 convert_reduce_fusion
  364.9 20.4 %all-to-all-done.3 = bf16[256,8,128]{2,1,0:T(8,128)(2,1)S(1)} async-done(((bf16[256,8,128]{2,1,0:T(8,128)(2,1)}), bf16[256,8,128]{2,1,0:T(8,128)(2,1)S(1)}, u32[]{:S(2)}, u32[]{:S(2)}) %all-to-all-start.3) | async-done | bytes 524320 | tf_op jit(solution)/shard_map/all_to_all | solution.py:241
  385.5 0.6 maximum_bitcast_fusion
  (21 shorter events, 0.3 us)
Async XLA Ops:
  7.4 0.7 copy-start.6
  17.2 48.1 %copy-start.7 = (bf16[1,256,2048]{2,1,0:T(8,128)(2,1)S(1)}, bf16[1,256,2048]{2,1,0:T(8,128)(2,1)}, u32[]{:S(2)}) copy-start(bf16[1,256,2048]{2,1,0:T(8,128)(2,1)} %param.8) | copy-start | bytes 3145732
  17.2 41.9 %all-to-all-start.1 = ((bf16[64,64,128]{2,1,0:T(8,128)(2,1)}), bf16[64,64,128]{2,1,0:T(8,128)(2,1)S(1)}, u32[]{:S(2)}, u32[]{:S(2)}) async-start(bf16[64,64,128]{2,1,0:T(8,128)(2,1)} %pack.5), calls=%async_computation.1 | async-start | bytes 2097152 | tf_op jit(solution)/shard_map/all_to_all | solution.py:235
  59.1 12.9 %copy-start.1 = (bf16[64,64,128]{2,1,0:T(8,128)(2,1)}, bf16[64,64,128]{2,1,0:T(8,128)(2,1)S(1)}, u32[]{:S(2)}) copy-start(bf16[64,64,128]{2,1,0:T(8,128)(2,1)S(1)} %all-to-all-done.1.q_ref) | copy-start | bytes 3145732
  59.1 34.8 %all-to-all-start.5 = ((bf16[64,64,128]{2,1,0:T(8,128)(2,1)}), bf16[64,64,128]{2,1,0:T(8,128)(2,1)S(1)}, u32[]{:S(2)}, u32[]{:S(2)}) async-start(bf16[64,64,128]{2,1,0:T(8,128)(2,1)} %pack.7), calls=%async_computation.5 | async-start | bytes 2097152 | tf_op jit(solution)/shard_map/all_to_all | solution.py:235
  65.3 1.2 copy-start.9
  66.5 1.2 copy-start.11
  93.8 1.0 copy-start.3
  94.8 79.7 %all-to-all-start.4 = ((bf16[64,64,384]{2,1,0:T(8,128)(2,1)}), bf16[64,64,384]{2,1,0:T(8,128)(2,1)S(1)}, u32[]{:S(2)}, u32[]{:S(2)}) async-start(bf16[64,64,384]{2,1,0:T(8,128)(2,1)} %pack.6), calls=%async_computation.4 | async-start | bytes 6291456 | tf_op jit(solution)/shard_map/all_to_all | solution.py:235
  101.0 79.8 %all-gather.4.cloned.1.call-start = ((), (), s32[]{:S(2)}) async-start(), calls=%async_computation.8 | async-start | bytes 5242880 | tf_op jit(solution)/shard_map/all_gather | solution.py:226
  101.8 1.2 copy-start.8
  103.0 1.2 copy-start.10
  104.2 1.2 copy-start.12
  174.5 79.7 %all-to-all-start = ((bf16[64,64,384]{2,1,0:T(8,128)(2,1)}), bf16[64,64,384]{2,1,0:T(8,128)(2,1)}, u32[]{:S(2)}, u32[]{:S(2)}) async-start(bf16[64,64,384]{2,1,0:T(8,128)(2,1)} %pack.4), calls=%async_computation | async-start | bytes 6291456 | tf_op jit(solution)/shard_map/all_to_all | solution.py:235
  187.2 128.8 %collective-permute-start.1 = (bf16[4,2048,256]{2,1,0:T(8,128)(2,1)}, bf16[4,2048,256]{2,1,0:T(8,128)(2,1)}, u32[]{:S(2)}, u32[]{:S(2)}) collective-permute-start(bf16[4,2048,256]{2,1,0:T(8,128)(2,1)} %bitcast.46), channel_id=1, source_target_pairs={{0,1},{1,0},{2,3},{3,2},{4,5},{5,4},{6,7},{7,6},{8,9},{9,8},{10,11... | collective-permute-start | bytes 12582920 | tf_op jit(solution)/shard_map/ppermute | solution.py:228
  187.7 1.2 copy-start.4
  205.0 1.0 copy-start.5
  254.2 41.1 %all-to-all-start.6 = ((bf16[256,16,128]{2,1,0:T(8,128)(2,1)}), bf16[256,16,128]{2,1,0:T(8,128)(2,1)S(1)}, u32[]{:S(2)}, u32[]{:S(2)}) async-start(bf16[256,16,128]{2,1,0:T(8,128)(2,1)} %bitcast.36), calls=%async_computation.6 | async-start | bytes 2097152 | tf_op jit(solution)/shard_map/all_to_all | solution.py:238
  262.8 1.2 copy-start.2
  295.3 37.1 %all-to-all-start.2 = ((bf16[256,16,128]{2,1,0:T(8,128)(2,1)}), bf16[256,16,128]{2,1,0:T(8,128)(2,1)S(1)}, u32[]{:S(2)}, u32[]{:S(2)}) async-start(bf16[256,16,128]{2,1,0:T(8,128)(2,1)} %bitcast.8), calls=%async_computation.2 | async-start | bytes 2097152 | tf_op jit(solution)/shard_map/all_to_all | solution.py:238
  310.7 5.2 %collective-permute-start = (s32[4,256,16]{2,1,0:T(8,128)S(1)}, s32[4,256,16]{2,1,0:T(8,128)S(1)}, u32[]{:S(2)}, u32[]{:S(2)}) collective-permute-start(s32[4,256,16]{2,1,0:T(8,128)S(1)} %bitcast.32), channel_id=1, source_target_pairs={{0,1},{1,0},{2,3},{3,2},{4,5},{5,4},{6,7},{7,6},{8,9},{9,8},{10,11... | collective-permute-start | bytes 196616 | tf_op jit(solution)/shard_map/ppermute | solution.py:229
  323.9 0.9 copy-start
  332.4 26.0 %all-to-all-start.7 = ((bf16[256,8,128]{2,1,0:T(8,128)(2,1)}), bf16[256,8,128]{2,1,0:T(8,128)(2,1)}, u32[]{:S(2)}, u32[]{:S(2)}) async-start(bf16[256,8,128]{2,1,0:T(8,128)(2,1)} %bitcast.35), calls=%async_computation.7 | async-start | bytes 1048576 | tf_op jit(solution)/shard_map/all_to_all | solution.py:241
  358.4 27.0 %all-to-all-start.3 = ((bf16[256,8,128]{2,1,0:T(8,128)(2,1)}), bf16[256,8,128]{2,1,0:T(8,128)(2,1)S(1)}, u32[]{:S(2)}, u32[]{:S(2)}) async-start(bf16[256,8,128]{2,1,0:T(8,128)(2,1)} %bitcast.13), calls=%async_computation.3 | async-start | bytes 1048576 | tf_op jit(solution)/shard_map/all_to_all | solution.py:241
Sparse Core Ops, SparseCore 0:
  103.7 51.7 all-gather.3

commit v2 on v1

--- a/solution.py
+++ b/solution.py
@@ -88,7 +88,7 @@
     )(slots.reshape(HEADS // 2, 2, TOK), *sources)
 
 
-def attention_kernel(kvg_ref, q_ref, out_ref, bias_ref):
+def attention_kernel(in_ref, out_ref, bias_ref):
     scale = 1.0 / math.sqrt(HEAD)
     to_exp2 = scale * math.log2(math.e)
 
@@ -100,13 +100,11 @@
         bias_ref[...] = jnp.where(keep, 0.0, -1e30)
 
     first = jnp.where(lax.broadcasted_iota(jnp.int32, (8, HEAD), 1) == 0, 1.0, 0.0).astype(BF)
-    kvg_pair = kvg_ref[...].astype(F32)
-    q_pair = q_ref[...].astype(F32)
-    step = 128
+    pair = in_ref[...].astype(F32)
+    step = 256
     for e in range(2):
-        kvg = kvg_pair[:, e * CELL : (e + 1) * CELL, :].reshape(SLOTS, 3 * HEAD).astype(BF)
-        q = q_pair[:, e * CELL : (e + 1) * CELL, :].reshape(SLOTS, HEAD).astype(BF)
-        k, v, g = (kvg[:, n * HEAD : (n + 1) * HEAD] for n in range(3))
+        rows = pair[:, e * CELL : (e + 1) * CELL, :].reshape(SLOTS, 4 * HEAD).astype(BF)
+        k, v, g, q = (rows[:, n * HEAD : (n + 1) * HEAD] for n in range(4))
         key_bias = jnp.where(dot(first, k, NT)[0:1, :] > 0.5 * EMPTY, -1e30, 0.0)
         for i in range(SLOTS // step):
             here = slice(i * step, (i + 1) * step)
@@ -124,14 +122,11 @@
             out_ref[0, i * tiles : (i + 1) * tiles, e] = dquery.reshape(tiles, 2 * CELL, HEAD)
 
 
-def attention(kvg, q):
+def attention(got):
     return pl.pallas_call(
         attention_kernel,
         grid=(HPC // 2,),
-        in_specs=[
-            pl.BlockSpec((OWNERS, 2 * CELL, 3 * HEAD), lambda p: (0, p, 0)),
-            pl.BlockSpec((OWNERS, 2 * CELL, HEAD), lambda p: (0, p, 0)),
-        ],
+        in_specs=[pl.BlockSpec((OWNERS, 2 * CELL, 4 * HEAD), lambda p: (0, p, 0))],
         out_specs=pl.BlockSpec((1, OWNERS // 2, 2, 2 * CELL, HEAD), lambda p: (p, 0, 0, 0, 0)),
         out_shape=jax.ShapeDtypeStruct((HPC // 2, OWNERS // 2, 2, 2 * CELL, HEAD), BF),
         scratch_shapes=[pltpu.VMEM((SLOTS, SLOTS), F32)],
@@ -142,22 +137,25 @@
             transcendentals=HPC * SLOTS * SLOTS,
         ),
         name="attention",
-    )(kvg, q)
-
-
-def grad_kernel(where_ref, rows_ref, slot_a, slot_b, act_a, act_b, out_ref, acc_ref):
+    )(got)
+
+
+def grad_kernel(where_ref, rows_ref, act_a, act_b, *refs):
+    earlier_ref, out_ref, acc_ref = refs if len(refs) == 3 else (None, *refs)
     b = pl.program_id(0)
     head, core = where_ref[0], where_ref[1]
+    features = acc_ref.shape[0]
     rows = rows_ref[...].reshape(OWNERS * 2 * CELL, HEAD)
-    lane = lax.broadcasted_iota(jnp.int32, (TOK, HEADS), 1)
-    place = lax.broadcasted_iota(jnp.int32, (TOK, OWNERS * 2 * CELL), 1)
+    line = lax.broadcasted_iota(jnp.int32, (2 * HEADS, TOK), 0)
+    place = lax.broadcasted_iota(jnp.int32, (OWNERS * 2 * CELL, TOK), 0)
     total = None
-    for slot_ref, act_ref, side in ((slot_a, act_a, core), (slot_b, act_b, 1 - core)):
-        slot = jnp.sum(jnp.where(lane == head, slot_ref[0], 0), axis=1, keepdims=True)
-        index = (slot // CELL) * (2 * CELL) + side * CELL + slot % CELL
+    for act_ref, side in ((act_a, core), (act_b, 1 - core)):
+        slot = act_ref[0, features:, :].astype(F32)
+        weight = jnp.where(line == head, 2.0 * CELL, jnp.where(line == HEADS + head, 1.0, 0.0))
+        index = jnp.sum(slot * weight, axis=0, keepdims=True).astype(jnp.int32) + side * CELL
         hot = jnp.where(place == index, 1.0, 0.0).astype(BF)
-        dquery = dot(hot, rows, NN).astype(BF)
-        term = dot(act_ref[0], dquery, NN)
+        dquery = dot(rows, hot, ((0,), (0,))).astype(BF)
+        term = dot(act_ref[0, :features, :], dquery, NT)
         total = term if total is None else total + term
 
     @pl.when(b == 0)
@@ -170,32 +168,41 @@
 
     @pl.when(b == pl.num_programs(0) - 1)
     def _():
-        out_ref[...] = acc_ref[...].astype(BF)
-
-
-def weight_grad(where, rows, slots, acts, features, seqs):
-    def slot_spec():
-        return pl.BlockSpec((1, TOK, HEADS), lambda b, w: (b, 0, 0))
-
+        if earlier_ref is None:
+            out_ref[...] = acc_ref[...]
+        else:
+            both = [ref[...].reshape(-1, CELL, HEAD) for ref in (earlier_ref, acc_ref)]
+            out_ref[...] = jnp.concatenate(both, axis=1).astype(BF)
+
+
+def weight_grad(where, rows, acts, features, seqs, earlier):
     def act_spec():
-        return pl.BlockSpec((1, features, TOK), lambda b, w: (b, 0, 0))
-
+        return pl.BlockSpec((1, features + 2 * HEADS, TOK), lambda b, w: (b, 0, 0))
+
+    in_specs = [
+        pl.BlockSpec((OWNERS, 2 * CELL, HEAD), lambda b, w: (b, 0, 0)),
+        act_spec(),
+        act_spec(),
+    ]
+    if earlier is None:
+        out = jax.ShapeDtypeStruct((features, HEAD), F32)
+        out_spec = pl.BlockSpec((features, HEAD), lambda b, w: (0, 0))
+        more = ()
+    else:
+        out = jax.ShapeDtypeStruct((features // CELL, 2 * CELL, HEAD), BF)
+        out_spec = pl.BlockSpec((features // CELL, 2 * CELL, HEAD), lambda b, w: (0, 0, 0))
+        in_specs.append(pl.BlockSpec((features, HEAD), lambda b, w: (0, 0)))
+        more = (earlier,)
     return pl.pallas_call(
         grad_kernel,
         grid_spec=pltpu.PrefetchScalarGridSpec(
             num_scalar_prefetch=1,
             grid=(seqs,),
-            in_specs=[
-                pl.BlockSpec((OWNERS, 2 * CELL, HEAD), lambda b, w: (b, 0, 0)),
-                slot_spec(),
-                slot_spec(),
-                act_spec(),
-                act_spec(),
-            ],
-            out_specs=pl.BlockSpec((features, HEAD), lambda b, w: (0, 0)),
+            in_specs=in_specs,
+            out_specs=out_spec,
             scratch_shapes=[pltpu.VMEM((features, HEAD), F32)],
         ),
-        out_shape=jax.ShapeDtypeStruct((features, HEAD), BF),
+        out_shape=out,
         compiler_params=params("arbitrary"),
         cost_estimate=pl.CostEstimate(
             flops=4 * seqs * TOK * features * HEAD * 2,
@@ -203,7 +210,7 @@
             transcendentals=0,
         ),
         name="weight_grad",
-    )(where, rows, *slots, *acts)
+    )(where, rows, *acts, *more)
 
 
 def on_device(activations, w_query, all_keys, values, grad_out, cluster):
@@ -218,32 +225,38 @@
     all_send = functools.partial(
         lax.all_to_all, axis_name=("dp", "seq"), split_axis=0, concat_axis=0, tiled=True
     )
-    kvg = [pack(slots, c, True, all_keys[0], values[0], grad_out[0]) for c in range(CHUNKS)]
     queries = jnp.dot(tokens_here, w_query, preferred_element_type=F32).astype(BF)
-    q = [pack(slots, c, False, queries) for c in range(CHUNKS)]
+    sent = [
+        pack(slots, c, True, all_keys[0], values[0], grad_out[0], queries) for c in range(CHUNKS)
+    ]
 
     swap = [(i, i ^ 1) for i in range(OWNERS)]
-    acts_mine = lax.all_gather(tokens_here.T, "dp")
-    slots_mine = lax.all_gather(slots.T, "dp")
+    carried = jnp.concatenate(
+        [tokens_here.T, (slots // CELL).astype(BF), (slots % CELL).astype(BF)], axis=0
+    )
+    acts_mine = lax.all_gather(carried, "dp")
     acts = (acts_mine, lax.ppermute(acts_mine, "seq", swap))
-    slot_cols = (slots_mine, lax.ppermute(slots_mine, "seq", swap))
     core = lax.axis_index("seq") % 2
     group = lax.axis_index("dp") * 2 + core
 
-    sums = []
+    got, last = [], None
     for c in range(CHUNKS):
-        got_kvg, got_q = seq_send(kvg[c]), seq_send(q[c])
-        rows = attention(got_kvg, got_q)
-        rows = rows.reshape(HPC // 2, OWNERS // 2, 2, 2 * CELL, HEAD)
+        block = sent[c]
+        if last is not None:
+            block, got[-1] = lax.optimization_barrier((block, last))
+        last = seq_send(block)
+        got.append(last)
+    part = None
+    for c in range(CHUNKS):
+        rows = attention(got[c])
         back = all_send(rows.reshape(devices, 2 * CELL, HEAD))
         where = jnp.stack([c * HPC + group, core]).astype(jnp.int32)
-        part = weight_grad(where, back, slot_cols, acts, features, seqs)
-        got = all_send(part.reshape(devices, features // devices, HEAD))
-        got = got.reshape(seqs, OWNERS // 2, 2, features // devices, HEAD)
-        total = jnp.sum(got.astype(F32), axis=1)
-        sums.append(total.reshape(HPC, features // devices, HEAD))
-    out = jnp.concatenate(sums, axis=0)
-    return out.transpose(1, 0, 2).reshape(features // devices, HEADS * HEAD)
+        part = weight_grad(where, back, acts, features, seqs, part)
+    terms = all_send(part)
+    terms = terms.reshape(seqs, OWNERS // 2, 2, CHUNKS, features // devices, HEAD)
+    out = jnp.sum(terms.astype(F32), axis=1)
+    out = out.transpose(3, 2, 0, 1, 4)
+    return out.reshape(features // devices, HEADS * HEAD)
 
 
 def solution(mesh):

time: 394 us -> 362 us (0.919)
  starting transfers between devices: 62.1 us -> 33.4 us
  blocking collectives: 9.99 us -> 36.9 us
  Pallas kernels: 64.4 us -> 47 us
  local copies, waits for them, and re-layouts: 19.5 us -> 4.93 us
    all_to_all x6 -> x2, waiting for transfers between devices: 192 us -> 119 us  [on_device(): last = seq_send(block)]
    all_gather x1, waiting for transfers between devices: 0.02 us -> 53.3 us  [on_device(): acts_mine = lax.all_gather(carried, 'dp')]
    all_to_all x0 -> x1, blocking collectives: none -> 36.9 us  [on_device(): terms = all_send(part)]
    all_to_all x6 -> x2, starting transfers between devices: 44.1 us -> 19.3 us  [on_device(): last = seq_send(block)]
    all_to_all x2, waiting for transfers between devices: 21.3 us -> 46 us  [on_device(): back = all_send(rows.reshape(devices, 2 * CELL, HEAD))]
    pallas_call x2, Pallas kernels: 33.6 us -> 22.2 us  [attention(): pl.pallas_call(attention_kernel, grid=(HPC // 2,), in_specs=[pl.BlockSpec...]
    all_gather x1 -> x0, blocking collectives: 9.99 us -> none  [on_device(): slots_mine = lax.all_gather(slots.T, 'dp')]
    unnamed x26 -> x15, local copies, waits for them, and re-layouts: 12.1 us -> 3.46 us
  transfers between devices with their start and end apart: 11 -> 6, of which waited for: 9 -> 5; matrix products, arithmetic and copies ran while one was open for 2% -> 0% of each run, Pallas kernels for 16% -> 9%
where the time goes in v2:
time: 362 us; the launch traced here: 361 us
  waiting for transfers between devices  218 us (60%)
  Pallas kernels  47 us (13%)
  blocking collectives  36.9 us (10%)
  starting transfers between devices  33.4 us (9%)
  between operations  13.6 us (4%)
  matrix products  6.18 us (2%)
  local copies, waits for them, and re-layouts  4.93 us (1%)
    all_to_all x2, waiting for transfers between devices, on_device(): last = seq_send(block)  119 us
    all_gather x1, waiting for transfers between devices, on_device(): acts_mine = lax.all_gather(carried, 'dp')  53.3 us
    all_to_all x2, waiting for transfers between devices, on_device(): back = all_send(rows.reshape(devices, 2 * CELL, HEAD))  46 us
    all_to_all x1, blocking collectives, on_device(): terms = all_send(part)  36.9 us
    pallas_call x2, Pallas kernels, attention(): pl.pallas_call(attention_kernel, grid=(HPC // 2,), in_specs=[pl.BlockSpec...  22.2 us
    all_to_all x2, starting transfers between devices, on_device(): last = seq_send(block)  19.3 us
    pallas_call x2, Pallas kernels, weight_grad(): pl.pallas_call(grad_kernel, grid_spec=pltpu.PrefetchScalarGridSpec(num_sc...  14.3 us
    all_to_all x2, starting transfers between devices, on_device(): back = all_send(rows.reshape(devices, 2 * CELL, HEAD))  13.4 us
  transfers between devices with their start and end apart: 6, of which 5 were waited for; matrix products, arithmetic and copies ran while one was open for 0% of the time, Pallas kernels for 9%

profile of v2, /device:TPU:1, one launch (start us, length us, event | category | flops | bytes accessed | tf_op | source)
XLA Modules:
  0.0 361.5 jit_solution(11296274617524515418)
XLA Ops:
  6.5 0.8 copy.13.col_ref
  7.4 0.0 copy-start
  7.4 0.7 copy-done
  8.1 0.6 slots.1
  8.7 0.0 copy-start.1
  8.7 0.0 copy-start.2
  8.8 0.0 copy-start.3
  8.8 6.2 %convolution_convert_fusion.refs_3_ = bf16[256,2048]{1,0:T(8,128)(2,1)S(1)} fusion(bf16[2048,2048]{1,0:T(8,128)(2,1)} %param.7, bf16[1,256,2048]{2,1,0:T(8,128)(2,1)} %param.6), kind=kOutput, calls=%fused_computation | convolution fusion | flops 2148007936 | bytes 10485760 | tf_op jit(solution)/shard_map/dot_general | solution.py:228
  15.0 0.0 copy-done.1
  15.0 0.0 copy-done.2
  15.0 0.0 copy-done.3
  15.0 4.9 %pack.3 = bf16[64,64,512]{2,1,0:T(8,128)(2,1)} custom-call(s32[8,2,256]{2,1,0:T(2,128)S(1)} %reshape.16.slot_ref, bf16[256,2048]{1,0:T(8,128)(2,1)S(1)} %bitcast.25, bf16[256,2048]{1,0:T(8,128)(2,1)S(1)} %bitcast.27, bf16[256,2048]{1,0:T(8,128)(2,1)S(1)} %bitcast.29, bf16[256,2048]{1,0:T(8,128)(2,1)S(1)} %convolution_convert_fusion.refs_3_), custom_call_target="tpu_custom_call" | custom-call | flops 4294967296 | bytes 6291456 | tf_op jit(solution)/shard_map/pack/pallas_call | solution.py:76
  19.9 0.0 copy-start.4
  19.9 1.0 copy-done.4
  20.9 13.3 %all-to-all-start = ((bf16[64,64,512]{2,1,0:T(8,128)(2,1)}), bf16[64,64,512]{2,1,0:T(8,128)(2,1)}, u32[]{:S(2)}, u32[]{:S(2)}) async-start(bf16[64,64,512]{2,1,0:T(8,128)(2,1)} %pack.3), calls=%async_computation | async-start | bytes 8388608 | tf_op jit(solution)/shard_map/all_to_all | solution.py:247
  34.2 0.0 copy-start.5
  34.2 1.2 copy-done.5
  35.5 4.9 %pack.2 = bf16[64,64,512]{2,1,0:T(8,128)(2,1)} custom-call(s32[8,2,256]{2,1,0:T(2,128)S(1)} %reshape.16.slot_ref, bf16[256,2048]{1,0:T(8,128)(2,1)S(1)} %bitcast.26, bf16[256,2048]{1,0:T(8,128)(2,1)S(1)} %bitcast.28, bf16[256,2048]{1,0:T(8,128)(2,1)S(1)} %bitcast.30, bf16[256,2048]{1,0:T(8,128)(2,1)S(1)} %copy-done.5), custom_call_target="tpu_custom_call" | custom-call | flops 4294967296 | bytes 6291456 | tf_op jit(solution)/shard_map/pack/pallas_call | solution.py:76
  40.4 0.0 copy-start.6
  40.4 89.7 %all-to-all-done.in_ref = bf16[64,64,512]{2,1,0:T(8,128)(2,1)} async-done(((bf16[64,64,512]{2,1,0:T(8,128)(2,1)}), bf16[64,64,512]{2,1,0:T(8,128)(2,1)}, u32[]{:S(2)}, u32[]{:S(2)}) %all-to-all-start) | async-done | bytes 4194336 | tf_op jit(solution)/shard_map/all_to_all | solution.py:247
  130.1 5.9 %all-to-all-start.1 = ((bf16[64,64,512]{2,1,0:T(8,128)(2,1)}), bf16[64,64,512]{2,1,0:T(8,128)(2,1)}, u32[]{:S(2)}, u32[]{:S(2)}) async-start(bf16[64,64,512]{2,1,0:T(8,128)(2,1)} %pack.2), calls=%async_computation.1 | async-start | bytes 8388608 | tf_op jit(solution)/shard_map/all_to_all | solution.py:247
  136.1 0.0 all-gather.3.cloned.1.call-start
  136.1 0.0 copy-done.6
  136.1 0.5 copy.14
  136.7 1.1 pad_maximum_fusion
  137.7 0.0 all-gather.3.cloned.1.call-update
  137.8 53.3 %all-gather.3.cloned.1.call-done = bf16[8320,256]{1,0:T(8,128)(2,1)} async-done(((bf16[2080,256]{1,0:T(8,128)(2,1)}), bf16[8320,256]{1,0:T(8,128)(2,1)}) %all-gather.3.cloned.1.call-update) | async-done | bytes 4259856 | tf_op jit(solution)/shard_map/all_gather | solution.py:237
  191.0 0.7 collective-permute-start
  191.7 11.1 %attention.3 = bf16[4,32,2,16,128]{4,3,2,1,0:T(8,128)(2,1)} custom-call(bf16[64,64,512]{2,1,0:T(8,128)(2,1)} %all-to-all-done.in_ref), custom_call_target="tpu_custom_call" | custom-call | flops 2147483648 | bytes 5242880 | tf_op jit(solution)/shard_map/attention/pallas_call | solution.py:126
  202.8 29.1 %all-to-all-done.1.in_ref = bf16[64,64,512]{2,1,0:T(8,128)(2,1)} async-done(((bf16[64,64,512]{2,1,0:T(8,128)(2,1)}), bf16[64,64,512]{2,1,0:T(8,128)(2,1)}, u32[]{:S(2)}, u32[]{:S(2)}) %all-to-all-start.1) | async-done | bytes 4194336 | tf_op jit(solution)/shard_map/all_to_all | solution.py:247
  231.9 8.3 %all-to-all-start.3 = ((bf16[256,16,128]{2,1,0:T(8,128)(2,1)}), bf16[256,16,128]{2,1,0:T(8,128)(2,1)S(1)}, u32[]{:S(2)}, u32[]{:S(2)}) async-start(bf16[256,16,128]{2,1,0:T(8,128)(2,1)} %bitcast.12), calls=%async_computation.3 | async-start | bytes 2097152 | tf_op jit(solution)/shard_map/all_to_all | solution.py:252
  240.2 11.1 %attention.2 = bf16[4,32,2,16,128]{4,3,2,1,0:T(8,128)(2,1)} custom-call(bf16[64,64,512]{2,1,0:T(8,128)(2,1)} %all-to-all-done.1.in_ref), custom_call_target="tpu_custom_call" | custom-call | flops 2147483648 | bytes 5242880 | tf_op jit(solution)/shard_map/attention/pallas_call | solution.py:126
  251.3 21.4 %all-to-all-done.3.rows_ref = bf16[256,16,128]{2,1,0:T(8,128)(2,1)S(1)} async-done(((bf16[256,16,128]{2,1,0:T(8,128)(2,1)}), bf16[256,16,128]{2,1,0:T(8,128)(2,1)S(1)}, u32[]{:S(2)}, u32[]{:S(2)}) %all-to-all-start.3) | async-done | bytes 1048608 | tf_op jit(solution)/shard_map/all_to_all | solution.py:252
  272.7 5.2 %all-to-all-start.2 = ((bf16[256,16,128]{2,1,0:T(8,128)(2,1)}), bf16[256,16,128]{2,1,0:T(8,128)(2,1)S(1)}, u32[]{:S(2)}, u32[]{:S(2)}) async-start(bf16[256,16,128]{2,1,0:T(8,128)(2,1)} %bitcast.8), calls=%async_computation.2 | async-start | bytes 2097152 | tf_op jit(solution)/shard_map/all_to_all | solution.py:252
  277.9 0.1 pad_add_fusion.where_ref
  278.0 0.1 pad_add_fusion.1.where_ref
  278.0 0.0 collective-permute-done.act_b
  278.0 7.2 %weight_grad.2.refs_0_ = f32[2048,128]{1,0:T(8,128)S(1)} custom-call(s32[2]{0:T(128)S(1)} %pad_add_fusion.1.where_ref, bf16[256,16,128]{2,1,0:T(8,128)(2,1)S(1)} %all-to-all-done.3.rows_ref, bf16[4,2080,256]{2,1,0:T(8,128)(2,1)} %bitcast.32, bf16[4,2080,256]{2,1,0:T(8,128)(2,1)} %collective-permute-done.act_b), custom_call_target="tpu_custom_call" | custom-call | flops 2147483648 | bytes 12582912 | tf_op jit(solution)/shard_map/weight_grad/pallas_call | solution.py:196
  285.2 24.6 %all-to-all-done.2.rows_ref = bf16[256,16,128]{2,1,0:T(8,128)(2,1)S(1)} async-done(((bf16[256,16,128]{2,1,0:T(8,128)(2,1)}), bf16[256,16,128]{2,1,0:T(8,128)(2,1)S(1)}, u32[]{:S(2)}, u32[]{:S(2)}) %all-to-all-start.2) | async-done | bytes 1048608 | tf_op jit(solution)/shard_map/all_to_all | solution.py:252
  309.8 7.2 %weight_grad.3 = bf16[256,16,128]{2,1,0:T(8,128)(2,1)S(1)} custom-call(s32[2]{0:T(128)S(1)} %pad_add_fusion.where_ref, bf16[256,16,128]{2,1,0:T(8,128)(2,1)S(1)} %all-to-all-done.2.rows_ref, bf16[4,2080,256]{2,1,0:T(8,128)(2,1)} %bitcast.33, bf16[4,2080,256]{2,1,0:T(8,128)(2,1)} %collective-permute-done.act_b, f32[2048,128]{1,0:T(8,128)S(1)} %weight_grad.2.refs_0_), custom_call_target="tpu_custom_call" | custom-call | flops 2147483648 | bytes 12582912 | tf_op jit(solution)/shard_map/weight_grad/pallas_call | solution.py:196
  317.0 36.9 %all_to_all.25 = bf16[256,16,128]{2,1,0:T(8,128)(2,1)S(1)} all-to-all(bf16[256,16,128]{2,1,0:T(8,128)(2,1)S(1)} %weight_grad.3), channel_id=1, replica_groups=mesh['dp'=4,'seq'=64] {'dp','seq'}, dimensions={0} | all-to-all | bytes 2097152 | tf_op jit(solution)/shard_map/all_to_all | solution.py:255
  353.9 0.1 convert_reduce_fusion
  354.0 0.6 copy.15
  (2 shorter events, 0.0 us)
Async XLA Ops:
  7.4 0.7 copy-start
  8.7 6.2 %copy-start.1 = (bf16[1,256,2048]{2,1,0:T(8,128)(2,1)S(1)}, bf16[1,256,2048]{2,1,0:T(8,128)(2,1)}, u32[]{:S(2)}) copy-start(bf16[1,256,2048]{2,1,0:T(8,128)(2,1)} %param.8) | copy-start | bytes 3145732
  8.7 6.2 %copy-start.2 = (bf16[1,256,2048]{2,1,0:T(8,128)(2,1)S(1)}, bf16[1,256,2048]{2,1,0:T(8,128)(2,1)}, u32[]{:S(2)}) copy-start(bf16[1,256,2048]{2,1,0:T(8,128)(2,1)} %param.9) | copy-start | bytes 3145732
  8.8 6.2 %copy-start.3 = (bf16[1,256,2048]{2,1,0:T(8,128)(2,1)S(1)}, bf16[1,256,2048]{2,1,0:T(8,128)(2,1)}, u32[]{:S(2)}) copy-start(bf16[1,256,2048]{2,1,0:T(8,128)(2,1)} %param.10) | copy-start | bytes 3145732
  19.9 1.0 copy-start.4
  20.9 109.2 %all-to-all-start = ((bf16[64,64,512]{2,1,0:T(8,128)(2,1)}), bf16[64,64,512]{2,1,0:T(8,128)(2,1)}, u32[]{:S(2)}, u32[]{:S(2)}) async-start(bf16[64,64,512]{2,1,0:T(8,128)(2,1)} %pack.3), calls=%async_computation | async-start | bytes 8388608 | tf_op jit(solution)/shard_map/all_to_all | solution.py:247
  34.2 1.2 copy-start.5
  40.4 95.7 %copy-start.6 = (bf16[1,256,2048]{2,1,0:T(8,128)(2,1)S(1)}, bf16[1,256,2048]{2,1,0:T(8,128)(2,1)}, u32[]{:S(2)}) copy-start(bf16[1,256,2048]{2,1,0:T(8,128)(2,1)} %param.6) | copy-start | bytes 3145732
  130.1 101.8 %all-to-all-start.1 = ((bf16[64,64,512]{2,1,0:T(8,128)(2,1)}), bf16[64,64,512]{2,1,0:T(8,128)(2,1)}, u32[]{:S(2)}, u32[]{:S(2)}) async-start(bf16[64,64,512]{2,1,0:T(8,128)(2,1)} %pack.2), calls=%async_computation.1 | async-start | bytes 8388608 | tf_op jit(solution)/shard_map/all_to_all | solution.py:247
  136.1 55.0 %all-gather.3.cloned.1.call-start = ((), (), s32[]{:S(2)}) async-start(), calls=%async_computation.5 | async-start | bytes 5324800 | tf_op jit(solution)/shard_map/all_gather | solution.py:237
  191.0 87.0 %collective-permute-start = (bf16[4,2080,256]{2,1,0:T(8,128)(2,1)}, bf16[4,2080,256]{2,1,0:T(8,128)(2,1)}, u32[]{:S(2)}, u32[]{:S(2)}) collective-permute-start(bf16[4,2080,256]{2,1,0:T(8,128)(2,1)} %bitcast.31), channel_id=1, source_target_pairs={{0,1},{1,0},{2,3},{3,2},{4,5},{5,4},{6,7},{7,6},{8,9},{9,8},{10,11... | collective-permute-start | bytes 12779528 | tf_op jit(solution)/shard_map/ppermute | solution.py:238
  231.9 40.8 %all-to-all-start.3 = ((bf16[256,16,128]{2,1,0:T(8,128)(2,1)}), bf16[256,16,128]{2,1,0:T(8,128)(2,1)S(1)}, u32[]{:S(2)}, u32[]{:S(2)}) async-start(bf16[256,16,128]{2,1,0:T(8,128)(2,1)} %bitcast.12), calls=%async_computation.3 | async-start | bytes 2097152 | tf_op jit(solution)/shard_map/all_to_all | solution.py:252
  272.7 37.1 %all-to-all-start.2 = ((bf16[256,16,128]{2,1,0:T(8,128)(2,1)}), bf16[256,16,128]{2,1,0:T(8,128)(2,1)S(1)}, u32[]{:S(2)}, u32[]{:S(2)}) async-start(bf16[256,16,128]{2,1,0:T(8,128)(2,1)} %bitcast.8), calls=%async_computation.2 | async-start | bytes 2097152 | tf_op jit(solution)/shard_map/all_to_all | solution.py:252
Sparse Core Ops, SparseCore 0:
  138.7 52.2 all-gather.2

commit v3 on v2

--- a/solution.py
+++ b/solution.py
@@ -14,8 +14,12 @@
 CELL = 8
 SLOTS = OWNERS * CELL
 HEADS = 16
+CARRIED = 2 * HEADS
 CHUNKS = 2
 HPC = HEADS // CHUNKS
+COMPACT = 96
+GROUP = 16
+FILLS = 4
 EMPTY = 128.0
 VMEM = 48 * 1024 * 1024
 BF = jnp.bfloat16
@@ -30,28 +34,156 @@
 NT = ((1,), (1,))
 
 
-def params(*semantics):
-    return pltpu.CompilerParams(vmem_limit_bytes=VMEM, dimension_semantics=semantics or None)
-
-
-def slot_kernel(col_ref, row_ref, out_ref):
+def params(*semantics, vmem=VMEM):
+    return pltpu.CompilerParams(vmem_limit_bytes=vmem, dimension_semantics=semantics or None)
+
+
+def slot_kernel(col_ref, row_ref, out_ref, held_ref, row_of_ref, over_ref):
     earlier = lax.broadcasted_iota(jnp.int32, (TOK, TOK), 0) < lax.broadcasted_iota(
         jnp.int32, (TOK, TOK), 1
     )
+    owners = lax.broadcasted_iota(jnp.int32, (OWNERS, TOK), 0)
+    lanes = lax.broadcasted_iota(jnp.int32, (HEADS * CELL, TOK), 0)
+    held = None
     for h in range(HEADS):
         row = row_ref[h : h + 1, :]
         same = (col_ref[:, h : h + 1] == row) & earlier
         rank = jnp.sum(jnp.where(same, 1, 0), axis=0, keepdims=True)
-        out_ref[h : h + 1, :] = (row % OWNERS) * CELL + (row // OWNERS) * 2 + rank
+        owner = (row + 4 * h + row // OWNERS) % OWNERS
+        cell = (row // OWNERS) * 2 + rank
+        out_ref[h : h + 1, :] = owner * CELL + cell
+        to_owner = jnp.where(owners == owner, 1.0, 0.0).astype(BF)
+        to_lane = jnp.where(lanes == h * CELL + cell, 1.0, 0.0).astype(BF)
+        term = dot(to_owner, to_lane, NT)
+        held = term if held is None else held + term
+    held_ref[...] = held
+    before = lax.broadcasted_iota(jnp.int32, (HEADS * CELL, HEADS * CELL), 0) < (
+        lax.broadcasted_iota(jnp.int32, (HEADS * CELL, HEADS * CELL), 1)
+    )
+    rank = dot(held.astype(BF), jnp.where(before, 1.0, 0.0).astype(BF), NN)
+    row_of = jnp.where(held > 0.5, rank + 1.0, -1.0)
+    row_of_ref[...] = row_of
+    most = jnp.max(jnp.max(row_of, axis=0, keepdims=True), axis=1, keepdims=True)
+    over_ref[...] = jnp.broadcast_to(jnp.where(most >= COMPACT, 1.0, 0.0), over_ref.shape)
 
 
 def slots_of(assign):
+    per_owner = jax.ShapeDtypeStruct((OWNERS, HEADS * CELL), F32)
     return pl.pallas_call(
         slot_kernel,
-        out_shape=jax.ShapeDtypeStruct((HEADS, TOK), jnp.int32),
+        out_shape=(
+            jax.ShapeDtypeStruct((HEADS, TOK), jnp.int32),
+            per_owner,
+            per_owner,
+            jax.ShapeDtypeStruct((8, HEAD), F32),
+        ),
         compiler_params=params(),
         name="slots",
     )(assign, assign.T)
+
+
+def compact_kernel(slot_ref, row_of_ref, held_ref, flag_ref, one_ref, two_ref, out_ref, buf_ref):
+    p = pl.program_id(0)
+
+    @pl.when(p < FILLS)
+    def _():
+        place = lax.broadcasted_iota(jnp.int32, (SLOTS, TOK), 0)
+        for e in range(0, HEADS // FILLS, 2):
+            parts = []
+            for h in (e, e + 1):
+                hot = jnp.where(place == slot_ref[0, h : h + 1, :], 1.0, 0.0).astype(BF)
+                here = slice(h * HEAD, (h + 1) * HEAD)
+                both = jnp.concatenate([one_ref[:, here], two_ref[:, here]], axis=1)
+                parts.append(dot(hot, both, NN).reshape(OWNERS, CELL, 2 * HEAD))
+            first = p * (HEADS // FILLS) * CELL + e * CELL
+            at = pl.ds(pl.multiple_of(first, 2 * CELL), 2 * CELL)
+            buf_ref[:, at, :] = jnp.concatenate(parts, axis=1).astype(BF)
+
+    @pl.when(p >= FILLS)
+    def _():
+        first = pl.multiple_of((p - FILLS) * GROUP, GROUP)
+        row_of = row_of_ref[pl.ds(first, GROUP), :]
+        row_of = jnp.where(row_of < COMPACT, row_of, -2.0 * COMPACT).astype(jnp.int32)
+        held = held_ref[pl.ds(first, GROUP), :]
+        notes = jnp.concatenate([held, jnp.broadcast_to(flag_ref[0:1, :], held.shape)], axis=1)
+        place = lax.broadcasted_iota(jnp.int32, (2 * COMPACT, 2 * HEAD), 0)
+        line = lax.broadcasted_iota(jnp.int32, (2 * CELL, 2 * HEAD), 0)
+        for d in range(0, GROUP, 2):
+            target = jnp.concatenate([row_of[d : d + 1], row_of[d + 1 : d + 2] + COMPACT], axis=1)
+            hot = jnp.where(place == target, 1.0, 0.0).astype(BF)
+            rows = buf_ref[pl.ds(first + d, 2)].reshape(2 * HEADS * CELL, 2 * HEAD)
+            block = dot(hot, rows, NN)
+            for e in range(2):
+                mine = block[e * COMPACT : (e + 1) * COMPACT]
+                top = jnp.where(line == 0, notes[d + e : d + e + 1], mine[: 2 * CELL])
+                out_ref[d + e] = jnp.concatenate([top, mine[2 * CELL :]], axis=0).astype(BF)
+
+
+def compact(slots, row_of, held, flag, one, two):
+    groups = OWNERS // GROUP
+    share = HEADS // FILLS
+    whole = pl.BlockSpec((OWNERS, HEADS * CELL), lambda p: (0, 0))
+    source = pl.BlockSpec((TOK, share * HEAD), lambda p: (0, jnp.minimum(p, FILLS - 1)))
+    return pl.pallas_call(
+        compact_kernel,
+        grid=(FILLS + groups,),
+        in_specs=[
+            pl.BlockSpec((1, share, TOK), lambda p: (jnp.minimum(p, FILLS - 1), 0, 0)),
+            whole,
+            whole,
+            pl.BlockSpec((8, HEAD), lambda p: (0, 0)),
+            source,
+            source,
+        ],
+        out_specs=pl.BlockSpec(
+            (GROUP, COMPACT, 2 * HEAD), lambda p: (jnp.maximum(p - FILLS, 0), 0, 0)
+        ),
+        out_shape=jax.ShapeDtypeStruct((OWNERS, COMPACT, 2 * HEAD), BF),
+        scratch_shapes=[pltpu.VMEM((OWNERS, HEADS * CELL, 2 * HEAD), BF)],
+        compiler_params=params("arbitrary", vmem=60 * 1024 * 1024),
+        cost_estimate=pl.CostEstimate(
+            flops=4 * 2**30, bytes_accessed=8 * 2**20, transcendentals=0
+        ),
+        name="compact",
+    )(slots.reshape(FILLS, share, TOK), row_of, held, flag, one, two)
+
+
+def spread_kernel(mark, got_ref, note_ref, out_ref):
+    slots = HEADS * CELL
+    row = lax.broadcasted_iota(jnp.int32, (slots, slots), 0)
+    col = lax.broadcasted_iota(jnp.int32, (slots, slots), 1)
+    held = note_ref[...].astype(F32)[:, 0, :HEAD].astype(BF)
+    rank = dot(jnp.where(col < row, 1.0, 0.0).astype(BF), held, NT)
+    is_held = dot(jnp.where(col == row, 1.0, 0.0).astype(BF), held, NT) > 0.5
+    target = jnp.where(is_held, rank + 1.0, -2.0 * COMPACT).astype(jnp.int32)
+    place = lax.broadcasted_iota(jnp.int32, (2 * slots, 2 * COMPACT), 1)
+    for s in range(0, GROUP, 2):
+        goal = jnp.concatenate([target[:, s : s + 1], target[:, s + 1 : s + 2] + COMPACT], axis=0)
+        hot = jnp.where(place == goal, 1.0, 0.0).astype(BF)
+        rows = dot(hot, got_ref[s : s + 2].reshape(2 * COMPACT, 2 * HEAD), NN)
+        if mark:
+            rows = jnp.concatenate(
+                [jnp.where(goal > 0, rows[:, :HEAD], EMPTY), rows[:, HEAD:]], axis=1
+            )
+        out_ref[s : s + 2] = rows.reshape(2, slots, 2 * HEAD).astype(BF)
+
+
+def spread(got, notes, mark):
+    return pl.pallas_call(
+        functools.partial(spread_kernel, mark),
+        grid=(OWNERS // GROUP,),
+        in_specs=[
+            pl.BlockSpec((GROUP, COMPACT, 2 * HEAD), lambda p: (p, 0, 0)),
+            pl.BlockSpec((GROUP, 2 * CELL, 2 * HEAD), lambda p: (p, 0, 0)),
+        ],
+        out_specs=pl.BlockSpec((GROUP, HEADS * CELL, 2 * HEAD), lambda p: (p, 0, 0)),
+        out_shape=jax.ShapeDtypeStruct((OWNERS, HEADS * CELL, 2 * HEAD), BF),
+        compiler_params=params("arbitrary"),
+        cost_estimate=pl.CostEstimate(
+            flops=2 * 2**30, bytes_accessed=8 * 2**20, transcendentals=0
+        ),
+        name="spread",
+    )(got, notes)
 
 
 def pack_kernel(mark, slot_ref, *refs):
@@ -88,7 +220,7 @@
     )(slots.reshape(HEADS // 2, 2, TOK), *sources)
 
 
-def attention_kernel(in_ref, out_ref, bias_ref):
+def attention_kernel(kv_ref, gq_ref, out_ref, bias_ref):
     scale = 1.0 / math.sqrt(HEAD)
     to_exp2 = scale * math.log2(math.e)
 
@@ -100,11 +232,14 @@
         bias_ref[...] = jnp.where(keep, 0.0, -1e30)
 
     first = jnp.where(lax.broadcasted_iota(jnp.int32, (8, HEAD), 1) == 0, 1.0, 0.0).astype(BF)
-    pair = in_ref[...].astype(F32)
+    pairs = [ref[...].astype(F32) for ref in (kv_ref, gq_ref)]
     step = 256
     for e in range(2):
-        rows = pair[:, e * CELL : (e + 1) * CELL, :].reshape(SLOTS, 4 * HEAD).astype(BF)
-        k, v, g, q = (rows[:, n * HEAD : (n + 1) * HEAD] for n in range(4))
+        kv, gq = (
+            pair[:, e * CELL : (e + 1) * CELL, :].reshape(SLOTS, 2 * HEAD).astype(BF)
+            for pair in pairs
+        )
+        k, v, g, q = kv[:, :HEAD], kv[:, HEAD:], gq[:, :HEAD], gq[:, HEAD:]
         key_bias = jnp.where(dot(first, k, NT)[0:1, :] > 0.5 * EMPTY, -1e30, 0.0)
         for i in range(SLOTS // step):
             here = slice(i * step, (i + 1) * step)
@@ -122,11 +257,14 @@
             out_ref[0, i * tiles : (i + 1) * tiles, e] = dquery.reshape(tiles, 2 * CELL, HEAD)
 
 
-def attention(got):
+def attention(kv, gq, first):
     return pl.pallas_call(
         attention_kernel,
         grid=(HPC // 2,),
-        in_specs=[pl.BlockSpec((OWNERS, 2 * CELL, 4 * HEAD), lambda p: (0, p, 0))],
+        in_specs=[
+            pl.BlockSpec((OWNERS, 2 * CELL, 2 * HEAD), lambda p: (0, first + p, 0)),
+            pl.BlockSpec((OWNERS, 2 * CELL, 2 * HEAD), lambda p: (0, first + p, 0)),
+        ],
         out_specs=pl.BlockSpec((1, OWNERS // 2, 2, 2 * CELL, HEAD), lambda p: (p, 0, 0, 0, 0)),
         out_shape=jax.ShapeDtypeStruct((HPC // 2, OWNERS // 2, 2, 2 * CELL, HEAD), BF),
         scratch_shapes=[pltpu.VMEM((SLOTS, SLOTS), F32)],
@@ -137,7 +275,7 @@
             transcendentals=HPC * SLOTS * SLOTS,
         ),
         name="attention",
-    )(got)
+    )(kv, gq)
 
 
 def grad_kernel(where_ref, rows_ref, act_a, act_b, *refs):
@@ -177,7 +315,7 @@
 
 def weight_grad(where, rows, acts, features, seqs, earlier):
     def act_spec():
-        return pl.BlockSpec((1, features + 2 * HEADS, TOK), lambda b, w: (b, 0, 0))
+        return pl.BlockSpec((1, features + CARRIED, TOK), lambda b, w: (b, 0, 0))
 
     in_specs = [
         pl.BlockSpec((OWNERS, 2 * CELL, HEAD), lambda b, w: (b, 0, 0)),
@@ -218,37 +356,49 @@
     features = tokens_here.shape[1]
     seqs = lax.axis_size("dp")
     devices = seqs * OWNERS
-    slots = slots_of(cluster[0])
+    slots, held, row_of, over = slots_of(cluster[0])
     seq_send = functools.partial(
         lax.all_to_all, axis_name="seq", split_axis=0, concat_axis=0, tiled=True
     )
     all_send = functools.partial(
         lax.all_to_all, axis_name=("dp", "seq"), split_axis=0, concat_axis=0, tiled=True
     )
+    keys, vals, grads = all_keys[0], values[0], grad_out[0]
+
+    core = lax.axis_index("seq") % 2
+    group = lax.axis_index("dp") * 2 + core
+    flag = over
+    for shift in range(1, seqs):
+        ring = [(i, (i + shift) % seqs) for i in range(seqs)]
+        flag = jnp.maximum(flag, lax.ppermute(over, "dp", ring))
+
+    got_kv = seq_send(compact(slots, row_of, held, jnp.zeros((8, HEAD), F32), keys, vals))
     queries = jnp.dot(tokens_here, w_query, preferred_element_type=F32).astype(BF)
-    sent = [
-        pack(slots, c, True, all_keys[0], values[0], grad_out[0], queries) for c in range(CHUNKS)
-    ]
-
-    swap = [(i, i ^ 1) for i in range(OWNERS)]
+    send_gq = compact(slots, row_of, held, flag, grads, queries)
     carried = jnp.concatenate(
         [tokens_here.T, (slots // CELL).astype(BF), (slots % CELL).astype(BF)], axis=0
     )
+    send_gq, got_kv, carried = lax.optimization_barrier((send_gq, got_kv, carried))
+    got_gq = seq_send(send_gq)
+
     acts_mine = lax.all_gather(carried, "dp")
-    acts = (acts_mine, lax.ppermute(acts_mine, "seq", swap))
-    core = lax.axis_index("seq") % 2
-    group = lax.axis_index("dp") * 2 + core
-
-    got, last = [], None
-    for c in range(CHUNKS):
-        block = sent[c]
-        if last is not None:
-            block, got[-1] = lax.optimization_barrier((block, last))
-        last = seq_send(block)
-        got.append(last)
+    acts = (acts_mine, lax.ppermute(acts_mine, "seq", [(i, i ^ 1) for i in range(OWNERS)]))
+
+    def send_all_slots(state):
+        def whole(mark, *sources):
+            parts = [pack(slots, c, mark, *sources) for c in range(CHUNKS)]
+            return seq_send(jnp.concatenate(parts, axis=1))
+
+        return jnp.zeros_like(state[0]), whole(True, keys, vals), whole(False, grads, queries)
+
+    too_many = jnp.max(got_gq[:, 0, HEAD]).astype(F32)
+    spreads = (spread(got_kv, got_kv, True), spread(got_gq, got_kv, False))
+    _, kv, gq = lax.while_loop(
+        lambda state: state[0] > 0.5, send_all_slots, (too_many, *spreads)
+    )
     part = None
     for c in range(CHUNKS):
-        rows = attention(got[c])
+        rows = attention(kv, gq, c * HPC // 2)
         back = all_send(rows.reshape(devices, 2 * CELL, HEAD))
         where = jnp.stack([c * HPC + group, core]).astype(jnp.int32)
         part = weight_grad(where, back, acts, features, seqs, part)

time: 362 us -> 335 us (0.925)
  waiting for transfers between devices: 218 us -> 166 us
  Pallas kernels: 47 us -> 62.1 us
  starting transfers between devices: 33.4 us -> 37.3 us
    all_gather x1, waiting for transfers between devices: 53.3 us -> 0.01 us  [on_device(): acts_mine = lax.all_gather(carried, 'dp')]
    pallas_call x3 -> x5, Pallas kernels: 10.4 us -> 25.5 us  [the longest x2 13.2 us: compact(): pl.pallas_call(compact_kernel, grid=(FILLS + groups,), in_specs=[pl.Block...]
  transfers between devices with their start and end apart: 6 -> 9, of which waited for: 5 -> 4; matrix products, arithmetic and copies ran while one was open for 0% -> 4% of each run, Pallas kernels for 9% -> 14%
where the time goes in v3:
time: 335 us; the launch traced here: 334 us
  waiting for transfers between devices  166 us (50%)
  Pallas kernels  62.1 us (19%)
  starting transfers between devices  37.3 us (11%)
  blocking collectives  36.9 us (11%)
  between operations  14.2 us (4%)
  matrix products  7.07 us (2%)
  local copies, waits for them, and re-layouts  6.26 us (2%)
  other arithmetic  3.56 us (1%)
    all_to_all x1, waiting for transfers between devices, on_device(): got_gq = seq_send(send_gq)  67.8 us
    all_to_all x1, waiting for transfers between devices, on_device(): seq_send(compact(slots, row_of, held, jnp.zeros((8, HEAD), F32), keys, va...  52.1 us
    all_to_all x2, waiting for transfers between devices, on_device(): back = all_send(rows.reshape(devices, 2 * CELL, HEAD))  45.8 us
    all_to_all x1, blocking collectives, on_device(): terms = all_send(part)  36.9 us
    pallas_call x2, Pallas kernels, attention(): pl.pallas_call(attention_kernel, grid=(HPC // 2,), in_specs=[pl.BlockSpec...  22.3 us
    pallas_call x2, Pallas kernels, weight_grad(): pl.pallas_call(grad_kernel, grid_spec=pltpu.PrefetchScalarGridSpec(num_sc...  14.3 us
    all_to_all x2, starting transfers between devices, on_device(): back = all_send(rows.reshape(devices, 2 * CELL, HEAD))  13.9 us
    pallas_call x2, Pallas kernels, compact(): pl.pallas_call(compact_kernel, grid=(FILLS + groups,), in_specs=[pl.Block...  13.2 us
  transfers between devices with their start and end apart: 9, of which 4 were waited for; matrix products, arithmetic and copies ran while one was open for 4% of the time, Pallas kernels for 14%

profile of v3, /device:TPU:1, one launch (start us, length us, event | category | flops | bytes accessed | tf_op | source)
XLA Modules:
  0.0 333.7 jit_solution(5843730674583843829)
XLA Ops:
  6.5 0.8 copy.13.col_ref
  7.4 0.7 copy-done.1
  8.1 1.1 slots.1
  9.2 0.6 copy-done.2
  9.8 0.6 reshape.22.slot_ref
  10.4 0.6 broadcast_in_dim.3.flag_ref
  11.0 0.0 copy-done.3
  11.0 6.6 %compact.3 = bf16[64,96,256]{2,1,0:T(8,128)(2,1)} custom-call(s32[4,4,256]{2,1,0:T(4,128)} %reshape.22.slot_ref, f32[64,128]{1,0:T(8,128)} %copy-done.3, f32[64,128]{1,0:T(8,128)} %copy-done.2, f32[8,128]{1,0:T(8,128)} %broadcast_in_dim.3.flag_ref, bf16[256,2048]{1,0:T(8,128)(2,1)} %bitcast.33, bf16[256,2048]{1,0:T(8,128)(2,1)} %bitcast.35), custom_call_target="tpu_custom_call" | custom-call | flops 4294967296 | bytes 8388608 | tf_op jit(solution)/shard_map/compact/pallas_call | solution.py:127
  17.7 13.2 %all-to-all-start.2 = ((bf16[64,96,256]{2,1,0:T(8,128)(2,1)}), bf16[64,96,256]{2,1,0:T(8,128)(2,1)S(1)}, u32[]{:S(2)}, u32[]{:S(2)}) async-start(bf16[64,96,256]{2,1,0:T(8,128)(2,1)} %compact.3), calls=%async_computation.2 | async-start | bytes 6291456 | tf_op jit(solution)/shard_map/all_to_all | solution.py:375
  30.8 2.6 collective-permute-start.2
  33.4 0.5 collective-permute-start.1
  33.9 0.6 collective-permute-start
  34.5 2.2 copy.14
  36.8 0.0 copy-start.4
  36.8 7.1 %convolution_convert_fusion.two_ref = bf16[256,2048]{1,0:T(8,128)(2,1)} fusion(bf16[2048,2048]{1,0:T(8,128)(2,1)} %param.9, bf16[1,256,2048]{2,1,0:T(8,128)(2,1)} %param.8), kind=kOutput, calls=%fused_computation.2 | convolution fusion | flops 2148007936 | bytes 10485760 | tf_op jit(solution)/shard_map/dot_general | solution.py:376
  43.9 0.0 copy-done.4
  43.9 1.1 pad_maximum_fusion.2
  45.0 0.0 collective-permute-done.2
  45.0 0.0 collective-permute-done.1
  45.0 0.0 collective-permute-done
  45.0 0.6 maximum_maximum_fusion.flag_ref
  45.6 6.6 %compact.2 = bf16[64,96,256]{2,1,0:T(8,128)(2,1)} custom-call(s32[4,4,256]{2,1,0:T(4,128)} %reshape.22.slot_ref, f32[64,128]{1,0:T(8,128)} %copy-done.3, f32[64,128]{1,0:T(8,128)} %copy-done.2, f32[8,128]{1,0:T(8,128)} %maximum_maximum_fusion.flag_ref, bf16[256,2048]{1,0:T(8,128)(2,1)} %bitcast.31, bf16[256,2048]{1,0:T(8,128)(2,1)} %convolution_convert_fusion.two_ref), custom_call_target="tpu_custom_call" | custom-call | flops 4294967296 | bytes 8388608 | tf_op jit(solution)/shard_map/compact/pallas_call | solution.py:127
  52.2 52.1 %all-to-all-done.2.got_ref.note_ref = bf16[64,96,256]{2,1,0:T(8,128)(2,1)S(1)} async-done(((bf16[64,96,256]{2,1,0:T(8,128)(2,1)}), bf16[64,96,256]{2,1,0:T(8,128)(2,1)S(1)}, u32[]{:S(2)}, u32[]{:S(2)}) %all-to-all-start.2) | async-done | bytes 3145760 | tf_op jit(solution)/shard_map/all_to_all | solution.py:375
  104.3 6.2 %all-to-all-start.3 = ((bf16[64,96,256]{2,1,0:T(8,128)(2,1)}), bf16[64,96,256]{2,1,0:T(8,128)(2,1)}, u32[]{:S(2)}, u32[]{:S(2)}) async-start(bf16[64,96,256]{2,1,0:T(8,128)(2,1)} %compact.2), calls=%async_computation.3 | async-start | bytes 6291456 | tf_op jit(solution)/shard_map/all_to_all | solution.py:382
  110.6 0.0 all-gather.3.cloned.1.call-start
  110.6 0.7 all-gather.3.cloned.1.call-update
  111.3 4.9 %spread.2 = bf16[64,128,256]{2,1,0:T(8,128)(2,1)} custom-call(bf16[64,96,256]{2,1,0:T(8,128)(2,1)S(1)} %all-to-all-done.2.got_ref.note_ref, bf16[64,96,256]{2,1,0:T(8,128)(2,1)S(1)} %all-to-all-done.2.got_ref.note_ref), custom_call_target="tpu_custom_call" | custom-call | flops 2147483648 | bytes 8388608 | tf_op jit(solution)/shard_map/spread/pallas_call | solution.py:172
  116.3 0.0 copy-done
  116.3 67.8 %all-to-all-done.3.got_ref = bf16[64,96,256]{2,1,0:T(8,128)(2,1)} async-done(((bf16[64,96,256]{2,1,0:T(8,128)(2,1)}), bf16[64,96,256]{2,1,0:T(8,128)(2,1)}, u32[]{:S(2)}, u32[]{:S(2)}) %all-to-all-start.3) | async-done | bytes 3145760 | tf_op jit(solution)/shard_map/all_to_all | solution.py:382
  184.0 1.6 slice_reduce_fusion
  186.3 0.0 copy-start.5
  186.3 0.0 copy-start.6
  186.3 6.3 %spread.3 = bf16[64,128,256]{2,1,0:T(8,128)(2,1)} custom-call(bf16[64,96,256]{2,1,0:T(8,128)(2,1)} %all-to-all-done.3.got_ref, bf16[64,96,256]{2,1,0:T(8,128)(2,1)} %copy-done), custom_call_target="tpu_custom_call" | custom-call | flops 2147483648 | bytes 8388608 | tf_op jit(solution)/shard_map/spread/pallas_call | solution.py:172
  192.5 0.3 collective-permute-start.3
  192.8 0.0 copy-done.5
  192.8 11.1 %attention.3 = bf16[4,32,2,16,128]{4,3,2,1,0:T(8,128)(2,1)} custom-call(bf16[64,128,256]{2,1,0:T(8,128)(2,1)} %get-tuple-element.58.kv_ref, bf16[64,128,256]{2,1,0:T(8,128)(2,1)} %get-tuple-element.59.gq_ref), custom_call_target="tpu_custom_call" | custom-call | flops 2147483648 | bytes 5242880 | tf_op jit(solution)/shard_map/attention/pallas_call | solution.py:261
  203.9 8.5 %all-to-all-start.5 = ((bf16[256,16,128]{2,1,0:T(8,128)(2,1)}), bf16[256,16,128]{2,1,0:T(8,128)(2,1)S(1)}, u32[]{:S(2)}, u32[]{:S(2)}) async-start(bf16[256,16,128]{2,1,0:T(8,128)(2,1)} %bitcast.12), calls=%async_computation.5 | async-start | bytes 2097152 | tf_op jit(solution)/shard_map/all_to_all | solution.py:402
  212.5 11.1 %attention.2 = bf16[4,32,2,16,128]{4,3,2,1,0:T(8,128)(2,1)} custom-call(bf16[64,128,256]{2,1,0:T(8,128)(2,1)} %get-tuple-element.58.kv_ref, bf16[64,128,256]{2,1,0:T(8,128)(2,1)} %get-tuple-element.59.gq_ref), custom_call_target="tpu_custom_call" | custom-call | flops 2147483648 | bytes 5242880 | tf_op jit(solution)/shard_map/attention/pallas_call | solution.py:261
  223.6 21.4 %all-to-all-done.5.rows_ref = bf16[256,16,128]{2,1,0:T(8,128)(2,1)S(1)} async-done(((bf16[256,16,128]{2,1,0:T(8,128)(2,1)}), bf16[256,16,128]{2,1,0:T(8,128)(2,1)S(1)}, u32[]{:S(2)}, u32[]{:S(2)}) %all-to-all-start.5) | async-done | bytes 1048608 | tf_op jit(solution)/shard_map/all_to_all | solution.py:402
  245.0 5.4 %all-to-all-start.4 = ((bf16[256,16,128]{2,1,0:T(8,128)(2,1)}), bf16[256,16,128]{2,1,0:T(8,128)(2,1)S(1)}, u32[]{:S(2)}, u32[]{:S(2)}) async-start(bf16[256,16,128]{2,1,0:T(8,128)(2,1)} %bitcast.9), calls=%async_computation.4 | async-start | bytes 2097152 | tf_op jit(solution)/shard_map/all_to_all | solution.py:402
  250.4 0.1 pad_add_fusion
  250.4 0.0 collective-permute-done.3.act_b
  250.4 7.1 %weight_grad.2.refs_0_ = f32[2048,128]{1,0:T(8,128)S(1)} custom-call(s32[2]{0:T(128)S(1)} %get-tuple-element.80.where_ref, bf16[256,16,128]{2,1,0:T(8,128)(2,1)S(1)} %all-to-all-done.5.rows_ref, bf16[4,2080,256]{2,1,0:T(8,128)(2,1)} %bitcast.26, bf16[4,2080,256]{2,1,0:T(8,128)(2,1)} %collective-permute-done.3.act_b), custom_call_target="tpu_custom_call" | custom-call | flops 2147483648 | bytes 12582912 | tf_op jit(solution)/shard_map/weight_grad/pallas_call | solution.py:334
  257.6 24.5 %all-to-all-done.4.rows_ref = bf16[256,16,128]{2,1,0:T(8,128)(2,1)S(1)} async-done(((bf16[256,16,128]{2,1,0:T(8,128)(2,1)}), bf16[256,16,128]{2,1,0:T(8,128)(2,1)S(1)}, u32[]{:S(2)}, u32[]{:S(2)}) %all-to-all-start.4) | async-done | bytes 1048608 | tf_op jit(solution)/shard_map/all_to_all | solution.py:402
  282.0 7.2 %weight_grad.3 = bf16[256,16,128]{2,1,0:T(8,128)(2,1)S(1)} custom-call(s32[2]{0:T(128)S(1)} %get-tuple-element.79.where_ref, bf16[256,16,128]{2,1,0:T(8,128)(2,1)S(1)} %all-to-all-done.4.rows_ref, bf16[4,2080,256]{2,1,0:T(8,128)(2,1)} %bitcast.27, bf16[4,2080,256]{2,1,0:T(8,128)(2,1)} %collective-permute-done.3.act_b, f32[2048,128]{1,0:T(8,128)S(1)} %weight_grad.2.refs_0_), custom_call_target="tpu_custom_call" | custom-call | flops 2147483648 | bytes 12582912 | tf_op jit(solution)/shard_map/weight_grad/pallas_call | solution.py:334
  289.2 36.9 %all_to_all.33 = bf16[256,16,128]{2,1,0:T(8,128)(2,1)S(1)} all-to-all(bf16[256,16,128]{2,1,0:T(8,128)(2,1)S(1)} %weight_grad.3), channel_id=1, replica_groups=mesh['dp'=4,'seq'=64] {'dp','seq'}, dimensions={0} | all-to-all | bytes 2097152 | tf_op jit(solution)/shard_map/all_to_all | solution.py:405
  326.1 0.1 convert_reduce_fusion
  326.3 0.6 copy.15
  (8 shorter events, 0.0 us)
Async XLA Ops:
  7.4 0.7 copy-start.1
  9.2 0.6 copy-start.2
  9.8 1.2 copy-start.3
  17.7 86.7 %all-to-all-start.2 = ((bf16[64,96,256]{2,1,0:T(8,128)(2,1)}), bf16[64,96,256]{2,1,0:T(8,128)(2,1)S(1)}, u32[]{:S(2)}, u32[]{:S(2)}) async-start(bf16[64,96,256]{2,1,0:T(8,128)(2,1)} %compact.3), calls=%async_computation.2 | async-start | bytes 6291456 | tf_op jit(solution)/shard_map/all_to_all | solution.py:375
  30.8 14.2 %collective-permute-start.2 = (f32[8,128]{1,0:T(8,128)S(1)}, f32[8,128]{1,0:T(8,128)S(1)}, u32[]{:S(2)}, u32[]{:S(2)}) collective-permute-start(f32[8,128]{1,0:T(8,128)S(1)} %get-tuple-element.55), channel_id=1, source_target_pairs={{0,192},{64,0},{128,64},{192,128},{1,193},{65,1},{129,65},{193,129... | collective-permute-start | bytes 12296 | tf_op jit(solution)/shard_map/ppermute | solution.py:373
  33.4 11.6 %collective-permute-start.1 = (f32[8,128]{1,0:T(8,128)S(1)}, f32[8,128]{1,0:T(8,128)S(1)}, u32[]{:S(2)}, u32[]{:S(2)}) collective-permute-start(f32[8,128]{1,0:T(8,128)S(1)} %get-tuple-element.55), channel_id=1, source_target_pairs={{0,128},{64,192},{128,0},{192,64},{1,129},{65,193},{129,1},{193,65... | collective-permute-start | bytes 12296 | tf_op jit(solution)/shard_map/ppermute | solution.py:373
  33.9 11.1 %collective-permute-start = (f32[8,128]{1,0:T(8,128)S(1)}, f32[8,128]{1,0:T(8,128)S(1)}, u32[]{:S(2)}, u32[]{:S(2)}) collective-permute-start(f32[8,128]{1,0:T(8,128)S(1)} %get-tuple-element.55), channel_id=1, source_target_pairs={{0,64},{64,128},{128,192},{192,0},{1,65},{65,129},{129,193},{193,1... | collective-permute-start | bytes 12296 | tf_op jit(solution)/shard_map/ppermute | solution.py:373
  36.8 7.1 %copy-start.4 = (bf16[1,256,2048]{1,2,0:T(8,128)(2,1)S(1)}, bf16[1,256,2048]{1,2,0:T(8,128)(2,1)}, u32[]{:S(2)}) copy-start(bf16[1,256,2048]{1,2,0:T(8,128)(2,1)} %copy.14) | copy-start | bytes 3145732
  104.3 11.9 %copy-start = (bf16[64,96,256]{2,1,0:T(8,128)(2,1)}, bf16[64,96,256]{2,1,0:T(8,128)(2,1)S(1)}, u32[]{:S(2)}) copy-start(bf16[64,96,256]{2,1,0:T(8,128)(2,1)S(1)} %all-to-all-done.2.got_ref.note_ref) | copy-start | bytes 9437188
  104.3 79.7 %all-to-all-start.3 = ((bf16[64,96,256]{2,1,0:T(8,128)(2,1)}), bf16[64,96,256]{2,1,0:T(8,128)(2,1)}, u32[]{:S(2)}, u32[]{:S(2)}) async-start(bf16[64,96,256]{2,1,0:T(8,128)(2,1)} %compact.2), calls=%async_computation.3 | async-start | bytes 6291456 | tf_op jit(solution)/shard_map/all_to_all | solution.py:382
  110.6 82.0 %all-gather.3.cloned.1.call-start = ((), (), s32[]{:S(2)}) async-start(), calls=%async_computation.7 | async-start | bytes 5324800 | tf_op jit(solution)/shard_map/all_gather | solution.py:384
  186.3 6.5 %copy-start.5 = (bf16[1,256,2048]{2,1,0:T(8,128)(2,1)S(1)}, bf16[1,256,2048]{2,1,0:T(8,128)(2,1)}, u32[]{:S(2)}) copy-start(bf16[1,256,2048]{2,1,0:T(8,128)(2,1)} %param.12) | copy-start | bytes 3145732
  186.3 6.5 %copy-start.6 = (bf16[1,256,2048]{2,1,0:T(8,128)(2,1)S(1)}, bf16[1,256,2048]{2,1,0:T(8,128)(2,1)}, u32[]{:S(2)}) copy-start(bf16[1,256,2048]{2,1,0:T(8,128)(2,1)} %param.10) | copy-start | bytes 3145732
  192.5 57.9 %collective-permute-start.3 = (bf16[4,2080,256]{2,1,0:T(8,128)(2,1)}, bf16[4,2080,256]{2,1,0:T(8,128)(2,1)}, u32[]{:S(2)}, u32[]{:S(2)}) collective-permute-start(bf16[4,2080,256]{2,1,0:T(8,128)(2,1)} %bitcast.25), channel_id=1, source_target_pairs={{0,1},{1,0},{2,3},{3,2},{4,5},{5,4},{6,7},{7,6},{8,9},{9,8},{10,11... | collective-permute-start | bytes 12779528 | tf_op jit(solution)/shard_map/ppermute | solution.py:385
  203.9 41.0 %all-to-all-start.5 = ((bf16[256,16,128]{2,1,0:T(8,128)(2,1)}), bf16[256,16,128]{2,1,0:T(8,128)(2,1)S(1)}, u32[]{:S(2)}, u32[]{:S(2)}) async-start(bf16[256,16,128]{2,1,0:T(8,128)(2,1)} %bitcast.12), calls=%async_computation.5 | async-start | bytes 2097152 | tf_op jit(solution)/shard_map/all_to_all | solution.py:402
  245.0 37.1 %all-to-all-start.4 = ((bf16[256,16,128]{2,1,0:T(8,128)(2,1)}), bf16[256,16,128]{2,1,0:T(8,128)(2,1)S(1)}, u32[]{:S(2)}, u32[]{:S(2)}) async-start(bf16[256,16,128]{2,1,0:T(8,128)(2,1)} %bitcast.9), calls=%async_computation.4 | async-start | bytes 2097152 | tf_op jit(solution)/shard_map/all_to_all | solution.py:402
Sparse Core Ops, SparseCore 0:
  113.2 52.2 all-gather.2

commit v4 on v3

--- a/solution.py
+++ b/solution.py
@@ -16,6 +16,7 @@
 HEADS = 16
 CARRIED = 2 * HEADS
 CHUNKS = 2
+YS, ZS = 4, 8
 HPC = HEADS // CHUNKS
 COMPACT = 96
 GROUP = 16
@@ -278,8 +279,7 @@
     )(kv, gq)
 
 
-def grad_kernel(where_ref, rows_ref, act_a, act_b, *refs):
-    earlier_ref, out_ref, acc_ref = refs if len(refs) == 3 else (None, *refs)
+def grad_kernel(where_ref, rows_ref, act_a, act_b, out_ref, acc_ref):
     b = pl.program_id(0)
     head, core = where_ref[0], where_ref[1]
     features = acc_ref.shape[0]
@@ -306,49 +306,41 @@
 
     @pl.when(b == pl.num_programs(0) - 1)
     def _():
-        if earlier_ref is None:
-            out_ref[...] = acc_ref[...]
-        else:
-            both = [ref[...].reshape(-1, CELL, HEAD) for ref in (earlier_ref, acc_ref)]
-            out_ref[...] = jnp.concatenate(both, axis=1).astype(BF)
-
-
-def weight_grad(where, rows, acts, features, seqs, earlier):
+        ys, zs, seqs, pair = out_ref.shape[:4]
+        for y in range(ys):
+            for z in range(zs):
+                for d in range(seqs):
+                    at = ((d * ys + y) * zs + z) * pair
+                    out_ref[y, z, d] = acc_ref[at : at + pair, :].astype(BF)
+
+
+def weight_grad(where, rows, acts, features, seqs):
     def act_spec():
         return pl.BlockSpec((1, features + CARRIED, TOK), lambda b, w: (b, 0, 0))
 
-    in_specs = [
-        pl.BlockSpec((OWNERS, 2 * CELL, HEAD), lambda b, w: (b, 0, 0)),
-        act_spec(),
-        act_spec(),
-    ]
-    if earlier is None:
-        out = jax.ShapeDtypeStruct((features, HEAD), F32)
-        out_spec = pl.BlockSpec((features, HEAD), lambda b, w: (0, 0))
-        more = ()
-    else:
-        out = jax.ShapeDtypeStruct((features // CELL, 2 * CELL, HEAD), BF)
-        out_spec = pl.BlockSpec((features // CELL, 2 * CELL, HEAD), lambda b, w: (0, 0, 0))
-        in_specs.append(pl.BlockSpec((features, HEAD), lambda b, w: (0, 0)))
-        more = (earlier,)
+    out = (YS, ZS, seqs, features // (YS * ZS * seqs), HEAD)
     return pl.pallas_call(
         grad_kernel,
         grid_spec=pltpu.PrefetchScalarGridSpec(
             num_scalar_prefetch=1,
             grid=(seqs,),
-            in_specs=in_specs,
-            out_specs=out_spec,
+            in_specs=[
+                pl.BlockSpec((OWNERS, 2 * CELL, HEAD), lambda b, w: (b, 0, 0)),
+                act_spec(),
+                act_spec(),
+            ],
+            out_specs=pl.BlockSpec(out, lambda b, w: (0, 0, 0, 0, 0)),
             scratch_shapes=[pltpu.VMEM((features, HEAD), F32)],
         ),
-        out_shape=out,
-        compiler_params=params("arbitrary"),
+        out_shape=jax.ShapeDtypeStruct(out, BF),
+        compiler_params=params("arbitrary", vmem=60 * 1024 * 1024),
         cost_estimate=pl.CostEstimate(
             flops=4 * seqs * TOK * features * HEAD * 2,
             bytes_accessed=12 * 2**20,
             transcendentals=0,
         ),
         name="weight_grad",
-    )(where, rows, *acts, *more)
+    )(where, rows, *acts)
 
 
 def on_device(activations, w_query, all_keys, values, grad_out, cluster):
@@ -396,17 +388,42 @@
     _, kv, gq = lax.while_loop(
         lambda state: state[0] > 0.5, send_all_slots, (too_many, *spreads)
     )
-    part = None
-    for c in range(CHUNKS):
-        rows = attention(kv, gq, c * HPC // 2)
-        back = all_send(rows.reshape(devices, 2 * CELL, HEAD))
-        where = jnp.stack([c * HPC + group, core]).astype(jnp.int32)
-        part = weight_grad(where, back, acts, features, seqs, part)
-    terms = all_send(part)
-    terms = terms.reshape(seqs, OWNERS // 2, 2, CHUNKS, features // devices, HEAD)
-    out = jnp.sum(terms.astype(F32), axis=1)
-    out = out.transpose(3, 2, 0, 1, 4)
-    return out.reshape(features // devices, HEADS * HEAD)
+    rows = [attention(kv, gq, c * HPC // 2).reshape(devices, 2 * CELL, HEAD) for c in range(CHUNKS)]
+    back = all_send(rows[0])
+    rows[1], back = lax.optimization_barrier((rows[1], back))
+    back_next = all_send(rows[1])
+    wheres = [jnp.stack([c * HPC + group, core]).astype(jnp.int32) for c in range(CHUNKS)]
+
+    def place(y, z, side):
+        return (y * ZS + z) * 2 + side
+
+    part = weight_grad(wheres[0], back, acts, features, seqs)
+    my_y = lax.axis_index("seq") // (2 * ZS)
+    first = lax.dynamic_index_in_dim(part, my_y, 0, False).astype(F32)
+    for shift in range(1, YS):
+        ring = [
+            (place(y, z, side), place((y + shift) % YS, z, side))
+            for y in range(YS)
+            for z in range(ZS)
+            for side in range(2)
+        ]
+        block = lax.dynamic_index_in_dim(part, (my_y + shift) % YS, 0, False)
+        first = first + lax.ppermute(block, "seq", ring).astype(F32)
+    back_next, first = lax.optimization_barrier((back_next, first))
+    part = weight_grad(wheres[1], back_next, acts, features, seqs)
+    along_y = [[place(y, z, side) for y in range(YS)] for z in range(ZS) for side in range(2)]
+    second = jnp.sum(seq_send(part, axis_index_groups=along_y).astype(F32), axis=0)
+    along_z = [[place(y, z, side) for z in range(ZS)] for y in range(YS) for side in range(2)]
+    both = jnp.concatenate([first, second], axis=2).astype(BF)
+    both = jnp.sum(seq_send(both, axis_index_groups=along_z).astype(F32), axis=0)
+    both = both.reshape(seqs, CHUNKS, 2, features // devices, HEAD).transpose(0, 2, 1, 3, 4)
+    both = both.reshape(2 * seqs, CHUNKS, features // devices, HEAD)
+    around = [
+        [d * OWNERS + p * 2 + side for d in range(seqs) for side in range(2)]
+        for p in range(OWNERS // 2)
+    ]
+    out = all_send(both, axis_index_groups=around)
+    return out.transpose(2, 1, 0, 3).reshape(features // devices, HEADS * HEAD)
 
 
 def solution(mesh):

time: 335 us -> 335 us (level)
  waiting for transfers between devices: 166 us -> 157 us
  starting transfers between devices: 37.3 us -> 42.7 us
    all_to_all x2, waiting for transfers between devices: 45.8 us -> 28.4 us  [the longest x1 21.4 us: on_device(): back = all_send(rows[0])]
    ppermute x0 -> x3, waiting for transfers between devices: none -> 9.49 us  [on_device(): first = first + lax.ppermute(block, 'seq', ring).astype(F32)]
    ppermute x0 -> x3, starting transfers between devices: none -> 4.23 us  [on_device(): first = first + lax.ppermute(block, 'seq', ring).astype(F32)]
    all_to_all x1 -> x3, blocking collectives: 36.9 us -> 35 us  [the longest x1 12.6 us: on_device(): seq_send(both, axis_index_groups=along_z).astype(F32)]
  transfers between devices with their start and end apart: 9 -> 12, of which waited for: 4 -> 6; matrix products, arithmetic and copies ran while one was open for 4% -> 5% of each run, Pallas kernels for 14% -> 14%
where the time goes in v4:
time: 335 us; the launch traced here: 334 us
  waiting for transfers between devices  157 us (47%)
  Pallas kernels  64.2 us (19%)
  starting transfers between devices  42.7 us (13%)
  blocking collectives  35 us (10%)
  between operations  14.3 us (4%)
  local copies, waits for them, and re-layouts  8.41 us (3%)
  matrix products  7.13 us (2%)
  other arithmetic  5.04 us (2%)
    all_to_all x1, waiting for transfers between devices, on_device(): got_gq = seq_send(send_gq)  67.8 us
    all_to_all x1, waiting for transfers between devices, on_device(): seq_send(compact(slots, row_of, held, jnp.zeros((8, HEAD), F32), keys, va...  50.8 us
    pallas_call x2, Pallas kernels, attention(): pl.pallas_call(attention_kernel, grid=(HPC // 2,), in_specs=[pl.BlockSpec...  22.2 us
    all_to_all x1, waiting for transfers between devices, on_device(): back = all_send(rows[0])  21.4 us
    pallas_call x2, Pallas kernels, weight_grad(): pl.pallas_call(grad_kernel, grid_spec=pltpu.PrefetchScalarGridSpec(num_sc...  16.4 us
    pallas_call x2, Pallas kernels, compact(): pl.pallas_call(compact_kernel, grid=(FILLS + groups,), in_specs=[pl.Block...  13.3 us
    all_to_all x1, starting transfers between devices, on_device(): seq_send(compact(slots, row_of, held, jnp.zeros((8, HEAD), F32), keys, va...  13.2 us
    all_to_all x1, blocking collectives, on_device(): seq_send(both, axis_index_groups=along_z).astype(F32)  12.6 us
  transfers between devices with their start and end apart: 12, of which 6 were waited for; matrix products, arithmetic and copies ran while one was open for 5% of the time, Pallas kernels for 14%

profile of v4, /device:TPU:1, one launch (start us, length us, event | category | flops | bytes accessed | tf_op | source)
XLA Modules:
  0.0 334.0 jit_solution(3253711961532580772)
XLA Ops:
  6.5 0.8 copy.26.col_ref
  7.4 0.7 copy-done.1
  8.1 1.1 slots.1
  9.2 0.6 copy-done.2
  9.8 0.6 reshape.27.slot_ref
  10.4 0.6 broadcast_in_dim.3.flag_ref
  11.0 6.7 %compact.3 = bf16[64,96,256]{2,1,0:T(8,128)(2,1)} custom-call(s32[4,4,256]{2,1,0:T(4,128)} %reshape.27.slot_ref, f32[64,128]{1,0:T(8,128)} %copy-done.3, f32[64,128]{1,0:T(8,128)} %copy-done.2, f32[8,128]{1,0:T(8,128)} %broadcast_in_dim.3.flag_ref, bf16[256,2048]{1,0:T(8,128)(2,1)} %bitcast.52, bf16[256,2048]{1,0:T(8,128)(2,1)} %bitcast.54), custom_call_target="tpu_custom_call" | custom-call | flops 4294967296 | bytes 8388608 | tf_op jit(solution)/shard_map/compact/pallas_call | solution.py:128
  17.7 13.2 %all-to-all-start.2 = ((bf16[64,96,256]{2,1,0:T(8,128)(2,1)}), bf16[64,96,256]{2,1,0:T(8,128)(2,1)S(1)}, u32[]{:S(2)}, u32[]{:S(2)}) async-start(bf16[64,96,256]{2,1,0:T(8,128)(2,1)} %compact.3), calls=%async_computation.2 | async-start | bytes 6291456 | tf_op jit(solution)/shard_map/all_to_all | solution.py:367
  30.9 1.3 collective-permute-start
  32.1 2.5 collective-permute-start.1
  34.6 1.1 collective-permute-start.2
  35.8 2.3 copy.27
  38.1 7.1 %convolution_convert_fusion.two_ref = bf16[256,2048]{1,0:T(8,128)(2,1)} fusion(bf16[2048,2048]{1,0:T(8,128)(2,1)} %param.9, bf16[1,256,2048]{2,1,0:T(8,128)(2,1)} %param.8), kind=kOutput, calls=%fused_computation.2 | convolution fusion | flops 2148007936 | bytes 10485760 | tf_op jit(solution)/shard_map/dot_general | solution.py:368
  45.2 1.1 pad_maximum_fusion.2
  46.3 0.6 maximum_maximum_fusion.flag_ref
  46.9 6.6 %compact.2 = bf16[64,96,256]{2,1,0:T(8,128)(2,1)} custom-call(s32[4,4,256]{2,1,0:T(4,128)} %reshape.27.slot_ref, f32[64,128]{1,0:T(8,128)} %copy-done.3, f32[64,128]{1,0:T(8,128)} %copy-done.2, f32[8,128]{1,0:T(8,128)} %maximum_maximum_fusion.flag_ref, bf16[256,2048]{1,0:T(8,128)(2,1)} %bitcast.50, bf16[256,2048]{1,0:T(8,128)(2,1)} %convolution_convert_fusion.two_ref), custom_call_target="tpu_custom_call" | custom-call | flops 4294967296 | bytes 8388608 | tf_op jit(solution)/shard_map/compact/pallas_call | solution.py:128
  53.5 50.8 %all-to-all-done.2.got_ref.note_ref = bf16[64,96,256]{2,1,0:T(8,128)(2,1)S(1)} async-done(((bf16[64,96,256]{2,1,0:T(8,128)(2,1)}), bf16[64,96,256]{2,1,0:T(8,128)(2,1)S(1)}, u32[]{:S(2)}, u32[]{:S(2)}) %all-to-all-start.2) | async-done | bytes 3145760 | tf_op jit(solution)/shard_map/all_to_all | solution.py:367
  104.4 6.2 %all-to-all-start.3 = ((bf16[64,96,256]{2,1,0:T(8,128)(2,1)}), bf16[64,96,256]{2,1,0:T(8,128)(2,1)}, u32[]{:S(2)}, u32[]{:S(2)}) async-start(bf16[64,96,256]{2,1,0:T(8,128)(2,1)} %compact.2), calls=%async_computation.3 | async-start | bytes 6291456 | tf_op jit(solution)/shard_map/all_to_all | solution.py:374
  110.6 0.0 all-gather.3.cloned.1.call-start
  110.7 0.7 all-gather.3.cloned.1.call-update
  111.4 4.9 %spread.2 = bf16[64,128,256]{2,1,0:T(8,128)(2,1)} custom-call(bf16[64,96,256]{2,1,0:T(8,128)(2,1)S(1)} %all-to-all-done.2.got_ref.note_ref, bf16[64,96,256]{2,1,0:T(8,128)(2,1)S(1)} %all-to-all-done.2.got_ref.note_ref), custom_call_target="tpu_custom_call" | custom-call | flops 2147483648 | bytes 8388608 | tf_op jit(solution)/shard_map/spread/pallas_call | solution.py:173
  116.2 67.8 %all-to-all-done.3.got_ref = bf16[64,96,256]{2,1,0:T(8,128)(2,1)} async-done(((bf16[64,96,256]{2,1,0:T(8,128)(2,1)}), bf16[64,96,256]{2,1,0:T(8,128)(2,1)}, u32[]{:S(2)}, u32[]{:S(2)}) %all-to-all-start.3) | async-done | bytes 3145760 | tf_op jit(solution)/shard_map/all_to_all | solution.py:374
  184.1 1.6 slice_reduce_fusion
  186.3 0.0 copy-start.7
  186.3 6.3 %spread.3 = bf16[64,128,256]{2,1,0:T(8,128)(2,1)} custom-call(bf16[64,96,256]{2,1,0:T(8,128)(2,1)} %all-to-all-done.3.got_ref, bf16[64,96,256]{2,1,0:T(8,128)(2,1)} %copy-done), custom_call_target="tpu_custom_call" | custom-call | flops 2147483648 | bytes 8388608 | tf_op jit(solution)/shard_map/spread/pallas_call | solution.py:173
  192.6 0.3 collective-permute-start.3
  192.8 11.1 %attention.3 = bf16[4,32,2,16,128]{4,3,2,1,0:T(8,128)(2,1)} custom-call(bf16[64,128,256]{2,1,0:T(8,128)(2,1)} %get-tuple-element.62.kv_ref, bf16[64,128,256]{2,1,0:T(8,128)(2,1)} %get-tuple-element.63.gq_ref), custom_call_target="tpu_custom_call" | custom-call | flops 2147483648 | bytes 5242880 | tf_op jit(solution)/shard_map/attention/pallas_call | solution.py:262
  203.9 8.5 %all-to-all-start.4 = ((bf16[256,16,128]{2,1,0:T(8,128)(2,1)}), bf16[256,16,128]{2,1,0:T(8,128)(2,1)S(1)}, u32[]{:S(2)}, u32[]{:S(2)}) async-start(bf16[256,16,128]{2,1,0:T(8,128)(2,1)} %bitcast.8), calls=%async_computation.4 | async-start | bytes 2097152 | tf_op jit(solution)/shard_map/all_to_all | solution.py:392
  212.5 11.1 %attention.2 = bf16[4,32,2,16,128]{4,3,2,1,0:T(8,128)(2,1)} custom-call(bf16[64,128,256]{2,1,0:T(8,128)(2,1)} %get-tuple-element.62.kv_ref, bf16[64,128,256]{2,1,0:T(8,128)(2,1)} %get-tuple-element.63.gq_ref), custom_call_target="tpu_custom_call" | custom-call | flops 2147483648 | bytes 5242880 | tf_op jit(solution)/shard_map/attention/pallas_call | solution.py:262
  223.6 21.4 %all-to-all-done.4.rows_ref = bf16[256,16,128]{2,1,0:T(8,128)(2,1)S(1)} async-done(((bf16[256,16,128]{2,1,0:T(8,128)(2,1)}), bf16[256,16,128]{2,1,0:T(8,128)(2,1)S(1)}, u32[]{:S(2)}, u32[]{:S(2)}) %all-to-all-start.4) | async-done | bytes 1048608 | tf_op jit(solution)/shard_map/all_to_all | solution.py:392
  245.0 5.4 %all-to-all-start.5 = ((bf16[256,16,128]{2,1,0:T(8,128)(2,1)}), bf16[256,16,128]{2,1,0:T(8,128)(2,1)S(1)}, u32[]{:S(2)}, u32[]{:S(2)}) async-start(bf16[256,16,128]{2,1,0:T(8,128)(2,1)} %bitcast.7), calls=%async_computation.5 | async-start | bytes 2097152 | tf_op jit(solution)/shard_map/all_to_all | solution.py:394
  250.5 0.6 pad_add_fusion
  251.1 8.2 %weight_grad.2 = bf16[4,8,4,16,128]{4,3,2,1,0:T(8,128)(2,1)} custom-call(s32[2]{0:T(128)} %get-tuple-element.90.where_ref, bf16[256,16,128]{2,1,0:T(8,128)(2,1)} %copy-done.5, bf16[4,2080,256]{2,1,0:T(8,128)(2,1)} %bitcast.43, bf16[4,2080,256]{2,1,0:T(8,128)(2,1)} %collective-permute-done.3.act_b), custom_call_target="tpu_custom_call" | custom-call | flops 2147483648 | bytes 12582912 | tf_op jit(solution)/shard_map/weight_grad/pallas_call | solution.py:322
  259.3 1.1 dynamic-slice_bitcast_fusion.2
  260.4 0.7 collective-permute-start.4
  261.0 2.4 collective-permute-start.5
  263.5 1.1 collective-permute-start.6
  264.6 2.6 collective-permute-done.4
  267.2 6.9 %collective-permute-done.5 = bf16[8,4,16,128]{3,2,1,0:T(8,128)(2,1)S(1)} collective-permute-done((bf16[8,4,16,128]{3,2,1,0:T(8,128)(2,1)S(1)}, bf16[8,4,16,128]{3,2,1,0:T(8,128)(2,1)S(1)}, u32[]{:S(2)}, u32[]{:S(2)}) %collective-permute-start.5) | collective-permute-done | bytes 131104 | tf_op jit(solution)/shard_map/ppermute | solution.py:411
  274.1 1.0 fusion.2
  275.1 7.0 %all-to-all-done.5.rows_ref = bf16[256,16,128]{2,1,0:T(8,128)(2,1)S(1)} async-done(((bf16[256,16,128]{2,1,0:T(8,128)(2,1)}), bf16[256,16,128]{2,1,0:T(8,128)(2,1)S(1)}, u32[]{:S(2)}, u32[]{:S(2)}) %all-to-all-start.5) | async-done | bytes 1048608 | tf_op jit(solution)/shard_map/all_to_all | solution.py:394
  282.1 1.0 copy-done.4
  283.1 8.2 %weight_grad.3 = bf16[4,8,4,16,128]{4,3,2,1,0:T(8,128)(2,1)} custom-call(s32[2]{0:T(128)} %get-tuple-element.91.where_ref, bf16[256,16,128]{2,1,0:T(8,128)(2,1)} %copy-done.4, bf16[4,2080,256]{2,1,0:T(8,128)(2,1)} %bitcast.44, bf16[4,2080,256]{2,1,0:T(8,128)(2,1)} %collective-permute-done.3.act_b), custom_call_target="tpu_custom_call" | custom-call | flops 2147483648 | bytes 12582912 | tf_op jit(solution)/shard_map/weight_grad/pallas_call | solution.py:322
  291.3 12.3 %all_to_all.43 = bf16[4,8,4,16,128]{4,3,2,1,0:T(8,128)(2,1)S(1)} all-to-all(bf16[4,8,4,16,128]{4,3,2,1,0:T(8,128)(2,1)} %weight_grad.3), channel_id=1, replica_groups={{0,16,32,48},{1,17,33,49},{2,18,34,50},{3,19,35,51},{4,20,36,52},{5,21,..., dimensions={0} | all-to-all | bytes 1048576 | tf_op jit(solution)/shard_map/all_to_all | solution.py:415
  303.6 0.1 reduce.1
  303.7 12.6 %all_to_all.44 = bf16[8,4,32,128]{3,2,1,0:T(8,128)(2,1)S(1)} all-to-all(bf16[8,4,32,128]{3,2,1,0:T(8,128)(2,1)S(1)} %pad_maximum_fusion.3), channel_id=1, replica_groups={{0,2,4,6,8,10,12,14},{1,3,5,7,9,11,13,15},{16,18,20,22,24,26,28,30},{17..., dimensions={0} | all-to-all | bytes 524288 | tf_op jit(solution)/shard_map/all_to_all | solution.py:418
  316.3 10.1 %all_to_all.45 = f32[8,2,8,128]{3,2,1,0:T(8,128)S(1)} all-to-all(f32[8,2,8,128]{3,2,1,0:T(8,128)S(1)} %bitcast.47), channel_id=1, replica_groups={{0,1,64,65,128,129,192,193},{2,3,66,67,130,131,194,195},{4,5,68,69,132,..., dimensions={0} | all-to-all | bytes 131072 | tf_op jit(solution)/shard_map/all_to_all | solution.py:425
  326.5 0.7 copy.33
  (26 shorter events, 0.2 us)
Async XLA Ops:
  7.4 0.7 copy-start.1
  9.2 0.6 copy-start.2
  9.8 1.2 copy-start.3
  17.7 86.7 %all-to-all-start.2 = ((bf16[64,96,256]{2,1,0:T(8,128)(2,1)}), bf16[64,96,256]{2,1,0:T(8,128)(2,1)S(1)}, u32[]{:S(2)}, u32[]{:S(2)}) async-start(bf16[64,96,256]{2,1,0:T(8,128)(2,1)} %compact.3), calls=%async_computation.2 | async-start | bytes 6291456 | tf_op jit(solution)/shard_map/all_to_all | solution.py:367
  30.9 15.5 %collective-permute-start = (f32[8,128]{1,0:T(8,128)S(1)}, f32[8,128]{1,0:T(8,128)S(1)}, u32[]{:S(2)}, u32[]{:S(2)}) collective-permute-start(f32[8,128]{1,0:T(8,128)S(1)} %get-tuple-element.59), channel_id=1, source_target_pairs={{0,64},{64,128},{128,192},{192,0},{1,65},{65,129},{129,193},{193,1... | collective-permute-start | bytes 12296 | tf_op jit(solution)/shard_map/ppermute | solution.py:365
  32.1 14.2 %collective-permute-start.1 = (f32[8,128]{1,0:T(8,128)S(1)}, f32[8,128]{1,0:T(8,128)S(1)}, u32[]{:S(2)}, u32[]{:S(2)}) collective-permute-start(f32[8,128]{1,0:T(8,128)S(1)} %get-tuple-element.59), channel_id=1, source_target_pairs={{0,128},{64,192},{128,0},{192,64},{1,129},{65,193},{129,1},{193,65... | collective-permute-start | bytes 12296 | tf_op jit(solution)/shard_map/ppermute | solution.py:365
  34.6 11.7 %collective-permute-start.2 = (f32[8,128]{1,0:T(8,128)S(1)}, f32[8,128]{1,0:T(8,128)S(1)}, u32[]{:S(2)}, u32[]{:S(2)}) collective-permute-start(f32[8,128]{1,0:T(8,128)S(1)} %get-tuple-element.59), channel_id=1, source_target_pairs={{0,192},{64,0},{128,64},{192,128},{1,193},{65,1},{129,65},{193,129... | collective-permute-start | bytes 12296 | tf_op jit(solution)/shard_map/ppermute | solution.py:365
  38.1 7.1 %copy-start.6 = (bf16[1,256,2048]{1,2,0:T(8,128)(2,1)S(1)}, bf16[1,256,2048]{1,2,0:T(8,128)(2,1)}, u32[]{:S(2)}) copy-start(bf16[1,256,2048]{1,2,0:T(8,128)(2,1)} %copy.27) | copy-start | bytes 3145732
  104.4 11.9 %copy-start = (bf16[64,96,256]{2,1,0:T(8,128)(2,1)}, bf16[64,96,256]{2,1,0:T(8,128)(2,1)S(1)}, u32[]{:S(2)}) copy-start(bf16[64,96,256]{2,1,0:T(8,128)(2,1)S(1)} %all-to-all-done.2.got_ref.note_ref) | copy-start | bytes 9437188
  104.4 79.7 %all-to-all-start.3 = ((bf16[64,96,256]{2,1,0:T(8,128)(2,1)}), bf16[64,96,256]{2,1,0:T(8,128)(2,1)}, u32[]{:S(2)}, u32[]{:S(2)}) async-start(bf16[64,96,256]{2,1,0:T(8,128)(2,1)} %compact.2), calls=%async_computation.3 | async-start | bytes 6291456 | tf_op jit(solution)/shard_map/all_to_all | solution.py:374
  110.6 82.0 %all-gather.3.cloned.1.call-start = ((), (), s32[]{:S(2)}) async-start(), calls=%async_computation.9 | async-start | bytes 5324800 | tf_op jit(solution)/shard_map/all_gather | solution.py:376
  186.3 6.5 %copy-start.7 = (bf16[1,256,2048]{2,1,0:T(8,128)(2,1)S(1)}, bf16[1,256,2048]{2,1,0:T(8,128)(2,1)}, u32[]{:S(2)}) copy-start(bf16[1,256,2048]{2,1,0:T(8,128)(2,1)} %param.12) | copy-start | bytes 3145732
  186.3 6.5 %copy-start.8 = (bf16[1,256,2048]{2,1,0:T(8,128)(2,1)S(1)}, bf16[1,256,2048]{2,1,0:T(8,128)(2,1)}, u32[]{:S(2)}) copy-start(bf16[1,256,2048]{2,1,0:T(8,128)(2,1)} %param.10) | copy-start | bytes 3145732
  192.6 58.5 %collective-permute-start.3 = (bf16[4,2080,256]{2,1,0:T(8,128)(2,1)}, bf16[4,2080,256]{2,1,0:T(8,128)(2,1)}, u32[]{:S(2)}, u32[]{:S(2)}) collective-permute-start(bf16[4,2080,256]{2,1,0:T(8,128)(2,1)} %bitcast.42), channel_id=1, source_target_pairs={{0,1},{1,0},{2,3},{3,2},{4,5},{5,4},{6,7},{7,6},{8,9},{9,8},{10,11... | collective-permute-start | bytes 12779528 | tf_op jit(solution)/shard_map/ppermute | solution.py:377
  203.9 41.0 %all-to-all-start.4 = ((bf16[256,16,128]{2,1,0:T(8,128)(2,1)}), bf16[256,16,128]{2,1,0:T(8,128)(2,1)S(1)}, u32[]{:S(2)}, u32[]{:S(2)}) async-start(bf16[256,16,128]{2,1,0:T(8,128)(2,1)} %bitcast.8), calls=%async_computation.4 | async-start | bytes 2097152 | tf_op jit(solution)/shard_map/all_to_all | solution.py:392
  245.0 6.1 %copy-start.5 = (bf16[256,16,128]{2,1,0:T(8,128)(2,1)}, bf16[256,16,128]{2,1,0:T(8,128)(2,1)S(1)}, u32[]{:S(2)}) copy-start(bf16[256,16,128]{2,1,0:T(8,128)(2,1)S(1)} %all-to-all-done.4.rows_ref) | copy-start | bytes 3145732
  245.0 37.1 %all-to-all-start.5 = ((bf16[256,16,128]{2,1,0:T(8,128)(2,1)}), bf16[256,16,128]{2,1,0:T(8,128)(2,1)S(1)}, u32[]{:S(2)}, u32[]{:S(2)}) async-start(bf16[256,16,128]{2,1,0:T(8,128)(2,1)} %bitcast.7), calls=%async_computation.5 | async-start | bytes 2097152 | tf_op jit(solution)/shard_map/all_to_all | solution.py:394
  260.4 6.9 %collective-permute-start.4 = (bf16[8,4,16,128]{3,2,1,0:T(8,128)(2,1)S(1)}, bf16[8,4,16,128]{3,2,1,0:T(8,128)(2,1)S(1)}, u32[]{:S(2)}, u32[]{:S(2)}) collective-permute-start(bf16[8,4,16,128]{3,2,1,0:T(8,128)(2,1)S(1)} %get-tuple-element.85), channel_id=1, source_target_pairs={{0,16},{1,17},{2,18},{3,19},{4,20},{5,21},{6,22},{7,23},{8,24},{9,... | collective-permute-start | bytes 393224 | tf_op jit(solution)/shard_map/ppermute | solution.py:411
  261.0 13.1 %collective-permute-start.5 = (bf16[8,4,16,128]{3,2,1,0:T(8,128)(2,1)S(1)}, bf16[8,4,16,128]{3,2,1,0:T(8,128)(2,1)S(1)}, u32[]{:S(2)}, u32[]{:S(2)}) collective-permute-start(bf16[8,4,16,128]{3,2,1,0:T(8,128)(2,1)S(1)} %get-tuple-element.87), channel_id=1, source_target_pairs={{0,32},{1,33},{2,34},{3,35},{4,36},{5,37},{6,38},{7,39},{8,40},{9,... | collective-permute-start | bytes 393224 | tf_op jit(solution)/shard_map/ppermute | solution.py:411
  263.5 10.6 %collective-permute-start.6 = (bf16[8,4,16,128]{3,2,1,0:T(8,128)(2,1)S(1)}, bf16[8,4,16,128]{3,2,1,0:T(8,128)(2,1)S(1)}, u32[]{:S(2)}, u32[]{:S(2)}) collective-permute-start(bf16[8,4,16,128]{3,2,1,0:T(8,128)(2,1)S(1)} %get-tuple-element.86), channel_id=1, source_target_pairs={{0,48},{1,49},{2,50},{3,51},{4,52},{5,53},{6,54},{7,55},{8,56},{9,... | collective-permute-start | bytes 393224 | tf_op jit(solution)/shard_map/ppermute | solution.py:411
  282.1 1.0 copy-start.4
Sparse Core Ops, SparseCore 0:
  113.3 52.2 all-gather.2

commit v5 on v3

--- a/solution.py
+++ b/solution.py
@@ -18,8 +18,8 @@
 CHUNKS = 2
 HPC = HEADS // CHUNKS
 COMPACT = 96
-GROUP = 16
-FILLS = 4
+GROUP = 32
+FILLS = 2
 EMPTY = 128.0
 VMEM = 48 * 1024 * 1024
 BF = jnp.bfloat16
@@ -148,7 +148,18 @@
     )(slots.reshape(FILLS, share, TOK), row_of, held, flag, one, two)
 
 
-def spread_kernel(mark, got_ref, note_ref, out_ref):
+def spread_kernel(mark, got_ref, note_ref, out_ref, flag_ref):
+    notes = got_ref[:, : 2 * CELL, HEAD:].astype(F32)[:, 0, :]
+    flag = jnp.broadcast_to(jnp.max(notes, axis=0, keepdims=True), flag_ref.shape)
+
+    @pl.when(pl.program_id(0) == 0)
+    def _():
+        flag_ref[...] = flag
+
+    @pl.when(pl.program_id(0) > 0)
+    def _():
+        flag_ref[...] = jnp.maximum(flag_ref[...], flag)
+
     slots = HEADS * CELL
     row = lax.broadcasted_iota(jnp.int32, (slots, slots), 0)
     col = lax.broadcasted_iota(jnp.int32, (slots, slots), 1)
@@ -176,8 +187,14 @@
             pl.BlockSpec((GROUP, COMPACT, 2 * HEAD), lambda p: (p, 0, 0)),
             pl.BlockSpec((GROUP, 2 * CELL, 2 * HEAD), lambda p: (p, 0, 0)),
         ],
-        out_specs=pl.BlockSpec((GROUP, HEADS * CELL, 2 * HEAD), lambda p: (p, 0, 0)),
-        out_shape=jax.ShapeDtypeStruct((OWNERS, HEADS * CELL, 2 * HEAD), BF),
+        out_specs=(
+            pl.BlockSpec((GROUP, HEADS * CELL, 2 * HEAD), lambda p: (p, 0, 0)),
+            pl.BlockSpec((8, HEAD), lambda p: (0, 0)),
+        ),
+        out_shape=(
+            jax.ShapeDtypeStruct((OWNERS, HEADS * CELL, 2 * HEAD), BF),
+            jax.ShapeDtypeStruct((8, HEAD), F32),
+        ),
         compiler_params=params("arbitrary"),
         cost_estimate=pl.CostEstimate(
             flops=2 * 2**30, bytes_accessed=8 * 2**20, transcendentals=0
@@ -232,29 +249,28 @@
         bias_ref[...] = jnp.where(keep, 0.0, -1e30)
 
     first = jnp.where(lax.broadcasted_iota(jnp.int32, (8, HEAD), 1) == 0, 1.0, 0.0).astype(BF)
-    pairs = [ref[...].astype(F32) for ref in (kv_ref, gq_ref)]
-    step = 256
-    for e in range(2):
-        kv, gq = (
-            pair[:, e * CELL : (e + 1) * CELL, :].reshape(SLOTS, 2 * HEAD).astype(BF)
-            for pair in pairs
-        )
-        k, v, g, q = kv[:, :HEAD], kv[:, HEAD:], gq[:, :HEAD], gq[:, HEAD:]
-        key_bias = jnp.where(dot(first, k, NT)[0:1, :] > 0.5 * EMPTY, -1e30, 0.0)
-        for i in range(SLOTS // step):
-            here = slice(i * step, (i + 1) * step)
-            n = (i + 1) * step
-            score = dot(q[here], k[:n], NT) * to_exp2 + bias_ref[here, :n] + key_bias[:, :n]
-            raised = jnp.exp2(score)
-            total = jnp.sum(raised, axis=1, keepdims=True)
-            weights = raised * (1.0 / jnp.where(total == 0.0, 1.0, total))
-            attended = dot(weights.astype(BF), v[:n], NN)
-            dweights = dot(g[here], v[:n], NT)
-            delta = jnp.sum(g[here].astype(F32) * attended, axis=1, keepdims=True)
-            dscores = (weights * (dweights - delta)).astype(BF)
-            dquery = (dot(dscores, k[:n], NN) * scale).astype(BF)
-            tiles = step // (2 * CELL)
-            out_ref[0, i * tiles : (i + 1) * tiles, e] = dquery.reshape(tiles, 2 * CELL, HEAD)
+    def halves(ref):
+        pair = ref[...].astype(F32)
+        heads = [pair[:, e * CELL : (e + 1) * CELL, :].reshape(SLOTS, 2 * HEAD) for e in range(2)]
+        return [x[:, n * HEAD : (n + 1) * HEAD].astype(BF) for n in range(2) for x in heads]
+
+    both = range(2)
+    k, v = (lambda x: (x[:2], x[2:]))(halves(kv_ref))
+    g, q = (lambda x: (x[:2], x[2:]))(halves(gq_ref))
+    key_bias = [
+        jnp.where(dot(first, k[e], NT)[0:1, :] > 0.5 * EMPTY, -1e30, 0.0) for e in both
+    ]
+    scores = [dot(q[e], k[e], NT) for e in both]
+    dweights = [dot(g[e], v[e], NT) for e in both]
+    raised = [jnp.exp2(scores[e] * to_exp2 + bias_ref[...] + key_bias[e]) for e in both]
+    totals = [jnp.sum(raised[e], axis=1, keepdims=True) for e in both]
+    weights = [raised[e] * (1.0 / jnp.where(totals[e] == 0.0, 1.0, totals[e])) for e in both]
+    attended = [dot(weights[e].astype(BF), v[e], NN) for e in both]
+    delta = [jnp.sum(g[e].astype(F32) * attended[e], axis=1, keepdims=True) for e in both]
+    dscores = [(weights[e] * (dweights[e] - delta[e])).astype(BF) for e in both]
+    for e in both:
+        dquery = (dot(dscores[e], k[e], NN) * scale).astype(BF)
+        out_ref[0, :, e] = dquery.reshape(OWNERS // 2, 2 * CELL, HEAD)
 
 
 def attention(kv, gq, first):
@@ -283,14 +299,17 @@
     b = pl.program_id(0)
     head, core = where_ref[0], where_ref[1]
     features = acc_ref.shape[0]
-    rows = rows_ref[...].reshape(OWNERS * 2 * CELL, HEAD)
+    rows = rows_ref[...].astype(F32)
+    low, high = (rows[:, e * CELL : (e + 1) * CELL].reshape(SLOTS, HEAD) for e in range(2))
+    mine = jnp.where(core == 0, low, high).astype(BF)
+    other = jnp.where(core == 0, high, low).astype(BF)
     line = lax.broadcasted_iota(jnp.int32, (2 * HEADS, TOK), 0)
-    place = lax.broadcasted_iota(jnp.int32, (OWNERS * 2 * CELL, TOK), 0)
+    place = lax.broadcasted_iota(jnp.int32, (SLOTS, TOK), 0)
     total = None
-    for act_ref, side in ((act_a, core), (act_b, 1 - core)):
+    for act_ref, rows in ((act_a, mine), (act_b, other)):
         slot = act_ref[0, features:, :].astype(F32)
-        weight = jnp.where(line == head, 2.0 * CELL, jnp.where(line == HEADS + head, 1.0, 0.0))
-        index = jnp.sum(slot * weight, axis=0, keepdims=True).astype(jnp.int32) + side * CELL
+        weight = jnp.where(line == head, 1.0 * CELL, jnp.where(line == HEADS + head, 1.0, 0.0))
+        index = jnp.sum(slot * weight, axis=0, keepdims=True).astype(jnp.int32)
         hot = jnp.where(place == index, 1.0, 0.0).astype(BF)
         dquery = dot(rows, hot, ((0,), (0,))).astype(BF)
         term = dot(act_ref[0, :features, :], dquery, NT)
@@ -391,10 +410,10 @@
 
         return jnp.zeros_like(state[0]), whole(True, keys, vals), whole(False, grads, queries)
 
-    too_many = jnp.max(got_gq[:, 0, HEAD]).astype(F32)
-    spreads = (spread(got_kv, got_kv, True), spread(got_gq, got_kv, False))
+    kv, _ = spread(got_kv, got_kv, True)
+    gq, flags = spread(got_gq, got_kv, False)
     _, kv, gq = lax.while_loop(
-        lambda state: state[0] > 0.5, send_all_slots, (too_many, *spreads)
+        lambda state: state[0] > 0.5, send_all_slots, (flags[0, 0], kv, gq)
     )
     part = None
     for c in range(CHUNKS):

time: 335 us -> 328 us (0.979)
  Pallas kernels: 62.1 us -> 51.5 us
  waiting for transfers between devices: 166 us -> 171 us
    pallas_call x2, Pallas kernels: 22.3 us -> 16.4 us  [attention(): pl.pallas_call(attention_kernel, grid=(HPC // 2,), in_specs=[pl.BlockSpec...]
  transfers between devices with their start and end apart: 9 -> 9, of which waited for: 4 -> 4; matrix products, arithmetic and copies ran while one was open for 4% -> 4% of each run, Pallas kernels for 14% -> 12%
where the time goes in v5:
time: 328 us; the launch traced here: 327 us
  waiting for transfers between devices  171 us (52%)
  Pallas kernels  51.5 us (16%)
  starting transfers between devices  37.2 us (11%)
  blocking collectives  36.9 us (11%)
  between operations  13.5 us (4%)
  matrix products  7.08 us (2%)
  local copies, waits for them, and re-layouts  6.75 us (2%)
    all_to_all x1, waiting for transfers between devices, on_device(): got_gq = seq_send(send_gq)  68.2 us
    all_to_all x1, waiting for transfers between devices, on_device(): seq_send(compact(slots, row_of, held, jnp.zeros((8, HEAD), F32), keys, va...  53.6 us
    all_to_all x2, waiting for transfers between devices, on_device(): back = all_send(rows.reshape(devices, 2 * CELL, HEAD))  49 us
    all_to_all x1, blocking collectives, on_device(): terms = all_send(part)  36.9 us
    pallas_call x2, Pallas kernels, attention(): pl.pallas_call(attention_kernel, grid=(HPC // 2,), in_specs=[pl.BlockSpec...  16.4 us
    pallas_call x2, Pallas kernels, weight_grad(): pl.pallas_call(grad_kernel, grid_spec=pltpu.PrefetchScalarGridSpec(num_sc...  14.2 us
    all_to_all x2, starting transfers between devices, on_device(): back = all_send(rows.reshape(devices, 2 * CELL, HEAD))  13.6 us
    all_to_all x1, starting transfers between devices, on_device(): seq_send(compact(slots, row_of, held, jnp.zeros((8, HEAD), F32), keys, va...  13.2 us
  transfers between devices with their start and end apart: 9, of which 4 were waited for; matrix products, arithmetic and copies ran while one was open for 4% of the time, Pallas kernels for 12%

profile of v5, /device:TPU:1, one launch (start us, length us, event | category | flops | bytes accessed | tf_op | source)
XLA Modules:
  0.0 326.8 jit_solution(12153700756579121628)
XLA Ops:
  6.5 0.8 copy.13.col_ref
  7.4 0.0 copy-start.1
  7.4 0.7 copy-done.1
  8.1 1.1 slots.1
  9.2 0.6 copy-done.2
  9.8 0.6 copy-done.3
  10.4 0.6 broadcast_in_dim.3.flag_ref
  11.0 5.1 %compact.3 = bf16[64,96,256]{2,1,0:T(8,128)(2,1)} custom-call(s32[2,8,256]{2,1,0:T(8,128)S(1)} %bitcast.32, f32[64,128]{1,0:T(8,128)} %copy-done.3, f32[64,128]{1,0:T(8,128)} %copy-done.2, f32[8,128]{1,0:T(8,128)} %broadcast_in_dim.3.flag_ref, bf16[256,2048]{1,0:T(8,128)(2,1)} %bitcast.37, bf16[256,2048]{1,0:T(8,128)(2,1)} %bitcast.39), custom_call_target="tpu_custom_call" | custom-call | flops 4294967296 | bytes 8388608 | tf_op jit(solution)/shard_map/compact/pallas_call | solution.py:127
  16.1 13.2 %all-to-all-start.2 = ((bf16[64,96,256]{2,1,0:T(8,128)(2,1)}), bf16[64,96,256]{2,1,0:T(8,128)(2,1)S(1)}, u32[]{:S(2)}, u32[]{:S(2)}) async-start(bf16[64,96,256]{2,1,0:T(8,128)(2,1)} %compact.3), calls=%async_computation.2 | async-start | bytes 6291456 | tf_op jit(solution)/shard_map/all_to_all | solution.py:394
  29.3 2.6 collective-permute-start.2
  31.8 0.5 collective-permute-start.1
  32.3 0.6 collective-permute-start
  32.9 2.3 copy.14
  35.2 0.0 copy-start.4
  35.2 7.1 %convolution_convert_fusion.two_ref = bf16[256,2048]{1,0:T(8,128)(2,1)} fusion(bf16[2048,2048]{1,0:T(8,128)(2,1)} %param.9, bf16[1,256,2048]{2,1,0:T(8,128)(2,1)} %param.8), kind=kOutput, calls=%fused_computation.2 | convolution fusion | flops 2148007936 | bytes 10485760 | tf_op jit(solution)/shard_map/dot_general | solution.py:395
  42.3 0.0 copy-done.4
  42.3 1.2 pad_maximum_fusion.2
  43.5 0.0 collective-permute-done.2
  43.5 0.0 collective-permute-done.1
  43.5 0.0 collective-permute-done
  43.5 0.6 maximum_maximum_fusion.flag_ref
  44.1 5.1 %compact.2 = bf16[64,96,256]{2,1,0:T(8,128)(2,1)} custom-call(s32[2,8,256]{2,1,0:T(8,128)S(1)} %bitcast.33, f32[64,128]{1,0:T(8,128)} %copy-done.3, f32[64,128]{1,0:T(8,128)} %copy-done.2, f32[8,128]{1,0:T(8,128)} %maximum_maximum_fusion.flag_ref, bf16[256,2048]{1,0:T(8,128)(2,1)} %bitcast.35, bf16[256,2048]{1,0:T(8,128)(2,1)} %convolution_convert_fusion.two_ref), custom_call_target="tpu_custom_call" | custom-call | flops 4294967296 | bytes 8388608 | tf_op jit(solution)/shard_map/compact/pallas_call | solution.py:127
  49.2 53.6 %all-to-all-done.2.note_ref.got_ref = bf16[64,96,256]{2,1,0:T(8,128)(2,1)S(1)} async-done(((bf16[64,96,256]{2,1,0:T(8,128)(2,1)}), bf16[64,96,256]{2,1,0:T(8,128)(2,1)S(1)}, u32[]{:S(2)}, u32[]{:S(2)}) %all-to-all-start.2) | async-done | bytes 3145760 | tf_op jit(solution)/shard_map/all_to_all | solution.py:394
  102.8 6.2 %all-to-all-start.3 = ((bf16[64,96,256]{2,1,0:T(8,128)(2,1)}), bf16[64,96,256]{2,1,0:T(8,128)(2,1)}, u32[]{:S(2)}, u32[]{:S(2)}) async-start(bf16[64,96,256]{2,1,0:T(8,128)(2,1)} %compact.2), calls=%async_computation.3 | async-start | bytes 6291456 | tf_op jit(solution)/shard_map/all_to_all | solution.py:401
  109.0 0.2 all-gather.3.cloned.1.call-start
  109.3 0.5 all-gather.3.cloned.1.call-update
  109.8 4.5 %spread.3 = (bf16[64,128,256]{2,1,0:T(8,128)(2,1)}, f32[8,128]{1,0:T(8,128)}) custom-call(bf16[64,96,256]{2,1,0:T(8,128)(2,1)S(1)} %all-to-all-done.2.note_ref.got_ref, bf16[64,96,256]{2,1,0:T(8,128)(2,1)S(1)} %all-to-all-done.2.note_ref.got_ref), custom_call_target="tpu_custom_call" | custom-call | flops 2147483648 | bytes 8388608 | tf_op jit(solution)/shard_map/spread/pallas_call | solution.py:183
  114.3 0.0 copy-done
  114.3 68.2 %all-to-all-done.3.got_ref = bf16[64,96,256]{2,1,0:T(8,128)(2,1)} async-done(((bf16[64,96,256]{2,1,0:T(8,128)(2,1)}), bf16[64,96,256]{2,1,0:T(8,128)(2,1)}, u32[]{:S(2)}, u32[]{:S(2)}) %all-to-all-start.3) | async-done | bytes 3145760 | tf_op jit(solution)/shard_map/all_to_all | solution.py:401
  182.5 5.0 %spread.2 = (bf16[64,128,256]{2,1,0:T(8,128)(2,1)}, f32[8,128]{1,0:T(8,128)S(1)}) custom-call(bf16[64,96,256]{2,1,0:T(8,128)(2,1)} %all-to-all-done.3.got_ref, bf16[64,96,256]{2,1,0:T(8,128)(2,1)} %copy-done), custom_call_target="tpu_custom_call" | custom-call | flops 2147483648 | bytes 8388608 | tf_op jit(solution)/shard_map/spread/pallas_call | solution.py:183
  187.5 0.5 slice.3
  188.0 0.3 collective-permute-start.3
  188.3 0.0 copy-done.5
  188.3 0.0 copy-done.6
  188.3 0.7 while.11
  189.0 8.2 %attention.3 = bf16[4,32,2,16,128]{4,3,2,1,0:T(8,128)(2,1)} custom-call(bf16[64,128,256]{2,1,0:T(8,128)(2,1)} %get-tuple-element.64.kv_ref, bf16[64,128,256]{2,1,0:T(8,128)(2,1)} %get-tuple-element.65.gq_ref), custom_call_target="tpu_custom_call" | custom-call | flops 2147483648 | bytes 5242880 | tf_op jit(solution)/shard_map/attention/pallas_call | solution.py:277
  197.1 8.4 %all-to-all-start.5 = ((bf16[256,16,128]{2,1,0:T(8,128)(2,1)}), bf16[256,16,128]{2,1,0:T(8,128)(2,1)S(1)}, u32[]{:S(2)}, u32[]{:S(2)}) async-start(bf16[256,16,128]{2,1,0:T(8,128)(2,1)} %bitcast.14), calls=%async_computation.5 | async-start | bytes 2097152 | tf_op jit(solution)/shard_map/all_to_all | solution.py:421
  205.6 8.2 %attention.2 = bf16[4,32,2,16,128]{4,3,2,1,0:T(8,128)(2,1)} custom-call(bf16[64,128,256]{2,1,0:T(8,128)(2,1)} %get-tuple-element.64.kv_ref, bf16[64,128,256]{2,1,0:T(8,128)(2,1)} %get-tuple-element.65.gq_ref), custom_call_target="tpu_custom_call" | custom-call | flops 2147483648 | bytes 5242880 | tf_op jit(solution)/shard_map/attention/pallas_call | solution.py:277
  213.8 24.3 %all-to-all-done.5.rows_ref = bf16[256,16,128]{2,1,0:T(8,128)(2,1)S(1)} async-done(((bf16[256,16,128]{2,1,0:T(8,128)(2,1)}), bf16[256,16,128]{2,1,0:T(8,128)(2,1)S(1)}, u32[]{:S(2)}, u32[]{:S(2)}) %all-to-all-start.5) | async-done | bytes 1048608 | tf_op jit(solution)/shard_map/all_to_all | solution.py:421
  238.1 5.2 %all-to-all-start.4 = ((bf16[256,16,128]{2,1,0:T(8,128)(2,1)}), bf16[256,16,128]{2,1,0:T(8,128)(2,1)S(1)}, u32[]{:S(2)}, u32[]{:S(2)}) async-start(bf16[256,16,128]{2,1,0:T(8,128)(2,1)} %bitcast.11), calls=%async_computation.4 | async-start | bytes 2097152 | tf_op jit(solution)/shard_map/all_to_all | solution.py:421
  243.3 0.1 pad_add_fusion
  243.3 0.0 collective-permute-done.3.act_b
  243.3 7.1 %weight_grad.2.refs_0_ = f32[2048,128]{1,0:T(8,128)S(1)} custom-call(s32[2]{0:T(128)S(1)} %get-tuple-element.86.where_ref, bf16[256,16,128]{2,1,0:T(8,128)(2,1)S(1)} %all-to-all-done.5.rows_ref, bf16[4,2080,256]{2,1,0:T(8,128)(2,1)} %bitcast.28, bf16[4,2080,256]{2,1,0:T(8,128)(2,1)} %collective-permute-done.3.act_b), custom_call_target="tpu_custom_call" | custom-call | flops 2147483648 | bytes 12582912 | tf_op jit(solution)/shard_map/weight_grad/pallas_call | solution.py:353
  250.4 24.7 %all-to-all-done.4.rows_ref = bf16[256,16,128]{2,1,0:T(8,128)(2,1)S(1)} async-done(((bf16[256,16,128]{2,1,0:T(8,128)(2,1)}), bf16[256,16,128]{2,1,0:T(8,128)(2,1)S(1)}, u32[]{:S(2)}, u32[]{:S(2)}) %all-to-all-start.4) | async-done | bytes 1048608 | tf_op jit(solution)/shard_map/all_to_all | solution.py:421
  275.2 7.1 %weight_grad.3 = bf16[256,16,128]{2,1,0:T(8,128)(2,1)S(1)} custom-call(s32[2]{0:T(128)S(1)} %get-tuple-element.85.where_ref, bf16[256,16,128]{2,1,0:T(8,128)(2,1)S(1)} %all-to-all-done.4.rows_ref, bf16[4,2080,256]{2,1,0:T(8,128)(2,1)} %bitcast.29, bf16[4,2080,256]{2,1,0:T(8,128)(2,1)} %collective-permute-done.3.act_b, f32[2048,128]{1,0:T(8,128)S(1)} %weight_grad.2.refs_0_), custom_call_target="tpu_custom_call" | custom-call | flops 2147483648 | bytes 12582912 | tf_op jit(solution)/shard_map/weight_grad/pallas_call | solution.py:353
  282.3 36.9 %all_to_all.33 = bf16[256,16,128]{2,1,0:T(8,128)(2,1)S(1)} all-to-all(bf16[256,16,128]{2,1,0:T(8,128)(2,1)S(1)} %weight_grad.3), channel_id=1, replica_groups=mesh['dp'=4,'seq'=64] {'dp','seq'}, dimensions={0} | all-to-all | bytes 2097152 | tf_op jit(solution)/shard_map/all_to_all | solution.py:424
  319.2 0.1 convert_reduce_fusion
  319.3 0.6 copy.15
  (7 shorter events, 0.0 us)
Async XLA Ops:
  7.4 0.7 copy-start.1
  9.2 0.6 copy-start.2
  9.8 0.6 copy-start.3
  16.1 86.7 %all-to-all-start.2 = ((bf16[64,96,256]{2,1,0:T(8,128)(2,1)}), bf16[64,96,256]{2,1,0:T(8,128)(2,1)S(1)}, u32[]{:S(2)}, u32[]{:S(2)}) async-start(bf16[64,96,256]{2,1,0:T(8,128)(2,1)} %compact.3), calls=%async_computation.2 | async-start | bytes 6291456 | tf_op jit(solution)/shard_map/all_to_all | solution.py:394
  29.3 14.2 %collective-permute-start.2 = (f32[8,128]{1,0:T(8,128)S(1)}, f32[8,128]{1,0:T(8,128)S(1)}, u32[]{:S(2)}, u32[]{:S(2)}) collective-permute-start(f32[8,128]{1,0:T(8,128)S(1)} %get-tuple-element.58), channel_id=1, source_target_pairs={{0,192},{64,0},{128,64},{192,128},{1,193},{65,1},{129,65},{193,129... | collective-permute-start | bytes 12296 | tf_op jit(solution)/shard_map/ppermute | solution.py:392
  31.8 11.7 %collective-permute-start.1 = (f32[8,128]{1,0:T(8,128)S(1)}, f32[8,128]{1,0:T(8,128)S(1)}, u32[]{:S(2)}, u32[]{:S(2)}) collective-permute-start(f32[8,128]{1,0:T(8,128)S(1)} %get-tuple-element.58), channel_id=1, source_target_pairs={{0,128},{64,192},{128,0},{192,64},{1,129},{65,193},{129,1},{193,65... | collective-permute-start | bytes 12296 | tf_op jit(solution)/shard_map/ppermute | solution.py:392
  32.3 11.1 %collective-permute-start = (f32[8,128]{1,0:T(8,128)S(1)}, f32[8,128]{1,0:T(8,128)S(1)}, u32[]{:S(2)}, u32[]{:S(2)}) collective-permute-start(f32[8,128]{1,0:T(8,128)S(1)} %get-tuple-element.58), channel_id=1, source_target_pairs={{0,64},{64,128},{128,192},{192,0},{1,65},{65,129},{129,193},{193,1... | collective-permute-start | bytes 12296 | tf_op jit(solution)/shard_map/ppermute | solution.py:392
  35.2 7.1 %copy-start.4 = (bf16[1,256,2048]{1,2,0:T(8,128)(2,1)S(1)}, bf16[1,256,2048]{1,2,0:T(8,128)(2,1)}, u32[]{:S(2)}) copy-start(bf16[1,256,2048]{1,2,0:T(8,128)(2,1)} %copy.14) | copy-start | bytes 3145732
  102.8 11.5 %copy-start = (bf16[64,96,256]{2,1,0:T(8,128)(2,1)}, bf16[64,96,256]{2,1,0:T(8,128)(2,1)S(1)}, u32[]{:S(2)}) copy-start(bf16[64,96,256]{2,1,0:T(8,128)(2,1)S(1)} %all-to-all-done.2.note_ref.got_ref) | copy-start | bytes 9437188
  102.8 79.7 %all-to-all-start.3 = ((bf16[64,96,256]{2,1,0:T(8,128)(2,1)}), bf16[64,96,256]{2,1,0:T(8,128)(2,1)}, u32[]{:S(2)}, u32[]{:S(2)}) async-start(bf16[64,96,256]{2,1,0:T(8,128)(2,1)} %compact.2), calls=%async_computation.3 | async-start | bytes 6291456 | tf_op jit(solution)/shard_map/all_to_all | solution.py:401
  109.0 79.0 %all-gather.3.cloned.1.call-start = ((), (), s32[]{:S(2)}) async-start(), calls=%async_computation.7 | async-start | bytes 5324800 | tf_op jit(solution)/shard_map/all_gather | solution.py:403
  182.5 5.8 %copy-start.5 = (bf16[1,256,2048]{2,1,0:T(8,128)(2,1)S(1)}, bf16[1,256,2048]{2,1,0:T(8,128)(2,1)}, u32[]{:S(2)}) copy-start(bf16[1,256,2048]{2,1,0:T(8,128)(2,1)} %param.12) | copy-start | bytes 3145732
  182.5 5.8 %copy-start.6 = (bf16[1,256,2048]{2,1,0:T(8,128)(2,1)S(1)}, bf16[1,256,2048]{2,1,0:T(8,128)(2,1)}, u32[]{:S(2)}) copy-start(bf16[1,256,2048]{2,1,0:T(8,128)(2,1)} %param.10) | copy-start | bytes 3145732
  188.0 55.3 %collective-permute-start.3 = (bf16[4,2080,256]{2,1,0:T(8,128)(2,1)}, bf16[4,2080,256]{2,1,0:T(8,128)(2,1)}, u32[]{:S(2)}, u32[]{:S(2)}) collective-permute-start(bf16[4,2080,256]{2,1,0:T(8,128)(2,1)} %bitcast.27), channel_id=1, source_target_pairs={{0,1},{1,0},{2,3},{3,2},{4,5},{5,4},{6,7},{7,6},{8,9},{9,8},{10,11... | collective-permute-start | bytes 12779528 | tf_op jit(solution)/shard_map/ppermute | solution.py:404
  197.1 40.9 %all-to-all-start.5 = ((bf16[256,16,128]{2,1,0:T(8,128)(2,1)}), bf16[256,16,128]{2,1,0:T(8,128)(2,1)S(1)}, u32[]{:S(2)}, u32[]{:S(2)}) async-start(bf16[256,16,128]{2,1,0:T(8,128)(2,1)} %bitcast.14), calls=%async_computation.5 | async-start | bytes 2097152 | tf_op jit(solution)/shard_map/all_to_all | solution.py:421
  238.1 37.1 %all-to-all-start.4 = ((bf16[256,16,128]{2,1,0:T(8,128)(2,1)}), bf16[256,16,128]{2,1,0:T(8,128)(2,1)S(1)}, u32[]{:S(2)}, u32[]{:S(2)}) async-start(bf16[256,16,128]{2,1,0:T(8,128)(2,1)} %bitcast.11), calls=%async_computation.4 | async-start | bytes 2097152 | tf_op jit(solution)/shard_map/all_to_all | solution.py:421
Sparse Core Ops, SparseCore 0:
  111.7 52.2 all-gather.2

commit v6 on v5

--- a/solution.py
+++ b/solution.py
@@ -270,48 +270,54 @@
     dscores = [(weights[e] * (dweights[e] - delta[e])).astype(BF) for e in both]
     for e in both:
         dquery = (dot(dscores[e], k[e], NN) * scale).astype(BF)
-        out_ref[0, :, e] = dquery.reshape(OWNERS // 2, 2 * CELL, HEAD)
-
-
-def attention(kv, gq, first):
+        at = slice(e * 2 * CELL, (e + 1) * 2 * CELL)
+        out_ref[0, :, 0, at] = dquery.reshape(OWNERS // 2, 2 * CELL, HEAD)
+
+
+def attention(kv, gq):
+    def pair_spec():
+        return pl.BlockSpec((OWNERS, 2 * CELL, 2 * HEAD), lambda p: (0, p, 0))
+
+    groups = HEADS // 2
     return pl.pallas_call(
         attention_kernel,
-        grid=(HPC // 2,),
-        in_specs=[
-            pl.BlockSpec((OWNERS, 2 * CELL, 2 * HEAD), lambda p: (0, first + p, 0)),
-            pl.BlockSpec((OWNERS, 2 * CELL, 2 * HEAD), lambda p: (0, first + p, 0)),
-        ],
-        out_specs=pl.BlockSpec((1, OWNERS // 2, 2, 2 * CELL, HEAD), lambda p: (p, 0, 0, 0, 0)),
-        out_shape=jax.ShapeDtypeStruct((HPC // 2, OWNERS // 2, 2, 2 * CELL, HEAD), BF),
+        grid=(groups,),
+        in_specs=[pair_spec(), pair_spec()],
+        out_specs=pl.BlockSpec(
+            (1, OWNERS // 2, 1, 4 * CELL, HEAD), lambda p: (p // 2, 0, p % 2, 0, 0)
+        ),
+        out_shape=jax.ShapeDtypeStruct((groups // 2, OWNERS // 2, 2, 4 * CELL, HEAD), BF),
         scratch_shapes=[pltpu.VMEM((SLOTS, SLOTS), F32)],
-        compiler_params=params("arbitrary"),
+        compiler_params=params("arbitrary", vmem=63 * 1024 * 1024),
         cost_estimate=pl.CostEstimate(
-            flops=HPC * 8 * SLOTS * SLOTS * HEAD,
-            bytes_accessed=5 * 2**20,
-            transcendentals=HPC * SLOTS * SLOTS,
+            flops=HEADS * 8 * SLOTS * SLOTS * HEAD,
+            bytes_accessed=10 * 2**20,
+            transcendentals=HEADS * SLOTS * SLOTS,
         ),
         name="attention",
     )(kv, gq)
 
 
-def grad_kernel(where_ref, rows_ref, act_a, act_b, *refs):
-    earlier_ref, out_ref, acc_ref = refs if len(refs) == 3 else (None, *refs)
+def grad_kernel(where_ref, rows_ref, act_a, act_b, out_ref, acc_ref):
     b = pl.program_id(0)
-    head, core = where_ref[0], where_ref[1]
+    group, core = where_ref[0], where_ref[1]
     features = acc_ref.shape[0]
     rows = rows_ref[...].astype(F32)
-    low, high = (rows[:, e * CELL : (e + 1) * CELL].reshape(SLOTS, HEAD) for e in range(2))
-    mine = jnp.where(core == 0, low, high).astype(BF)
-    other = jnp.where(core == 0, high, low).astype(BF)
+    parts = [rows[:, n * CELL : (n + 1) * CELL].reshape(SLOTS, HEAD) for n in range(4)]
     line = lax.broadcasted_iota(jnp.int32, (2 * HEADS, TOK), 0)
     place = lax.broadcasted_iota(jnp.int32, (SLOTS, TOK), 0)
     total = None
-    for act_ref, rows in ((act_a, mine), (act_b, other)):
+    for act_ref, side in ((act_a, core), (act_b, 1 - core)):
         slot = act_ref[0, features:, :].astype(F32)
-        weight = jnp.where(line == head, 1.0 * CELL, jnp.where(line == HEADS + head, 1.0, 0.0))
-        index = jnp.sum(slot * weight, axis=0, keepdims=True).astype(jnp.int32)
-        hot = jnp.where(place == index, 1.0, 0.0).astype(BF)
-        dquery = dot(rows, hot, ((0,), (0,))).astype(BF)
+        dquery = []
+        for e in range(2):
+            head = 2 * group + e
+            mine = jnp.where(side == 0, parts[2 * e], parts[2 * e + 1]).astype(BF)
+            weight = jnp.where(line == head, 1.0 * CELL, jnp.where(line == HEADS + head, 1.0, 0.0))
+            index = jnp.sum(slot * weight, axis=0, keepdims=True).astype(jnp.int32)
+            hot = jnp.where(place == index, 1.0, 0.0).astype(BF)
+            dquery.append(dot(mine, hot, ((0,), (0,))))
+        dquery = jnp.concatenate(dquery, axis=0).astype(BF)
         term = dot(act_ref[0, :features, :], dquery, NT)
         total = term if total is None else total + term
 
@@ -325,49 +331,37 @@
 
     @pl.when(b == pl.num_programs(0) - 1)
     def _():
-        if earlier_ref is None:
-            out_ref[...] = acc_ref[...]
-        else:
-            both = [ref[...].reshape(-1, CELL, HEAD) for ref in (earlier_ref, acc_ref)]
-            out_ref[...] = jnp.concatenate(both, axis=1).astype(BF)
-
-
-def weight_grad(where, rows, acts, features, seqs, earlier):
+        both = [acc_ref[:, e * HEAD : (e + 1) * HEAD].reshape(-1, CELL, HEAD) for e in range(2)]
+        out_ref[...] = jnp.concatenate(both, axis=1).astype(BF)
+
+
+def weight_grad(where, rows, acts, features, seqs):
     def act_spec():
         return pl.BlockSpec((1, features + CARRIED, TOK), lambda b, w: (b, 0, 0))
 
-    in_specs = [
-        pl.BlockSpec((OWNERS, 2 * CELL, HEAD), lambda b, w: (b, 0, 0)),
-        act_spec(),
-        act_spec(),
-    ]
-    if earlier is None:
-        out = jax.ShapeDtypeStruct((features, HEAD), F32)
-        out_spec = pl.BlockSpec((features, HEAD), lambda b, w: (0, 0))
-        more = ()
-    else:
-        out = jax.ShapeDtypeStruct((features // CELL, 2 * CELL, HEAD), BF)
-        out_spec = pl.BlockSpec((features // CELL, 2 * CELL, HEAD), lambda b, w: (0, 0, 0))
-        in_specs.append(pl.BlockSpec((features, HEAD), lambda b, w: (0, 0)))
-        more = (earlier,)
+    out = (features // CELL, 2 * CELL, HEAD)
     return pl.pallas_call(
         grad_kernel,
         grid_spec=pltpu.PrefetchScalarGridSpec(
             num_scalar_prefetch=1,
             grid=(seqs,),
-            in_specs=in_specs,
-            out_specs=out_spec,
-            scratch_shapes=[pltpu.VMEM((features, HEAD), F32)],
-        ),
-        out_shape=out,
+            in_specs=[
+                pl.BlockSpec((OWNERS, 4 * CELL, HEAD), lambda b, w: (b, 0, 0)),
+                act_spec(),
+                act_spec(),
+            ],
+            out_specs=pl.BlockSpec(out, lambda b, w: (0, 0, 0)),
+            scratch_shapes=[pltpu.VMEM((features, 2 * HEAD), F32)],
+        ),
+        out_shape=jax.ShapeDtypeStruct(out, BF),
         compiler_params=params("arbitrary"),
         cost_estimate=pl.CostEstimate(
-            flops=4 * seqs * TOK * features * HEAD * 2,
+            flops=8 * seqs * TOK * features * HEAD * 2,
             bytes_accessed=12 * 2**20,
             transcendentals=0,
         ),
         name="weight_grad",
-    )(where, rows, *acts, *more)
+    )(where, rows, *acts)
 
 
 def on_device(activations, w_query, all_keys, values, grad_out, cluster):
@@ -415,16 +409,12 @@
     _, kv, gq = lax.while_loop(
         lambda state: state[0] > 0.5, send_all_slots, (flags[0, 0], kv, gq)
     )
-    part = None
-    for c in range(CHUNKS):
-        rows = attention(kv, gq, c * HPC // 2)
-        back = all_send(rows.reshape(devices, 2 * CELL, HEAD))
-        where = jnp.stack([c * HPC + group, core]).astype(jnp.int32)
-        part = weight_grad(where, back, acts, features, seqs, part)
-    terms = all_send(part)
-    terms = terms.reshape(seqs, OWNERS // 2, 2, CHUNKS, features // devices, HEAD)
+    back = all_send(attention(kv, gq).reshape(devices, 4 * CELL, HEAD))
+    where = jnp.stack([group, core]).astype(jnp.int32)
+    terms = all_send(weight_grad(where, back, acts, features, seqs))
+    terms = terms.reshape(seqs, OWNERS // 2, 2, 2, features // devices, HEAD)
     out = jnp.sum(terms.astype(F32), axis=1)
-    out = out.transpose(3, 2, 0, 1, 4)
+    out = out.transpose(3, 0, 1, 2, 4)
     return out.reshape(features // devices, HEADS * HEAD)
 
 

time: 328 us -> 320 us (0.976)
  Pallas kernels: 51.5 us -> 43.3 us
  waiting for transfers between devices: 171 us -> 176 us
  starting transfers between devices: 37.2 us -> 33.2 us
    pallas_call x2 -> x1, Pallas kernels: 14.2 us -> 7.89 us  [weight_grad(): pl.pallas_call(grad_kernel, grid_spec=pltpu.PrefetchScalarGridSpec(num_sc...]
    all_to_all x2 -> x1, waiting for transfers between devices: 49 us -> 54.8 us  [on_device(): back = all_send(attention(kv, gq).reshape(devices, 4 * CELL, HEAD))]
    all_to_all x2 -> x1, starting transfers between devices: 13.6 us -> 8.45 us  [on_device(): back = all_send(attention(kv, gq).reshape(devices, 4 * CELL, HEAD))]
    pallas_call x2 -> x1, Pallas kernels: 16.4 us -> 14.6 us  [attention(): pl.pallas_call(attention_kernel, grid=(groups,), in_specs=[pair_spec(), p...]
  transfers between devices with their start and end apart: 9 -> 8, of which waited for: 4 -> 3; matrix products, arithmetic and copies ran while one was open for 4% -> 4% of each run, Pallas kernels for 12% -> 9%
where the time goes in v6:
time: 320 us; the launch traced here: 319 us
  waiting for transfers between devices  176 us (55%)
  Pallas kernels  43.3 us (14%)
  blocking collectives  36.8 us (11%)
  starting transfers between devices  33.2 us (10%)
  between operations  13.5 us (4%)
  matrix products  7.08 us (2%)
  local copies, waits for them, and re-layouts  6.13 us (2%)
    all_to_all x1, waiting for transfers between devices, on_device(): got_gq = seq_send(send_gq)  68.2 us
    all_to_all x1, waiting for transfers between devices, on_device(): back = all_send(attention(kv, gq).reshape(devices, 4 * CELL, HEAD))  54.8 us
    all_to_all x1, waiting for transfers between devices, on_device(): seq_send(compact(slots, row_of, held, jnp.zeros((8, HEAD), F32), keys, va...  52.4 us
    all_to_all x1, blocking collectives, on_device(): terms = all_send(weight_grad(where, back, acts, features, seqs))  36.8 us
    pallas_call x1, Pallas kernels, attention(): pl.pallas_call(attention_kernel, grid=(groups,), in_specs=[pair_spec(), p...  14.6 us
    all_to_all x1, starting transfers between devices, on_device(): seq_send(compact(slots, row_of, held, jnp.zeros((8, HEAD), F32), keys, va...  13.2 us
    pallas_call x2, Pallas kernels, compact(): pl.pallas_call(compact_kernel, grid=(FILLS + groups,), in_specs=[pl.Block...  10.2 us
    pallas_call x2, Pallas kernels, spread(): pl.pallas_call(functools.partial(spread_kernel, mark), grid=(OWNERS // GR...  9.57 us
  transfers between devices with their start and end apart: 8, of which 3 were waited for; matrix products, arithmetic and copies ran while one was open for 4% of the time, Pallas kernels for 9%

profile of v6, /device:TPU:1, one launch (start us, length us, event | category | flops | bytes accessed | tf_op | source)
XLA Modules:
  0.0 319.2 jit_solution(13661932337404829415)
XLA Ops:
  6.5 0.8 copy.11.col_ref
  7.4 0.0 copy-start.1
  7.4 0.7 copy-done.1
  8.1 1.1 slots.1
  9.2 0.0 copy-start.2
  9.2 0.6 copy-done.2
  9.8 0.0 copy-start.3
  9.8 0.6 copy-done.3
  10.4 0.6 broadcast_in_dim.3.flag_ref
  11.0 5.1 %compact.3 = bf16[64,96,256]{2,1,0:T(8,128)(2,1)} custom-call(s32[2,8,256]{2,1,0:T(8,128)S(1)} %bitcast.29, f32[64,128]{1,0:T(8,128)} %copy-done.3, f32[64,128]{1,0:T(8,128)} %copy-done.2, f32[8,128]{1,0:T(8,128)} %broadcast_in_dim.3.flag_ref, bf16[256,2048]{1,0:T(8,128)(2,1)} %bitcast.35, bf16[256,2048]{1,0:T(8,128)(2,1)} %bitcast.37), custom_call_target="tpu_custom_call" | custom-call | flops 4294967296 | bytes 8388608 | tf_op jit(solution)/shard_map/compact/pallas_call | solution.py:127
  16.1 13.2 %all-to-all-start.2 = ((bf16[64,96,256]{2,1,0:T(8,128)(2,1)}), bf16[64,96,256]{2,1,0:T(8,128)(2,1)S(1)}, u32[]{:S(2)}, u32[]{:S(2)}) async-start(bf16[64,96,256]{2,1,0:T(8,128)(2,1)} %compact.3), calls=%async_computation.2 | async-start | bytes 6291456 | tf_op jit(solution)/shard_map/all_to_all | solution.py:388
  29.3 1.3 collective-permute-start
  30.6 2.4 collective-permute-start.1
  33.0 1.2 collective-permute-start.2
  34.2 2.2 copy.12
  36.4 0.0 copy-start.4
  36.5 7.1 %convolution_convert_fusion.two_ref = bf16[256,2048]{1,0:T(8,128)(2,1)} fusion(bf16[2048,2048]{1,0:T(8,128)(2,1)} %param.9, bf16[1,256,2048]{2,1,0:T(8,128)(2,1)} %param.8), kind=kOutput, calls=%fused_computation.2 | convolution fusion | flops 2148007936 | bytes 10485760 | tf_op jit(solution)/shard_map/dot_general | solution.py:389
  43.5 0.0 copy-done.4
  43.5 1.2 pad_maximum_fusion.2
  44.7 0.0 collective-permute-done
  44.7 0.0 collective-permute-done.1
  44.7 0.0 collective-permute-done.2
  44.7 0.6 maximum_maximum_fusion.flag_ref
  45.3 5.1 %compact.2 = bf16[64,96,256]{2,1,0:T(8,128)(2,1)} custom-call(s32[2,8,256]{2,1,0:T(8,128)S(1)} %bitcast.30, f32[64,128]{1,0:T(8,128)} %copy-done.3, f32[64,128]{1,0:T(8,128)} %copy-done.2, f32[8,128]{1,0:T(8,128)} %maximum_maximum_fusion.flag_ref, bf16[256,2048]{1,0:T(8,128)(2,1)} %bitcast.33, bf16[256,2048]{1,0:T(8,128)(2,1)} %convolution_convert_fusion.two_ref), custom_call_target="tpu_custom_call" | custom-call | flops 4294967296 | bytes 8388608 | tf_op jit(solution)/shard_map/compact/pallas_call | solution.py:127
  50.4 52.4 %all-to-all-done.2.note_ref.got_ref = bf16[64,96,256]{2,1,0:T(8,128)(2,1)S(1)} async-done(((bf16[64,96,256]{2,1,0:T(8,128)(2,1)}), bf16[64,96,256]{2,1,0:T(8,128)(2,1)S(1)}, u32[]{:S(2)}, u32[]{:S(2)}) %all-to-all-start.2) | async-done | bytes 3145760 | tf_op jit(solution)/shard_map/all_to_all | solution.py:388
  102.8 0.0 copy-start
  102.8 6.2 %all-to-all-start.3 = ((bf16[64,96,256]{2,1,0:T(8,128)(2,1)}), bf16[64,96,256]{2,1,0:T(8,128)(2,1)}, u32[]{:S(2)}, u32[]{:S(2)}) async-start(bf16[64,96,256]{2,1,0:T(8,128)(2,1)} %compact.2), calls=%async_computation.3 | async-start | bytes 6291456 | tf_op jit(solution)/shard_map/all_to_all | solution.py:395
  109.0 0.2 all-gather.3.cloned.1.call-start
  109.3 0.5 all-gather.3.cloned.1.call-update
  109.8 4.5 %spread.3 = (bf16[64,128,256]{2,1,0:T(8,128)(2,1)}, f32[8,128]{1,0:T(8,128)}) custom-call(bf16[64,96,256]{2,1,0:T(8,128)(2,1)S(1)} %all-to-all-done.2.note_ref.got_ref, bf16[64,96,256]{2,1,0:T(8,128)(2,1)S(1)} %all-to-all-done.2.note_ref.got_ref), custom_call_target="tpu_custom_call" | custom-call | flops 2147483648 | bytes 8388608 | tf_op jit(solution)/shard_map/spread/pallas_call | solution.py:183
  114.3 0.0 copy-done
  114.3 68.2 %all-to-all-done.3.got_ref = bf16[64,96,256]{2,1,0:T(8,128)(2,1)} async-done(((bf16[64,96,256]{2,1,0:T(8,128)(2,1)}), bf16[64,96,256]{2,1,0:T(8,128)(2,1)}, u32[]{:S(2)}, u32[]{:S(2)}) %all-to-all-start.3) | async-done | bytes 3145760 | tf_op jit(solution)/shard_map/all_to_all | solution.py:395
  182.5 0.0 copy-start.5
  182.5 0.0 copy-start.6
  182.5 5.0 %spread.2 = (bf16[64,128,256]{2,1,0:T(8,128)(2,1)}, f32[8,128]{1,0:T(8,128)S(1)}) custom-call(bf16[64,96,256]{2,1,0:T(8,128)(2,1)} %all-to-all-done.3.got_ref, bf16[64,96,256]{2,1,0:T(8,128)(2,1)} %copy-done), custom_call_target="tpu_custom_call" | custom-call | flops 2147483648 | bytes 8388608 | tf_op jit(solution)/shard_map/spread/pallas_call | solution.py:183
  187.5 0.5 slice.3
  188.0 0.3 collective-permute-start.3
  188.3 0.0 copy-done.5
  188.3 0.0 copy-done.6
  188.3 0.7 while.11
  189.0 14.6 %attention.1 = bf16[4,32,2,32,128]{4,3,2,1,0:T(8,128)(2,1)} custom-call(bf16[64,128,256]{2,1,0:T(8,128)(2,1)} %get-tuple-element.64.kv_ref, bf16[64,128,256]{2,1,0:T(8,128)(2,1)} %get-tuple-element.65.gq_ref), custom_call_target="tpu_custom_call" | custom-call | flops 4294967296 | bytes 10485760 | tf_op jit(solution)/shard_map/attention/pallas_call | solution.py:282
  203.5 8.5 %all-to-all-start.4 = ((bf16[256,32,128]{2,1,0:T(8,128)(2,1)}), bf16[256,32,128]{2,1,0:T(8,128)(2,1)S(1)}, u32[]{:S(2)}, u32[]{:S(2)}) async-start(bf16[256,32,128]{2,1,0:T(8,128)(2,1)} %bitcast.28), calls=%async_computation.4 | async-start | bytes 4194304 | tf_op jit(solution)/shard_map/all_to_all | solution.py:412
  212.0 0.1 pad_add_fusion.where_ref
  212.1 54.8 %all-to-all-done.4.rows_ref = bf16[256,32,128]{2,1,0:T(8,128)(2,1)S(1)} async-done(((bf16[256,32,128]{2,1,0:T(8,128)(2,1)}), bf16[256,32,128]{2,1,0:T(8,128)(2,1)S(1)}, u32[]{:S(2)}, u32[]{:S(2)}) %all-to-all-start.4) | async-done | bytes 2097184 | tf_op jit(solution)/shard_map/all_to_all | solution.py:412
  266.8 0.0 collective-permute-done.3.act_b
  266.8 7.9 %weight_grad.1 = bf16[256,16,128]{2,1,0:T(8,128)(2,1)S(1)} custom-call(s32[2]{0:T(128)S(1)} %pad_add_fusion.where_ref, bf16[256,32,128]{2,1,0:T(8,128)(2,1)S(1)} %all-to-all-done.4.rows_ref, bf16[4,2080,256]{2,1,0:T(8,128)(2,1)} %bitcast.32, bf16[4,2080,256]{2,1,0:T(8,128)(2,1)} %collective-permute-done.3.act_b), custom_call_target="tpu_custom_call" | custom-call | flops 4294967296 | bytes 12582912 | tf_op jit(solution)/shard_map/weight_grad/pallas_call | solution.py:343
  274.7 36.8 %all_to_all.28 = bf16[256,16,128]{2,1,0:T(8,128)(2,1)S(1)} all-to-all(bf16[256,16,128]{2,1,0:T(8,128)(2,1)S(1)} %weight_grad.1), channel_id=1, replica_groups=mesh['dp'=4,'seq'=64] {'dp','seq'}, dimensions={0} | all-to-all | bytes 2097152 | tf_op jit(solution)/shard_map/all_to_all | solution.py:414
  311.6 0.8 convert_reduce_fusion
  (2 shorter events, 0.0 us)
Async XLA Ops:
  7.4 0.7 copy-start.1
  9.2 0.6 copy-start.2
  9.8 0.6 copy-start.3
  16.1 86.7 %all-to-all-start.2 = ((bf16[64,96,256]{2,1,0:T(8,128)(2,1)}), bf16[64,96,256]{2,1,0:T(8,128)(2,1)S(1)}, u32[]{:S(2)}, u32[]{:S(2)}) async-start(bf16[64,96,256]{2,1,0:T(8,128)(2,1)} %compact.3), calls=%async_computation.2 | async-start | bytes 6291456 | tf_op jit(solution)/shard_map/all_to_all | solution.py:388
  29.3 15.4 %collective-permute-start = (f32[8,128]{1,0:T(8,128)S(1)}, f32[8,128]{1,0:T(8,128)S(1)}, u32[]{:S(2)}, u32[]{:S(2)}) collective-permute-start(f32[8,128]{1,0:T(8,128)S(1)} %get-tuple-element.58), channel_id=1, source_target_pairs={{0,64},{64,128},{128,192},{192,0},{1,65},{65,129},{129,193},{193,1... | collective-permute-start | bytes 12296 | tf_op jit(solution)/shard_map/ppermute | solution.py:386
  30.6 14.1 %collective-permute-start.1 = (f32[8,128]{1,0:T(8,128)S(1)}, f32[8,128]{1,0:T(8,128)S(1)}, u32[]{:S(2)}, u32[]{:S(2)}) collective-permute-start(f32[8,128]{1,0:T(8,128)S(1)} %get-tuple-element.58), channel_id=1, source_target_pairs={{0,128},{64,192},{128,0},{192,64},{1,129},{65,193},{129,1},{193,65... | collective-permute-start | bytes 12296 | tf_op jit(solution)/shard_map/ppermute | solution.py:386
  33.0 11.7 %collective-permute-start.2 = (f32[8,128]{1,0:T(8,128)S(1)}, f32[8,128]{1,0:T(8,128)S(1)}, u32[]{:S(2)}, u32[]{:S(2)}) collective-permute-start(f32[8,128]{1,0:T(8,128)S(1)} %get-tuple-element.58), channel_id=1, source_target_pairs={{0,192},{64,0},{128,64},{192,128},{1,193},{65,1},{129,65},{193,129... | collective-permute-start | bytes 12296 | tf_op jit(solution)/shard_map/ppermute | solution.py:386
  36.4 7.1 %copy-start.4 = (bf16[1,256,2048]{1,2,0:T(8,128)(2,1)S(1)}, bf16[1,256,2048]{1,2,0:T(8,128)(2,1)}, u32[]{:S(2)}) copy-start(bf16[1,256,2048]{1,2,0:T(8,128)(2,1)} %copy.12) | copy-start | bytes 3145732
  102.8 11.5 %copy-start = (bf16[64,96,256]{2,1,0:T(8,128)(2,1)}, bf16[64,96,256]{2,1,0:T(8,128)(2,1)S(1)}, u32[]{:S(2)}) copy-start(bf16[64,96,256]{2,1,0:T(8,128)(2,1)S(1)} %all-to-all-done.2.note_ref.got_ref) | copy-start | bytes 9437188
  102.8 79.7 %all-to-all-start.3 = ((bf16[64,96,256]{2,1,0:T(8,128)(2,1)}), bf16[64,96,256]{2,1,0:T(8,128)(2,1)}, u32[]{:S(2)}, u32[]{:S(2)}) async-start(bf16[64,96,256]{2,1,0:T(8,128)(2,1)} %compact.2), calls=%async_computation.3 | async-start | bytes 6291456 | tf_op jit(solution)/shard_map/all_to_all | solution.py:395
  109.0 79.0 %all-gather.3.cloned.1.call-start = ((), (), s32[]{:S(2)}) async-start(), calls=%async_computation.6 | async-start | bytes 5324800 | tf_op jit(solution)/shard_map/all_gather | solution.py:397
  182.5 5.8 %copy-start.5 = (bf16[1,256,2048]{2,1,0:T(8,128)(2,1)S(1)}, bf16[1,256,2048]{2,1,0:T(8,128)(2,1)}, u32[]{:S(2)}) copy-start(bf16[1,256,2048]{2,1,0:T(8,128)(2,1)} %param.12) | copy-start | bytes 3145732
  182.5 5.8 %copy-start.6 = (bf16[1,256,2048]{2,1,0:T(8,128)(2,1)S(1)}, bf16[1,256,2048]{2,1,0:T(8,128)(2,1)}, u32[]{:S(2)}) copy-start(bf16[1,256,2048]{2,1,0:T(8,128)(2,1)} %param.10) | copy-start | bytes 3145732
  188.0 78.8 %collective-permute-start.3 = (bf16[4,2080,256]{2,1,0:T(8,128)(2,1)}, bf16[4,2080,256]{2,1,0:T(8,128)(2,1)}, u32[]{:S(2)}, u32[]{:S(2)}) collective-permute-start(bf16[4,2080,256]{2,1,0:T(8,128)(2,1)} %bitcast.31), channel_id=1, source_target_pairs={{0,1},{1,0},{2,3},{3,2},{4,5},{5,4},{6,7},{7,6},{8,9},{9,8},{10,11... | collective-permute-start | bytes 12779528 | tf_op jit(solution)/shard_map/ppermute | solution.py:398
  203.5 63.3 %all-to-all-start.4 = ((bf16[256,32,128]{2,1,0:T(8,128)(2,1)}), bf16[256,32,128]{2,1,0:T(8,128)(2,1)S(1)}, u32[]{:S(2)}, u32[]{:S(2)}) async-start(bf16[256,32,128]{2,1,0:T(8,128)(2,1)} %bitcast.28), calls=%async_computation.4 | async-start | bytes 4194304 | tf_op jit(solution)/shard_map/all_to_all | solution.py:412
Sparse Core Ops, SparseCore 0:
  111.7 52.2 all-gather.2

commit v7 on v6

--- a/solution.py
+++ b/solution.py
@@ -38,7 +38,7 @@
     return pltpu.CompilerParams(vmem_limit_bytes=vmem, dimension_semantics=semantics or None)
 
 
-def slot_kernel(col_ref, row_ref, out_ref, held_ref, row_of_ref, over_ref):
+def slot_kernel(col_ref, row_ref, out_ref, row_of_ref, over_ref):
     earlier = lax.broadcasted_iota(jnp.int32, (TOK, TOK), 0) < lax.broadcasted_iota(
         jnp.int32, (TOK, TOK), 1
     )
@@ -56,7 +56,6 @@
         to_lane = jnp.where(lanes == h * CELL + cell, 1.0, 0.0).astype(BF)
         term = dot(to_owner, to_lane, NT)
         held = term if held is None else held + term
-    held_ref[...] = held
     before = lax.broadcasted_iota(jnp.int32, (HEADS * CELL, HEADS * CELL), 0) < (
         lax.broadcasted_iota(jnp.int32, (HEADS * CELL, HEADS * CELL), 1)
     )
@@ -74,7 +73,6 @@
         out_shape=(
             jax.ShapeDtypeStruct((HEADS, TOK), jnp.int32),
             per_owner,
-            per_owner,
             jax.ShapeDtypeStruct((8, HEAD), F32),
         ),
         compiler_params=params(),
@@ -82,7 +80,7 @@
     )(assign, assign.T)
 
 
-def compact_kernel(slot_ref, row_of_ref, held_ref, flag_ref, one_ref, two_ref, out_ref, buf_ref):
+def compact_kernel(slot_ref, row_of_ref, flag_ref, one_ref, two_ref, out_ref, buf_ref):
     p = pl.program_id(0)
 
     @pl.when(p < FILLS)
@@ -103,8 +101,8 @@
     def _():
         first = pl.multiple_of((p - FILLS) * GROUP, GROUP)
         row_of = row_of_ref[pl.ds(first, GROUP), :]
+        held = jnp.where(row_of > 0.5, 1.0, 0.0)
         row_of = jnp.where(row_of < COMPACT, row_of, -2.0 * COMPACT).astype(jnp.int32)
-        held = held_ref[pl.ds(first, GROUP), :]
         notes = jnp.concatenate([held, jnp.broadcast_to(flag_ref[0:1, :], held.shape)], axis=1)
         place = lax.broadcasted_iota(jnp.int32, (2 * COMPACT, 2 * HEAD), 0)
         line = lax.broadcasted_iota(jnp.int32, (2 * CELL, 2 * HEAD), 0)
@@ -119,7 +117,7 @@
                 out_ref[d + e] = jnp.concatenate([top, mine[2 * CELL :]], axis=0).astype(BF)
 
 
-def compact(slots, row_of, held, flag, one, two):
+def compact(slots, row_of, flag, one, two):
     groups = OWNERS // GROUP
     share = HEADS // FILLS
     whole = pl.BlockSpec((OWNERS, HEADS * CELL), lambda p: (0, 0))
@@ -129,7 +127,6 @@
         grid=(FILLS + groups,),
         in_specs=[
             pl.BlockSpec((1, share, TOK), lambda p: (jnp.minimum(p, FILLS - 1), 0, 0)),
-            whole,
             whole,
             pl.BlockSpec((8, HEAD), lambda p: (0, 0)),
             source,
@@ -145,7 +142,7 @@
             flops=4 * 2**30, bytes_accessed=8 * 2**20, transcendentals=0
         ),
         name="compact",
-    )(slots.reshape(FILLS, share, TOK), row_of, held, flag, one, two)
+    )(slots.reshape(FILLS, share, TOK), row_of, flag, one, two)
 
 
 def spread_kernel(mark, got_ref, note_ref, out_ref, flag_ref):
@@ -369,7 +366,7 @@
     features = tokens_here.shape[1]
     seqs = lax.axis_size("dp")
     devices = seqs * OWNERS
-    slots, held, row_of, over = slots_of(cluster[0])
+    slots, row_of, over = slots_of(cluster[0])
     seq_send = functools.partial(
         lax.all_to_all, axis_name="seq", split_axis=0, concat_axis=0, tiled=True
     )
@@ -385,9 +382,9 @@
         ring = [(i, (i + shift) % seqs) for i in range(seqs)]
         flag = jnp.maximum(flag, lax.ppermute(over, "dp", ring))
 
-    got_kv = seq_send(compact(slots, row_of, held, jnp.zeros((8, HEAD), F32), keys, vals))
+    got_kv = seq_send(compact(slots, row_of, over, keys, vals))
     queries = jnp.dot(tokens_here, w_query, preferred_element_type=F32).astype(BF)
-    send_gq = compact(slots, row_of, held, flag, grads, queries)
+    send_gq = compact(slots, row_of, flag, grads, queries)
     carried = jnp.concatenate(
         [tokens_here.T, (slots // CELL).astype(BF), (slots % CELL).astype(BF)], axis=0
     )

time: 320 us -> 319 us (level)
  no operation moved by 1% of the time
where the time goes in v7:
time: 319 us
  waiting for transfers between devices  176 us (55%)
  Pallas kernels  43.3 us (14%)
  blocking collectives  36.8 us (12%)
  starting transfers between devices  33.4 us (10%)
  between operations  13.5 us (4%)
  matrix products  7.07 us (2%)
  local copies, waits for them, and re-layouts  5.52 us (2%)
    all_to_all x1, waiting for transfers between devices, on_device(): got_gq = seq_send(send_gq)  68.2 us
    all_to_all x1, waiting for transfers between devices, on_device(): back = all_send(attention(kv, gq).reshape(devices, 4 * CELL, HEAD))  54.8 us
    all_to_all x1, waiting for transfers between devices, on_device(): got_kv = seq_send(compact(slots, row_of, over, keys, vals))  52.4 us
    all_to_all x1, blocking collectives, on_device(): terms = all_send(weight_grad(where, back, acts, features, seqs))  36.8 us
    pallas_call x1, Pallas kernels, attention(): pl.pallas_call(attention_kernel, grid=(groups,), in_specs=[pair_spec(), p...  14.5 us
    all_to_all x1, starting transfers between devices, on_device(): got_kv = seq_send(compact(slots, row_of, over, keys, vals))  13.3 us
    pallas_call x2, Pallas kernels, compact(): pl.pallas_call(compact_kernel, grid=(FILLS + groups,), in_specs=[pl.Block...  10.2 us
    pallas_call x2, Pallas kernels, spread(): pl.pallas_call(functools.partial(spread_kernel, mark), grid=(OWNERS // GR...  9.56 us
  transfers between devices with their start and end apart: 8, of which 3 were waited for; matrix products, arithmetic and copies ran while one was open for 4% of the time, Pallas kernels for 9%

profile of v7, /device:TPU:1, one launch (start us, length us, event | category | flops | bytes accessed | tf_op | source)
XLA Modules:
  0.0 318.7 jit_solution(5757058065227508642)
XLA Ops:
  6.5 0.8 copy.11.col_ref
  7.4 0.0 copy-start.1
  7.4 0.7 copy-done.1
  8.1 1.1 slots.1
  9.2 0.0 copy-start.2
  9.2 0.6 copy-done.2
  9.8 0.0 copy-start.4
  9.8 0.6 copy-done.4
  10.4 5.1 %compact.3 = bf16[64,96,256]{2,1,0:T(8,128)(2,1)} custom-call(s32[2,8,256]{2,1,0:T(8,128)S(1)} %bitcast.29, f32[64,128]{1,0:T(8,128)} %copy-done.4, f32[8,128]{1,0:T(8,128)} %copy-done.2, bf16[256,2048]{1,0:T(8,128)(2,1)} %bitcast.35, bf16[256,2048]{1,0:T(8,128)(2,1)} %bitcast.37), custom_call_target="tpu_custom_call" | custom-call | flops 4294967296 | bytes 8388608 | tf_op jit(solution)/shard_map/compact/pallas_call | solution.py:125
  15.5 0.0 copy-start.3
  15.5 13.3 %all-to-all-start.2 = ((bf16[64,96,256]{2,1,0:T(8,128)(2,1)}), bf16[64,96,256]{2,1,0:T(8,128)(2,1)S(1)}, u32[]{:S(2)}, u32[]{:S(2)}) async-start(bf16[64,96,256]{2,1,0:T(8,128)(2,1)} %compact.3), calls=%async_computation.2 | async-start | bytes 6291456 | tf_op jit(solution)/shard_map/all_to_all | solution.py:385
  28.8 0.0 copy-done.3
  28.8 1.3 collective-permute-start
  30.1 2.4 collective-permute-start.1
  32.5 1.2 collective-permute-start.2
  33.7 2.3 copy.12
  36.0 0.0 copy-start.5
  36.0 7.1 %convolution_convert_fusion.two_ref = bf16[256,2048]{1,0:T(8,128)(2,1)} fusion(bf16[2048,2048]{1,0:T(8,128)(2,1)} %param.9, bf16[1,256,2048]{2,1,0:T(8,128)(2,1)} %param.8), kind=kOutput, calls=%fused_computation.2 | convolution fusion | flops 2148007936 | bytes 10485760 | tf_op jit(solution)/shard_map/dot_general | solution.py:386
  43.0 0.0 copy-done.5
  43.1 1.2 pad_maximum_fusion.2
  44.2 0.0 collective-permute-done
  44.2 0.0 collective-permute-done.1
  44.2 0.0 collective-permute-done.2
  44.2 0.6 maximum_maximum_fusion.flag_ref
  44.8 5.1 %compact.2 = bf16[64,96,256]{2,1,0:T(8,128)(2,1)} custom-call(s32[2,8,256]{2,1,0:T(8,128)S(1)} %bitcast.30, f32[64,128]{1,0:T(8,128)} %copy-done.4, f32[8,128]{1,0:T(8,128)} %maximum_maximum_fusion.flag_ref, bf16[256,2048]{1,0:T(8,128)(2,1)} %bitcast.33, bf16[256,2048]{1,0:T(8,128)(2,1)} %convolution_convert_fusion.two_ref), custom_call_target="tpu_custom_call" | custom-call | flops 4294967296 | bytes 8388608 | tf_op jit(solution)/shard_map/compact/pallas_call | solution.py:125
  49.9 52.4 %all-to-all-done.2.note_ref.got_ref = bf16[64,96,256]{2,1,0:T(8,128)(2,1)S(1)} async-done(((bf16[64,96,256]{2,1,0:T(8,128)(2,1)}), bf16[64,96,256]{2,1,0:T(8,128)(2,1)S(1)}, u32[]{:S(2)}, u32[]{:S(2)}) %all-to-all-start.2) | async-done | bytes 3145760 | tf_op jit(solution)/shard_map/all_to_all | solution.py:385
  102.3 0.0 copy-start
  102.3 6.2 %all-to-all-start.3 = ((bf16[64,96,256]{2,1,0:T(8,128)(2,1)}), bf16[64,96,256]{2,1,0:T(8,128)(2,1)}, u32[]{:S(2)}, u32[]{:S(2)}) async-start(bf16[64,96,256]{2,1,0:T(8,128)(2,1)} %compact.2), calls=%async_computation.3 | async-start | bytes 6291456 | tf_op jit(solution)/shard_map/all_to_all | solution.py:392
  108.5 0.2 all-gather.3.cloned.1.call-start
  108.8 0.5 all-gather.3.cloned.1.call-update
  109.3 4.5 %spread.3 = (bf16[64,128,256]{2,1,0:T(8,128)(2,1)}, f32[8,128]{1,0:T(8,128)}) custom-call(bf16[64,96,256]{2,1,0:T(8,128)(2,1)S(1)} %all-to-all-done.2.note_ref.got_ref, bf16[64,96,256]{2,1,0:T(8,128)(2,1)S(1)} %all-to-all-done.2.note_ref.got_ref), custom_call_target="tpu_custom_call" | custom-call | flops 2147483648 | bytes 8388608 | tf_op jit(solution)/shard_map/spread/pallas_call | solution.py:180
  113.8 0.0 copy-done
  113.8 68.2 %all-to-all-done.3.got_ref = bf16[64,96,256]{2,1,0:T(8,128)(2,1)} async-done(((bf16[64,96,256]{2,1,0:T(8,128)(2,1)}), bf16[64,96,256]{2,1,0:T(8,128)(2,1)}, u32[]{:S(2)}, u32[]{:S(2)}) %all-to-all-start.3) | async-done | bytes 3145760 | tf_op jit(solution)/shard_map/all_to_all | solution.py:392
  182.0 0.0 copy-start.6
  182.0 5.0 %spread.2 = (bf16[64,128,256]{2,1,0:T(8,128)(2,1)}, f32[8,128]{1,0:T(8,128)S(1)}) custom-call(bf16[64,96,256]{2,1,0:T(8,128)(2,1)} %all-to-all-done.3.got_ref, bf16[64,96,256]{2,1,0:T(8,128)(2,1)} %copy-done), custom_call_target="tpu_custom_call" | custom-call | flops 2147483648 | bytes 8388608 | tf_op jit(solution)/shard_map/spread/pallas_call | solution.py:180
  187.0 0.5 slice.3
  187.5 0.3 collective-permute-start.3
  187.8 0.0 copy-done.6
  187.8 0.0 copy-done.7
  187.8 0.7 while.11
  188.5 14.5 %attention.1 = bf16[4,32,2,32,128]{4,3,2,1,0:T(8,128)(2,1)} custom-call(bf16[64,128,256]{2,1,0:T(8,128)(2,1)} %get-tuple-element.62.kv_ref, bf16[64,128,256]{2,1,0:T(8,128)(2,1)} %get-tuple-element.63.gq_ref), custom_call_target="tpu_custom_call" | custom-call | flops 4294967296 | bytes 10485760 | tf_op jit(solution)/shard_map/attention/pallas_call | solution.py:279
  203.0 8.5 %all-to-all-start.4 = ((bf16[256,32,128]{2,1,0:T(8,128)(2,1)}), bf16[256,32,128]{2,1,0:T(8,128)(2,1)S(1)}, u32[]{:S(2)}, u32[]{:S(2)}) async-start(bf16[256,32,128]{2,1,0:T(8,128)(2,1)} %bitcast.28), calls=%async_computation.4 | async-start | bytes 4194304 | tf_op jit(solution)/shard_map/all_to_all | solution.py:409
  211.5 0.1 pad_add_fusion.where_ref
  211.6 54.8 %all-to-all-done.4.rows_ref = bf16[256,32,128]{2,1,0:T(8,128)(2,1)S(1)} async-done(((bf16[256,32,128]{2,1,0:T(8,128)(2,1)}), bf16[256,32,128]{2,1,0:T(8,128)(2,1)S(1)}, u32[]{:S(2)}, u32[]{:S(2)}) %all-to-all-start.4) | async-done | bytes 2097184 | tf_op jit(solution)/shard_map/all_to_all | solution.py:409
  266.3 0.0 collective-permute-done.3.act_b
  266.3 7.9 %weight_grad.1 = bf16[256,16,128]{2,1,0:T(8,128)(2,1)S(1)} custom-call(s32[2]{0:T(128)S(1)} %pad_add_fusion.where_ref, bf16[256,32,128]{2,1,0:T(8,128)(2,1)S(1)} %all-to-all-done.4.rows_ref, bf16[4,2080,256]{2,1,0:T(8,128)(2,1)} %bitcast.32, bf16[4,2080,256]{2,1,0:T(8,128)(2,1)} %collective-permute-done.3.act_b), custom_call_target="tpu_custom_call" | custom-call | flops 4294967296 | bytes 12582912 | tf_op jit(solution)/shard_map/weight_grad/pallas_call | solution.py:340
  274.2 36.8 %all_to_all.28 = bf16[256,16,128]{2,1,0:T(8,128)(2,1)S(1)} all-to-all(bf16[256,16,128]{2,1,0:T(8,128)(2,1)S(1)} %weight_grad.1), channel_id=1, replica_groups=mesh['dp'=4,'seq'=64] {'dp','seq'}, dimensions={0} | all-to-all | bytes 2097152 | tf_op jit(solution)/shard_map/all_to_all | solution.py:411
  311.1 0.8 convert_reduce_fusion
  (3 shorter events, 0.0 us)
Async XLA Ops:
  7.4 0.7 copy-start.1
  9.2 0.6 copy-start.2
  9.8 0.6 copy-start.4
  15.5 13.3 %copy-start.3 = (f32[8,128]{1,0:T(8,128)S(1)}, f32[8,128]{1,0:T(8,128)}, u32[]{:S(2)}) copy-start(f32[8,128]{1,0:T(8,128)} %copy-done.2) | copy-start | bytes 12292
  15.5 86.8 %all-to-all-start.2 = ((bf16[64,96,256]{2,1,0:T(8,128)(2,1)}), bf16[64,96,256]{2,1,0:T(8,128)(2,1)S(1)}, u32[]{:S(2)}, u32[]{:S(2)}) async-start(bf16[64,96,256]{2,1,0:T(8,128)(2,1)} %compact.3), calls=%async_computation.2 | async-start | bytes 6291456 | tf_op jit(solution)/shard_map/all_to_all | solution.py:385
  28.8 15.4 %collective-permute-start = (f32[8,128]{1,0:T(8,128)S(1)}, f32[8,128]{1,0:T(8,128)S(1)}, u32[]{:S(2)}, u32[]{:S(2)}) collective-permute-start(f32[8,128]{1,0:T(8,128)S(1)} %copy-done.3), channel_id=1, source_target_pairs={{0,64},{64,128},{128,192},{192,0},{1,65},{65,129},{129,193},{193,1... | collective-permute-start | bytes 12296 | tf_op jit(solution)/shard_map/ppermute | solution.py:383
  30.1 14.1 %collective-permute-start.1 = (f32[8,128]{1,0:T(8,128)S(1)}, f32[8,128]{1,0:T(8,128)S(1)}, u32[]{:S(2)}, u32[]{:S(2)}) collective-permute-start(f32[8,128]{1,0:T(8,128)S(1)} %copy-done.3), channel_id=1, source_target_pairs={{0,128},{64,192},{128,0},{192,64},{1,129},{65,193},{129,1},{193,65... | collective-permute-start | bytes 12296 | tf_op jit(solution)/shard_map/ppermute | solution.py:383
  32.5 11.7 %collective-permute-start.2 = (f32[8,128]{1,0:T(8,128)S(1)}, f32[8,128]{1,0:T(8,128)S(1)}, u32[]{:S(2)}, u32[]{:S(2)}) collective-permute-start(f32[8,128]{1,0:T(8,128)S(1)} %copy-done.3), channel_id=1, source_target_pairs={{0,192},{64,0},{128,64},{192,128},{1,193},{65,1},{129,65},{193,129... | collective-permute-start | bytes 12296 | tf_op jit(solution)/shard_map/ppermute | solution.py:383
  36.0 7.1 %copy-start.5 = (bf16[1,256,2048]{1,2,0:T(8,128)(2,1)S(1)}, bf16[1,256,2048]{1,2,0:T(8,128)(2,1)}, u32[]{:S(2)}) copy-start(bf16[1,256,2048]{1,2,0:T(8,128)(2,1)} %copy.12) | copy-start | bytes 3145732
  102.3 11.5 %copy-start = (bf16[64,96,256]{2,1,0:T(8,128)(2,1)}, bf16[64,96,256]{2,1,0:T(8,128)(2,1)S(1)}, u32[]{:S(2)}) copy-start(bf16[64,96,256]{2,1,0:T(8,128)(2,1)S(1)} %all-to-all-done.2.note_ref.got_ref) | copy-start | bytes 9437188
  102.3 79.7 %all-to-all-start.3 = ((bf16[64,96,256]{2,1,0:T(8,128)(2,1)}), bf16[64,96,256]{2,1,0:T(8,128)(2,1)}, u32[]{:S(2)}, u32[]{:S(2)}) async-start(bf16[64,96,256]{2,1,0:T(8,128)(2,1)} %compact.2), calls=%async_computation.3 | async-start | bytes 6291456 | tf_op jit(solution)/shard_map/all_to_all | solution.py:392
  108.5 79.0 %all-gather.3.cloned.1.call-start = ((), (), s32[]{:S(2)}) async-start(), calls=%async_computation.6 | async-start | bytes 5324800 | tf_op jit(solution)/shard_map/all_gather | solution.py:394
  182.0 5.8 %copy-start.6 = (bf16[1,256,2048]{2,1,0:T(8,128)(2,1)S(1)}, bf16[1,256,2048]{2,1,0:T(8,128)(2,1)}, u32[]{:S(2)}) copy-start(bf16[1,256,2048]{2,1,0:T(8,128)(2,1)} %param.12) | copy-start | bytes 3145732
  182.0 5.8 %copy-start.7 = (bf16[1,256,2048]{2,1,0:T(8,128)(2,1)S(1)}, bf16[1,256,2048]{2,1,0:T(8,128)(2,1)}, u32[]{:S(2)}) copy-start(bf16[1,256,2048]{2,1,0:T(8,128)(2,1)} %param.10) | copy-start | bytes 3145732
  187.5 78.8 %collective-permute-start.3 = (bf16[4,2080,256]{2,1,0:T(8,128)(2,1)}, bf16[4,2080,256]{2,1,0:T(8,128)(2,1)}, u32[]{:S(2)}, u32[]{:S(2)}) collective-permute-start(bf16[4,2080,256]{2,1,0:T(8,128)(2,1)} %bitcast.31), channel_id=1, source_target_pairs={{0,1},{1,0},{2,3},{3,2},{4,5},{5,4},{6,7},{7,6},{8,9},{9,8},{10,11... | collective-permute-start | bytes 12779528 | tf_op jit(solution)/shard_map/ppermute | solution.py:395
  203.0 63.3 %all-to-all-start.4 = ((bf16[256,32,128]{2,1,0:T(8,128)(2,1)}), bf16[256,32,128]{2,1,0:T(8,128)(2,1)S(1)}, u32[]{:S(2)}, u32[]{:S(2)}) async-start(bf16[256,32,128]{2,1,0:T(8,128)(2,1)} %bitcast.28), calls=%async_computation.4 | async-start | bytes 4194304 | tf_op jit(solution)/shard_map/all_to_all | solution.py:409
Sparse Core Ops, SparseCore 0:
  111.2 52.2 all-gather.2
